TPU v7x, 256 devices: a whole 4x4x8 slice. The times are simulated.
256 devices in a mesh: slab: 64 (over y, x_hi, z), mode: 4 (over x_lo, core).
Axes of the slice: x: 4 (x_hi: 2, x_lo: 2; x = x_hi * 2 + x_lo), y: 4, z: 8, core: 2. Of those that a mesh axis runs over, the one named last changes fastest.
Arguments:
- eigvec: bfloat16 [81920, 3, 1024], P('slab', None, 'mode'), may hold values from -6 to 6
- species: int32 [81920], P('slab'), may hold values from 0 to 3
- mode_cot: float32 [1024], P('mode'), may hold values from -4 to 4
- neighbours: int32 [81920, 16], P('slab'), may hold values from 0 to 2560, as said below
- pair_features: bfloat16 [1310720, 128], P(('slab', 'mode')), may hold values from -130 to 130
- w_in: bfloat16 [128, 256], replicated, may hold values from -0.5 to 0.5
- b_in: float32 [256], replicated, may hold values from -3 to 3
- w_out: bfloat16 [9, 256], replicated, may hold values from -0.375 to 0.375
Outputs:
- features_grad: bfloat16 [1310720, 128], P(('slab', 'mode'))
- grad_w_in: float32 [128, 256], replicated
- grad_b_in: float32 [256], replicated
- grad_w_out: float32 [9, 256], replicated
Inputs may be any that keep to these rules, and one draw needn't show every extreme that they name: `neighbours`: atom r of a slab (0 to 1279) lists extended indices from r to r + 1280; extended index x stands for atom (slab * 1280 + x - 640) mod 81920; the value 1280 + 2 * 640 marks an empty slot.
All inputs are finite; a program needn't handle non-finite values.
Results may differ from a plain program's by a relative error of at most 0.019.
Values may be sent and summed in bfloat16 or wider, within the bound.
No kernel may reach another device: no remote copies, remote signals or barrier semaphores. Data moves between devices by JAX's collectives and lax.ppermute only.
A program may use at most 64 MiB of HBM per device.

v0:
```python
import jax
import jax.numpy as jnp
from jax import lax
from jax.sharding import PartitionSpec as P

MASS_TABLE = (1.35, 2.94, 2.79, 2.95)
CLIP_NORM = 100.0


def with_halo(block, sides, width):
    for axis, dim in sides:
        count = lax.axis_size(axis)
        forward = [(i, i + 1) for i in range(count - 1)]
        forward.append((count - 1, 0))
        backward = [(target, source) for source, target in forward]
        low = lax.ppermute(
            lax.slice_in_dim(block, block.shape[dim] - width, None, axis=dim), axis, forward
        )
        high = lax.ppermute(lax.slice_in_dim(block, 0, width, axis=dim), axis, backward)
        block = jnp.concatenate([low, block, high], axis=dim)
    return block


def atom_masses(species):
    kinds = jnp.arange(4, dtype=jnp.int32)
    onehot = (species[:, None] == kinds[None, :]).astype(jnp.float32)
    return jnp.sum(onehot * jnp.asarray(MASS_TABLE, jnp.float32)[None, :], axis=1)


def mlp_backward(features, pair_cot, w_in, b_in, w_out):
    preact = jnp.dot(features, w_in, preferred_element_type=jnp.float32) + b_in[None, :]
    sigmoid_pre = jax.nn.sigmoid(preact)
    hidden = (preact * sigmoid_pre).astype(jnp.bfloat16)
    hidden_cot = lax.dot_general(
        pair_cot, w_out, (((0,), (0,)), ((), ())), preferred_element_type=jnp.float32
    )
    pre_cot = (hidden_cot * sigmoid_pre * (1.0 + preact * (1.0 - sigmoid_pre))).astype(jnp.bfloat16)
    features_grad = lax.dot_general(
        pre_cot, w_in, (((1,), (1,)), ((), ())), preferred_element_type=jnp.float32
    ).astype(jnp.bfloat16)
    grad_w_in = lax.dot_general(
        features, pre_cot, (((0,), (0,)), ((), ())), preferred_element_type=jnp.float32
    )
    grad_b_in = jnp.sum(pre_cot.astype(jnp.float32), axis=0)
    grad_w_out = jnp.dot(pair_cot, hidden, preferred_element_type=jnp.float32)
    return (features_grad, grad_w_in, grad_b_in, grad_w_out)


def shards(eigvec, species, mode_cot, neighbours, pair_features, w_in, b_in, w_out):
    atom_count = eigvec.shape[0]
    local_modes = eigvec.shape[2]
    slot_count = neighbours.shape[1]
    rim_width = atom_count // 2
    block_size = min(128, atom_count)
    sentinel = atom_count + 2 * rim_width
    inv_root = lax.rsqrt(atom_masses(species))
    scaled = (eigvec.astype(jnp.float32) * inv_root[:, None, None]).astype(jnp.bfloat16)
    weighted = (scaled.astype(jnp.float32) * mode_cot[None, None, :]).astype(jnp.bfloat16)
    flat_rows = scaled.reshape(atom_count, 3 * local_modes)
    extended = with_halo(flat_rows, (("slab", 0),), rim_width)

    def fill_block(step, terms):
        offset = step * block_size
        left = lax.dynamic_slice_in_dim(weighted, offset, block_size, 0)
        own_rows = lax.dynamic_slice_in_dim(scaled, offset, block_size, 0)
        nbr_block = lax.dynamic_slice_in_dim(neighbours, offset, block_size, 0)
        live_mask = (nbr_block < sentinel).astype(jnp.float32)
        row_index = jnp.clip(nbr_block, 0, sentinel - 1)
        partners = jnp.take(extended, row_index.reshape(-1), axis=0).reshape(
            block_size, slot_count * 3, local_modes
        )
        pair_raw = lax.dot_general(
            left, partners, (((2,), (2,)), ((0,), (0,))), preferred_element_type=jnp.float32
        )
        pair_terms = jnp.transpose(
            pair_raw.reshape(block_size, 3, slot_count, 3), (1, 3, 0, 2)
        ).reshape(9, block_size, slot_count)
        self_raw = lax.dot_general(
            left, own_rows, (((2,), (2,)), ((0,), (0,))), preferred_element_type=jnp.float32
        )
        self_terms = jnp.transpose(self_raw, (1, 2, 0)).reshape(9, block_size)
        block_terms = (pair_terms - self_terms[:, :, None]) * live_mask[None]
        return lax.dynamic_update_slice_in_dim(terms, block_terms, offset, 1)

    terms = lax.fori_loop(
        0, atom_count // block_size, fill_block, jnp.zeros((9, atom_count, slot_count), jnp.float32)
    )
    flat = terms.reshape(9, atom_count * slot_count)
    quarter = atom_count // lax.axis_size("mode") * slot_count
    summed_whole = lax.psum(flat.astype(jnp.bfloat16), "mode").astype(jnp.float32)
    summed = lax.dynamic_slice_in_dim(summed_whole, lax.axis_index("mode") * quarter, quarter, 1)
    pair_cot = summed.astype(jnp.bfloat16)
    features_grad, part_w_in, part_b_in, part_w_out = mlp_backward(
        pair_features, pair_cot, w_in, b_in, w_out
    )
    raw_w_in, raw_b_in, raw_w_out = lax.psum((part_w_in, part_b_in, part_w_out), ("slab", "mode"))
    norm_sq = (
        jnp.sum(raw_w_in * raw_w_in) + jnp.sum(raw_b_in * raw_b_in) + jnp.sum(raw_w_out * raw_w_out)
    )
    factor = jnp.minimum(1.0, CLIP_NORM / jnp.sqrt(norm_sq + 1e-06))
    return (features_grad, raw_w_in * factor, raw_b_in * factor, raw_w_out * factor)


def solution(mesh):
    return jax.shard_map(
        shards,
        mesh=mesh,
        in_specs=(
            P("slab", None, "mode"),
            P("slab"),
            P("mode"),
            P("slab", None),
            P(("slab", "mode"), None),
            P(),
            P(),
            P(),
        ),
        out_specs=(P(("slab", "mode"), None), P(), P(), P()),
        check_vma=False,
    )
```

profile of v0, /device:TPU:1, one launch (start us, length us, event | category | flops | bytes accessed | tf_op | source)
XLA Modules:
  0.0 724.8 jit_solution(17617018411366280254)
XLA Ops:
  7.3 4.1 copy.62
  11.4 3.4 multiply_convert_fusion.1
  16.3 2.5 collective-permute-start
  18.8 8.9 %collective-permute-start.1 = (bf16[640,768]{0,1:T(8,128)(2,1)}, bf16[640,768]{0,1:T(8,128)(2,1)}, u32[]{:S(2)}, u32[]{:S(2)}) collective-permute-start(bf16[640,768]{0,1:T(8,128)(2,1)} %bitcast.6), channel_id=1, source_target_pairs={{4,0},{8,4},{12,8},{16,12},{20,16},{24,20},{28,24},{32,28},{36,32}... | collective-permute-start | bytes 2949128 | tf_op jit(solution)/shard_map/ppermute | solution.py:19
  27.7 21.8 %collective-permute-done = bf16[640,768]{0,1:T(8,128)(2,1)} collective-permute-done((bf16[640,768]{0,1:T(8,128)(2,1)}, bf16[640,768]{0,1:T(8,128)(2,1)}, u32[]{:S(2)}, u32[]{:S(2)}) %collective-permute-start) | collective-permute-done | bytes 983072 | tf_op jit(solution)/shard_map/ppermute | solution.py:16
  49.4 3.2 pad_maximum_fusion
  52.7 6.3 copy.64
  59.7 341.2 %while.13 = (s32[]{:T(128)}, bf16[9,1280,16]{1,2,0:T(8,128)(2,1)}, bf16[1280,3,256]{0,2,1:T(8,128)(2,1)}, s32[1280,16]{0,1:T(8,128)}, bf16[2560,768]{1,0:T(8,128...) while((s32[]{:T(128)}, bf16[9,1280,16]{1,2,0:T(8,128)(2,1)}, ...), condition=%wide.region_2.3_spmd, body=%wide.region_1.2_spmd.sunk | while | flops 11681798 | bytes 18693280 | solution.py:85
  60.6 12.8 %gather_fusion = bf16[2048,768]{1,0:T(8,128)(2,1)} fusion(bf16[2560,768]{1,0:T(8,128)(2,1)} %get-tuple-element.260, s32[2048]{0:T(1024)S(1)} %broadcast_clamp_fusion.2), kind=kCustom, calls=%fused_computation.clone.1 | custom fusion | bytes 6299648 | tf_op jit(solution)/shard_map/while/body/eval_jaxpr/jit(_take)/gather | solution.py:69
  73.4 5.9 gather.15
  80.9 1.8 copy.77
  82.9 3.7 fusion.34
  90.1 2.0 convolution_bitcast_fusion.3
  94.8 12.8 %gather_fusion = bf16[2048,768]{1,0:T(8,128)(2,1)} fusion(bf16[2560,768]{1,0:T(8,128)(2,1)} %get-tuple-element.260, s32[2048]{0:T(1024)S(1)} %broadcast_clamp_fusion.2), kind=kCustom, calls=%fused_computation.clone.1 | custom fusion | bytes 6299648 | tf_op jit(solution)/shard_map/while/body/eval_jaxpr/jit(_take)/gather | solution.py:69
  107.5 5.9 gather.15
  115.0 1.8 copy.77
  117.0 3.7 fusion.34
  124.2 2.0 convolution_bitcast_fusion.3
  128.9 12.8 %gather_fusion = bf16[2048,768]{1,0:T(8,128)(2,1)} fusion(bf16[2560,768]{1,0:T(8,128)(2,1)} %get-tuple-element.260, s32[2048]{0:T(1024)S(1)} %broadcast_clamp_fusion.2), kind=kCustom, calls=%fused_computation.clone.1 | custom fusion | bytes 6299648 | tf_op jit(solution)/shard_map/while/body/eval_jaxpr/jit(_take)/gather | solution.py:69
  141.6 5.9 gather.15
  149.2 1.8 copy.77
  151.1 3.7 fusion.34
  158.4 2.0 convolution_bitcast_fusion.3
  163.0 12.8 %gather_fusion = bf16[2048,768]{1,0:T(8,128)(2,1)} fusion(bf16[2560,768]{1,0:T(8,128)(2,1)} %get-tuple-element.260, s32[2048]{0:T(1024)S(1)} %broadcast_clamp_fusion.2), kind=kCustom, calls=%fused_computation.clone.1 | custom fusion | bytes 6299648 | tf_op jit(solution)/shard_map/while/body/eval_jaxpr/jit(_take)/gather | solution.py:69
  175.8 5.9 gather.15
  183.3 1.8 copy.77
  185.3 3.7 fusion.34
  192.5 2.0 convolution_bitcast_fusion.3
  197.1 12.8 %gather_fusion = bf16[2048,768]{1,0:T(8,128)(2,1)} fusion(bf16[2560,768]{1,0:T(8,128)(2,1)} %get-tuple-element.260, s32[2048]{0:T(1024)S(1)} %broadcast_clamp_fusion.2), kind=kCustom, calls=%fused_computation.clone.1 | custom fusion | bytes 6299648 | tf_op jit(solution)/shard_map/while/body/eval_jaxpr/jit(_take)/gather | solution.py:69
  209.9 5.9 gather.15
  217.4 1.8 copy.77
  219.4 3.7 fusion.34
  226.6 2.0 convolution_bitcast_fusion.3
  231.2 12.8 %gather_fusion = bf16[2048,768]{1,0:T(8,128)(2,1)} fusion(bf16[2560,768]{1,0:T(8,128)(2,1)} %get-tuple-element.260, s32[2048]{0:T(1024)S(1)} %broadcast_clamp_fusion.2), kind=kCustom, calls=%fused_computation.clone.1 | custom fusion | bytes 6299648 | tf_op jit(solution)/shard_map/while/body/eval_jaxpr/jit(_take)/gather | solution.py:69
  244.0 5.9 gather.15
  251.5 1.8 copy.77
  253.5 3.7 fusion.34
  260.7 2.0 convolution_bitcast_fusion.3
  265.3 12.8 %gather_fusion = bf16[2048,768]{1,0:T(8,128)(2,1)} fusion(bf16[2560,768]{1,0:T(8,128)(2,1)} %get-tuple-element.260, s32[2048]{0:T(1024)S(1)} %broadcast_clamp_fusion.2), kind=kCustom, calls=%fused_computation.clone.1 | custom fusion | bytes 6299648 | tf_op jit(solution)/shard_map/while/body/eval_jaxpr/jit(_take)/gather | solution.py:69
  278.1 5.9 gather.15
  287.6 3.7 fusion.34
  294.8 2.0 convolution_bitcast_fusion.3
  299.5 12.8 %gather_fusion = bf16[2048,768]{1,0:T(8,128)(2,1)} fusion(bf16[2560,768]{1,0:T(8,128)(2,1)} %get-tuple-element.260, s32[2048]{0:T(1024)S(1)} %broadcast_clamp_fusion.2), kind=kCustom, calls=%fused_computation.clone.1 | custom fusion | bytes 6299648 | tf_op jit(solution)/shard_map/while/body/eval_jaxpr/jit(_take)/gather | solution.py:69
  312.2 5.9 gather.15
  319.8 1.8 copy.77
  321.7 3.7 fusion.34
  328.9 2.0 convolution_bitcast_fusion.3
  333.6 12.8 %gather_fusion = bf16[2048,768]{1,0:T(8,128)(2,1)} fusion(bf16[2560,768]{1,0:T(8,128)(2,1)} %get-tuple-element.260, s32[2048]{0:T(1024)S(1)} %broadcast_clamp_fusion.2), kind=kCustom, calls=%fused_computation.clone.1 | custom fusion | bytes 6299648 | tf_op jit(solution)/shard_map/while/body/eval_jaxpr/jit(_take)/gather | solution.py:69
  346.3 5.9 gather.15
  355.8 3.7 fusion.34
  363.1 2.0 convolution_bitcast_fusion.3
  367.7 12.8 %gather_fusion = bf16[2048,768]{1,0:T(8,128)(2,1)} fusion(bf16[2560,768]{1,0:T(8,128)(2,1)} %get-tuple-element.260, s32[2048]{0:T(1024)S(1)} %broadcast_clamp_fusion.2), kind=kCustom, calls=%fused_computation.clone.1 | custom fusion | bytes 6299648 | tf_op jit(solution)/shard_map/while/body/eval_jaxpr/jit(_take)/gather | solution.py:69
  380.5 5.9 gather.15
  390.0 3.7 fusion.34
  397.2 2.0 convolution_bitcast_fusion.3
  400.9 3.6 copy.66
  404.5 11.8 %convert_element_type.49 = bf16[9,20480]{1,0:T(8,128)(2,1)} reshape(bf16[9,1280,16]{2,1,0:T(8,128)(2,1)} %copy.66) | data formatting | bytes 737280 | tf_op jit(solution)/shard_map/convert_element_type | solution.py:90
  416.6 3.1 convolution_add_fusion
  419.8 39.3 %all-reduce.4.cloned.1.call-done = bf16[9,20480]{1,0:T(8,128)(2,1)} async-done(((bf16[9,20480]{1,0:T(8,128)(2,1)}), bf16[9,20480]{1,0:T(8,128)(2,1)}) %all-reduce.4.cloned.1.call-update) | async-done | bytes 368656 | tf_op jit(solution)/shard_map/psum | solution.py:90
  459.1 4.2 convert_reduce_fusion
  466.4 3.6 convolution_convert_fusion
  470.1 4.1 fusion.8
  474.1 77.8 %all-reduce = (f32[256]{0:T(256)S(1)}, f32[9,256]{1,0:T(8,128)S(1)}) all-reduce(f32[256]{0:T(256)S(1)} %get-tuple-element.187, f32[9,256]{1,0:T(8,128)S(1)} %fusion.8), channel_id=1, replica_groups=mesh['slab'=64,'mode'=4] {'slab','mode'}, use_global_device_ids=true, to_apply=%region_7.8 | all-reduce | flops 2560 | bytes 20480 | tf_op jit(solution)/shard_map/psum | solution.py:96
  553.2 158.3 %all-reduce.6.cloned.1.call-done = f32[128,256]{0,1:T(8,128)} async-done(((f32[128,256]{0,1:T(8,128)}), f32[128,256]{0,1:T(8,128)}) %all-reduce.6.cloned.1.call-update) | async-done | bytes 131088 | tf_op jit(solution)/shard_map/psum | solution.py:96
  (196 shorter events, 96.3 us)
Async XLA Ops:
  7.2 409.4 %copy-start = (bf16[5120,128]{1,0:T(8,128)(2,1)S(1)}, bf16[5120,128]{1,0:T(8,128)(2,1)}, u32[]{:S(2)}) copy-start(bf16[5120,128]{1,0:T(8,128)(2,1)} %param.15) | copy-start | bytes 3932164
  7.2 4.1 copy-start.6
  7.2 4.1 copy-start.3
  7.2 4.2 copy-start.5
  7.2 451.9 %all-reduce.4.cloned.1.call-start = ((), (), s32[]{:S(2)}) async-start(), calls=%async_computation | async-start | bytes 1310720 | tf_op jit(solution)/shard_map/psum | solution.py:90
  16.3 33.1 %collective-permute-start = (bf16[640,768]{0,1:T(8,128)(2,1)}, bf16[640,768]{0,1:T(8,128)(2,1)}, u32[]{:S(2)}, u32[]{:S(2)}) collective-permute-start(bf16[640,768]{0,1:T(8,128)(2,1)} %bitcast.4), channel_id=1, source_target_pairs={{0,4},{4,8},{8,12},{12,16},{16,20},{20,24},{24,28},{28,32},{32,36}... | collective-permute-start | bytes 2949128 | tf_op jit(solution)/shard_map/ppermute | solution.py:16
  18.8 30.6 %collective-permute-start.1 = (bf16[640,768]{0,1:T(8,128)(2,1)}, bf16[640,768]{0,1:T(8,128)(2,1)}, u32[]{:S(2)}, u32[]{:S(2)}) collective-permute-start(bf16[640,768]{0,1:T(8,128)(2,1)} %bitcast.6), channel_id=1, source_target_pairs={{4,0},{8,4},{12,8},{16,12},{20,16},{24,20},{28,24},{32,28},{36,32}... | collective-permute-start | bytes 2949128 | tf_op jit(solution)/shard_map/ppermute | solution.py:19
  400.9 15.7 %copy-start.2 = (bf16[128,256]{1,0:T(8,128)(2,1)S(1)}, bf16[128,256]{1,0:T(8,128)(2,1)}, u32[]{:S(2)}) copy-start(bf16[128,256]{1,0:T(8,128)(2,1)} %param.16) | copy-start | bytes 196612
  400.9 15.8 %copy-start.4 = (f32[256]{0:T(256)S(1)}, f32[256]{0:T(256)}, u32[]{:S(2)}) copy-start(f32[256]{0:T(256)} %param.17) | copy-start | bytes 3076
  416.3 42.8 %copy-start.7 = (bf16[9,256]{1,0:T(8,128)(2,1)S(1)}, bf16[9,256]{1,0:T(8,128)(2,1)}, u32[]{:S(2)}) copy-start(bf16[9,256]{1,0:T(8,128)(2,1)} %param.18) | copy-start | bytes 13828
  416.3 295.2 %all-reduce.6.cloned.1.call-start = ((), (), s32[]{:S(2)}) async-start(), calls=%async_computation.1 | async-start | bytes 262144 | tf_op jit(solution)/shard_map/psum | solution.py:96
  463.3 1.5 copy-start.1
Sparse Core Ops, SparseCore 0:
  416.4 42.6 all-reduce.3
  470.2 241.2 all-reduce.5
where the time goes:
time: 729 us; the launch traced here: 725 us
  local copies, waits for them, and re-layouts  300 us (41%)
  waiting for transfers between devices  219 us (30%)
  blocking collectives  77.8 us (11%)
  matrix products  73.6 us (10%)
  other arithmetic  25.5 us (3%)
  between operations  16.2 us (2%)
  starting transfers between devices  11.6 us (2%)
    gather x20, local copies, waits for them, and re-layouts, fill_block(): jnp.take(extended, row_index.reshape(-1), axis=0)  186 us
    psum x1, waiting for transfers between devices, shards(): lax.psum((part_w_in, part_b_in, part_w_out), ('slab', 'mode'))  158 us
    psum x1, blocking collectives, shards(): lax.psum((part_w_in, part_b_in, part_w_out), ('slab', 'mode'))  77.8 us
    psum x1, waiting for transfers between devices, shards(): lax.psum(flat.astype(jnp.bfloat16), 'mode').astype(jnp.float32)  39.3 us
    dot_general x10, matrix products, fill_block(): lax.dot_general(left, partners, (((2,), (2,)), ((0,), (0,))), preferred_e...  37 us
    dynamic_slice x20, local copies, waits for them, and re-layouts, fill_block(): own_rows = lax.dynamic_slice_in_dim(scaled, offset, block_size, 0)  25.4 us
    ppermute x1, waiting for transfers between devices, with_halo(): lax.ppermute(lax.slice_in_dim(block, block.shape[dim] - width, None, axis...  21.8 us
    dot_general x10, matrix products, fill_block(): lax.dot_general(left, own_rows, (((2,), (2,)), ((0,), (0,))), preferred_e...  20 us
  transfers between devices with their start and end apart: 4, of which 3 were waited for; matrix products, arithmetic and copies ran while one was open for 1% of the time, Pallas kernels for 0%

commit v1 on v0

v1 whole, which is shorter than its diff:
```python
import functools

import jax
import jax.numpy as jnp
from jax import lax
from jax.experimental import pallas as pl
from jax.experimental.pallas import tpu as pltpu
from jax.sharding import PartitionSpec as P

MASS_TABLE = (1.35, 2.94, 2.79, 2.95)
CLIP_NORM = 100.0
T = 128
ATOMS = 1280
RIM = 640
BLOCKS = ATOMS // T
REACH = RIM // T
GROUPS = ATOMS // 8
QUARTER = GROUPS // 4
F32, BF16 = jnp.float32, jnp.bfloat16
VMEM = pl.BlockSpec(memory_space=pltpu.VMEM)
SMEM = pl.BlockSpec(memory_space=pltpu.SMEM)
PARAMS = pltpu.CompilerParams(vmem_limit_bytes=40 << 20)


def nt_dot(x, y):
    return lax.dot_general(x, y, (((1,), (1,)), ((), ())), preferred_element_type=F32)


def tn_dot(x, y):
    return lax.dot_general(x, y, (((0,), (0,)), ((), ())), preferred_element_type=F32)


def scale_kernel(eig, species, high, low):
    def half(base, out):
        for blk in range(REACH):
            rows = slice(base + blk * T, base + (blk + 1) * T)
            kind = species[:, rows]
            mass = jnp.full(kind.shape, MASS_TABLE[3], F32)
            for k in range(3):
                mass = jnp.where(kind == k, MASS_TABLE[k], mass)
            inv = jnp.broadcast_to(lax.rsqrt(mass), (T, T)).T
            inv = jnp.concatenate([inv, inv], axis=1)
            for a in range(3):
                out[a, blk * T:(blk + 1) * T, :] = (eig[a, rows, :].astype(F32) * inv).astype(BF16)

    half(RIM, high)
    half(0, low)


def add_tile(left, right, tile, lane, where_tile, acc):
    dense = nt_dot(left, right)
    here = where_tile == tile
    for a in range(3):
        for b in range(3):
            part = dense[a * T:(a + 1) * T, b * T:(b + 1) * T]
            got = jnp.take_along_axis(part, lane, axis=1, mode="promise_in_bounds")
            acc[3 * a + b] = jnp.where(here, got, acc[3 * a + b])


def fold_matrix():
    row = lax.broadcasted_iota(jnp.int32, (T // 8, T), 0)
    col = lax.broadcasted_iota(jnp.int32, (T // 8, T), 1)
    return (col // 8 == row).astype(BF16)


def own_kernel(high, low, mode_cot, nbr_t, out, weighted, lane_ref, tile_ref, stack, acc):
    row = lax.broadcasted_iota(jnp.int32, (T, T), 0)
    col = lax.broadcasted_iota(jnp.int32, (T, T), 1)
    diagonal = (row % 8) == (col // 16)
    cot = mode_cot[...]
    for blk in range(BLOCKS):
        n = nbr_t[:, blk * T:(blk + 1) * T].astype(F32)
        n = jnp.concatenate([n] * 8, axis=0).T.astype(jnp.int32)
        live = diagonal & (n < ATOMS + 2 * RIM)
        tile_ref[blk] = jnp.where(live, n >> 7, -1)
        lane_ref[blk] = n & (T - 1)
        src, base = (low, blk * T) if blk < REACH else (high, blk * T - RIM)
        for a in range(3):
            s = src[a, base:base + T, :]
            stack[blk, a * T:(a + 1) * T, :] = s
            weighted[blk, a * T:(a + 1) * T, :] = (s.astype(F32) * cot).astype(BF16)
    fold = fold_matrix()

    def block(i, carry):
        left = weighted[i]
        lane, where_tile = lane_ref[i], tile_ref[i]
        acc[...] = jnp.zeros_like(acc)

        def tile(j, carry):
            add_tile(left, stack[j], j + REACH, lane, where_tile, acc)
            return carry

        lax.fori_loop(jnp.maximum(i - REACH, 0), jnp.minimum(i + REACH, BLOCKS - 1) + 1, tile, 0)
        mine = stack[i]
        live = where_tile >= 0
        for a in range(3):
            for b in range(3):
                both = left[a * T:(a + 1) * T].astype(F32) * mine[b * T:(b + 1) * T].astype(F32)
                self_term = jnp.sum(both, axis=1, keepdims=True)
                term = jnp.where(live, acc[3 * a + b] - self_term, 0.0)
                folded = jnp.dot(fold, term.astype(BF16), preferred_element_type=F32)
                out[3 * a + b, pl.ds(pl.multiple_of(i * 16, 16), 16), :] = folded
        return carry

    lax.fori_loop(0, BLOCKS, block, 0)


def halo_kernel(mode_index, below, above, weighted, lane_ref, tile_ref, own,
                out0, out1, out2, out3, acc, total):
    fold = fold_matrix()

    def block(src, shift, lo, hi, i):
        left = weighted[i]
        lane, where_tile = lane_ref[i], tile_ref[i]
        acc[...] = jnp.zeros_like(acc)

        def tile(t, carry):
            rows = pl.ds(pl.multiple_of((t - shift) * T, T), T)
            right = jnp.concatenate([src[b, rows, :] for b in range(3)], axis=0)
            add_tile(left, right, t, lane, where_tile, acc)
            return carry

        lax.fori_loop(lo, hi, tile, 0)
        at = pl.ds(pl.multiple_of(i * 16, 16), 16)
        for c in range(9):
            folded = jnp.dot(fold, acc[c].astype(BF16), preferred_element_type=F32)
            total[c, at, :] = own[c, at, :] + folded

    def low_block(i, carry):
        block(below, 0, i, REACH, i)
        return carry

    def high_block(i, carry):
        block(above, 3 * REACH, 3 * REACH, i + 2 * REACH + 1, i)
        return carry

    lax.fori_loop(0, REACH, low_block, 0)
    lax.fori_loop(REACH, BLOCKS, high_block, 0)
    m = mode_index[0]
    for k, out in enumerate((out0, out1, out2, out3)):
        q = lax.rem(m + k, 4)
        out[...] = total[:, pl.ds(pl.multiple_of(q * QUARTER, 8), QUARTER), :].astype(BF16)


CHUNK = 512


def forward_kernel(features, w_in, b_in, hidden, slope):
    pre = jnp.dot(features[...], w_in[...], preferred_element_type=F32) + b_in[...]
    sig = 1.0 / (1.0 + jnp.exp(-pre))
    hidden[...] = (pre * sig).astype(BF16)
    slope[...] = (sig * (1.0 + pre * (1.0 - sig))).astype(BF16)


def backward_kernel(mode_index, p0, p1, p2, p3, features, hidden, slope, w_in, w_out,
                    grad, g0, g1, g2, g3, cot, sums):
    step = pl.program_id(0)

    @pl.when(step == 0)
    def _():
        whole = sum(p[...].astype(F32) for p in (p0, p1, p2, p3))
        whole = jnp.concatenate([whole, jnp.zeros((7, QUARTER, T), F32)], axis=0)
        cot[...] = jnp.swapaxes(whole, 0, 1).astype(BF16)
        sums[...] = jnp.zeros_like(sums)

    per = CHUNK // T
    pair_cot = jnp.concatenate([cot[step * per + g] for g in range(per)], axis=1)
    pre_cot32 = tn_dot(pair_cot, w_out[...]) * slope[...].astype(F32)
    pre_cot = pre_cot32.astype(BF16)
    grad[...] = nt_dot(pre_cot, w_in[...]).astype(BF16)
    part_in = tn_dot(features[...], pre_cot)
    part_out = jnp.dot(pair_cot, hidden[...], preferred_element_type=F32)
    part_b = jnp.sum(pre_cot.astype(F32), axis=0, keepdims=True)
    part_b = jnp.concatenate([part_b, jnp.zeros((7, 256), F32)], axis=0)
    for h in range(2):
        cols = slice(h * T, (h + 1) * T)
        sums[h * 152:h * 152 + 128, :] += part_in[:, cols]
        sums[h * 152 + 128:h * 152 + 144, :] += part_out[:, cols]
        sums[h * 152 + 144:h * 152 + 152, :] += part_b[:, cols]

    @pl.when(step == pl.num_programs(0) - 1)
    def _():
        m = mode_index[0]
        for k, out in enumerate((g0, g1, g2, g3)):
            q = lax.rem(m + k, 4)
            out[...] = sums[pl.ds(pl.multiple_of(q * ROWS, 8), ROWS), :]


SUM_ROWS = 320
ROWS = SUM_ROWS // 4


def finish_kernel(mode_index, c0, c1, c2, c3, grad_w_in, grad_b_in, grad_w_out, whole):
    m = mode_index[0]
    for k, part in enumerate((c0, c1, c2, c3)):
        q = lax.rem(m + 4 - k, 4)
        whole[pl.ds(pl.multiple_of(q * ROWS, 8), ROWS), :] = part[...]
    both = []
    for start, rows in ((0, 128), (128, 9), (144, 1)):
        both.append(jnp.concatenate([whole[h * 152 + start:h * 152 + start + rows, :] for h in range(2)], axis=1))
    w, o, b = both
    norm_sq = jnp.sum(w * w) + jnp.sum(b * b) + jnp.sum(o * o)
    factor = jnp.minimum(1.0, CLIP_NORM / jnp.sqrt(jnp.broadcast_to(norm_sq + 1e-06, (1, 256))))
    grad_w_in[...] = w * factor
    grad_b_in[...] = b * factor
    grad_w_out[...] = o * factor


def shape(dims, dtype=F32):
    return jax.ShapeDtypeStruct(dims, dtype)


def cost(flops, moved):
    return pl.CostEstimate(flops=flops, bytes_accessed=moved, transcendentals=0)


def ring(axis, k):
    n = lax.axis_size(axis)
    return [(i, (i + k) % n) for i in range(n)]


def shards(eigvec, species, mode_cot, neighbours, pair_features, w_in, b_in, w_out):
    eig = jnp.transpose(eigvec, (1, 0, 2))
    m = lax.axis_index("mode").astype(jnp.int32).reshape(1)
    high, low = pl.pallas_call(
        scale_kernel, out_shape=[shape((3, RIM, 256), BF16)] * 2,
        in_specs=[VMEM] * 2, out_specs=[VMEM] * 2, compiler_params=PARAMS,
        cost_estimate=cost(1 << 20, 4 << 20), name="scale",
    )(eig, species.reshape(1, ATOMS))
    below = lax.ppermute(high, "slab", ring("slab", 1))
    above = lax.ppermute(low, "slab", ring("slab", lax.axis_size("slab") - 1))
    own, weighted, lane, tile = pl.pallas_call(
        own_kernel,
        out_shape=[shape((9, GROUPS, T)), shape((BLOCKS, 3 * T, 256), BF16),
                   shape((BLOCKS, T, T), jnp.int32), shape((BLOCKS, T, T), jnp.int32)],
        in_specs=[VMEM] * 4, out_specs=[VMEM] * 4,
        scratch_shapes=[pltpu.VMEM((BLOCKS, 3 * T, 256), BF16), pltpu.VMEM((9, T, T), F32)],
        compiler_params=PARAMS, cost_estimate=cost(12_000_000_000, 6 << 20), name="own",
    )(high, low, mode_cot.reshape(1, 256), neighbours.T)
    slots = pair_features.shape[0]
    steps = slots // CHUNK
    rows_spec = lambda width: pl.BlockSpec((CHUNK, width), lambda s: (s, 0))
    full = lambda *dims: pl.BlockSpec(dims, lambda s: (0,) * len(dims))
    hidden, slope = pl.pallas_call(
        forward_kernel, out_shape=[shape((slots, 256), BF16)] * 2, grid=(steps,),
        in_specs=[rows_spec(128), full(128, 256), full(1, 256)], out_specs=[rows_spec(256)] * 2,
        compiler_params=PARAMS, cost_estimate=cost(4_000_000_000, 7 << 20), name="forward",
    )(pair_features, w_in, b_in.reshape(1, 256))
    parts = pl.pallas_call(
        halo_kernel, out_shape=[shape((9, QUARTER, T), BF16)] * 4,
        in_specs=[SMEM] + [VMEM] * 6, out_specs=[VMEM] * 4,
        scratch_shapes=[pltpu.VMEM((9, T, T), F32), pltpu.VMEM((9, GROUPS, T), F32)],
        compiler_params=PARAMS, cost_estimate=cost(5_000_000_000, 6 << 20), name="halo",
    )(m, below, above, weighted, lane, tile, own)
    parts = [parts[0]] + [lax.ppermute(parts[k], "mode", ring("mode", k)) for k in (1, 2, 3)]
    w_out16 = jnp.concatenate([w_out, jnp.zeros((7, 256), BF16)], axis=0)
    features_grad, *sums = pl.pallas_call(
        backward_kernel,
        out_shape=[shape((slots, 128), BF16)] + [shape((ROWS, T))] * 4, grid=(steps,),
        in_specs=[SMEM] + [full(9, QUARTER, T)] * 4
        + [rows_spec(128), rows_spec(256), rows_spec(256), full(128, 256), full(16, 256)],
        out_specs=[rows_spec(128)] + [full(ROWS, T)] * 4,
        scratch_shapes=[pltpu.VMEM((QUARTER, 16, T), BF16), pltpu.VMEM((SUM_ROWS, T), F32)],
        compiler_params=PARAMS, cost_estimate=cost(2_000_000_000, 9 << 20), name="backward",
    )(m, *parts, pair_features, hidden, slope, w_in, w_out16)
    share = sums[0]
    for k in (1, 2, 3):
        share = share + lax.ppermute(sums[k], "mode", ring("mode", k))
    line = [[g * 8 + k for k in range(8)] for g in range(8)]
    plane = [[k * 8 + g for k in range(8)] for g in range(8)]
    for groups in (line, plane):
        spread = jnp.broadcast_to(share[None], (8, ROWS, T))
        got = lax.all_to_all(spread, "slab", 0, 0, axis_index_groups=groups, tiled=True)
        share = jnp.sum(got, axis=0)
    pieces = [share] + [lax.ppermute(share, "mode", ring("mode", k)) for k in (1, 2, 3)]
    grad_w_in, grad_b_in, grad_w_out = pl.pallas_call(
        finish_kernel, out_shape=[shape((128, 256)), shape((1, 256)), shape((9, 256))],
        in_specs=[SMEM] + [VMEM] * 4, out_specs=[VMEM] * 3,
        scratch_shapes=[pltpu.VMEM((SUM_ROWS, T), F32)],
        compiler_params=PARAMS, name="finish",
    )(m, *pieces)
    return (features_grad, grad_w_in, grad_b_in.reshape(256), grad_w_out)


def solution(mesh):
    return jax.shard_map(
        shards,
        mesh=mesh,
        in_specs=(
            P("slab", None, "mode"),
            P("slab"),
            P("mode"),
            P("slab", None),
            P(("slab", "mode"), None),
            P(),
            P(),
            P(),
        ),
        out_specs=(P(("slab", "mode"), None), P(), P(), P()),
        check_vma=False,
    )
```

time: 729 us -> 139 us (0.19)
  local copies, waits for them, and re-layouts: 300 us -> 2.34 us
  waiting for transfers between devices: 219 us -> 6.24 us
  Pallas kernels: 0 us -> 81.6 us
  matrix products: 73.6 us -> 0 us
  blocking collectives: 77.8 us -> 30.2 us
  other arithmetic: 25.5 us -> 0.05 us
  between operations: 16.2 us -> 0.77 us
    psum x2 -> x0, waiting for transfers between devices: 198 us -> none  [the longest x1 158 us: shards(): lax.psum((part_w_in, part_b_in, part_w_out), ('slab', 'mode'))]
    gather x20 -> x0, local copies, waits for them, and re-layouts: 186 us -> none  [fill_block(): jnp.take(extended, row_index.reshape(-1), axis=0)]
    pallas_call x0 -> x6, Pallas kernels: none -> 81.6 us  [the longest x1 50.3 us: shards(): pl.pallas_call(own_kernel, out_shape=[shape((9, GROUPS, T)), shape((BLOCK...]
    psum x1 -> x0, blocking collectives: 77.8 us -> none  [shards(): lax.psum((part_w_in, part_b_in, part_w_out), ('slab', 'mode'))]
    dot_general x25 -> x0, matrix products: 73.6 us -> none  [the longest x10 37 us: fill_block(): lax.dot_general(left, partners, (((2,), (2,)), ((0,), (0,))), preferred_e...]
    dynamic_slice x30 -> x0, local copies, waits for them, and re-layouts: 43.5 us -> none  [the longest x20 25.4 us: fill_block(): own_rows = lax.dynamic_slice_in_dim(scaled, offset, block_size, 0)]
    all_to_all x0 -> x2, blocking collectives: none -> 30.2 us  [shards(): lax.all_to_all(spread, 'slab', 0, 0, axis_index_groups=groups, tiled=True)]
    transpose x20 -> x0, local copies, waits for them, and re-layouts: 19.3 us -> none  [the longest x10 10.3 us: fill_block(): self_terms = jnp.transpose(self_raw, (1, 2, 0)).reshape(9, block_size)]
  transfers between devices with their start and end apart: 4 -> 11, of which waited for: 3 -> 7; matrix products, arithmetic and copies ran while one was open for 1% -> 0% of each run, Pallas kernels for 0% -> 39%
where the time goes in v1:
time: 139 us
  Pallas kernels  81.6 us (59%)
  blocking collectives  30.2 us (22%)
  starting transfers between devices  18 us (13%)
  waiting for transfers between devices  6.24 us (4%)
  local copies, waits for them, and re-layouts  2.34 us (2%)
    pallas_call x1, Pallas kernels, shards(): pl.pallas_call(own_kernel, out_shape=[shape((9, GROUPS, T)), shape((BLOCK...  50.3 us
    all_to_all x2, blocking collectives, shards(): lax.all_to_all(spread, 'slab', 0, 0, axis_index_groups=groups, tiled=True)  30.2 us
    pallas_call x1, Pallas kernels, shards(): pl.pallas_call(halo_kernel, out_shape=[shape((9, QUARTER, T), BF16)] * 4,...  19.3 us
    ppermute x1, starting transfers between devices, shards(): above = lax.ppermute(low, 'slab', ring('slab', lax.axis_size('slab') - 1))  8.85 us
    pallas_call x1, Pallas kernels, shards(): pl.pallas_call(backward_kernel, out_shape=[shape((slots, 128), BF16)] + [...  6.22 us
    pallas_call x1, Pallas kernels, shards(): pl.pallas_call(forward_kernel, out_shape=[shape((slots, 256), BF16)] * 2,...  3.72 us
    ppermute x3, waiting for transfers between devices, shards(): share = share + lax.ppermute(sums[k], 'mode', ring('mode', k))  3.3 us
    ppermute x3, starting transfers between devices, shards(): lax.ppermute(share, 'mode', ring('mode', k))  3.22 us
  transfers between devices with their start and end apart: 11, of which 7 were waited for; matrix products, arithmetic and copies ran while one was open for 0% of the time, Pallas kernels for 39%

profile of v1, /device:TPU:1, one launch (start us, length us, event | category | flops | bytes accessed | tf_op | source)
XLA Modules:
  0.0 139.2 jit_solution(13293997090657036591)
XLA Ops:
  0.6 0.0 copy-start.4
  0.6 0.7 reshape.26.species
  1.3 0.0 copy-start
  1.4 1.5 %copy-done = bf16[1280,3,256]{2,0,1:T(8,128)(2,1)S(1)} copy-done((bf16[1280,3,256]{2,0,1:T(8,128)(2,1)S(1)}, bf16[1280,3,256]{2,0,1:T(8,128)(2,1)}, u32[]{:S(2)}) %copy-start) | copy-done | bytes 1966104
  2.9 0.0 copy-start.2
  2.9 1.2 scale.1
  4.1 2.5 %collective-permute-start = (bf16[3,640,256]{2,1,0:T(8,128)(2,1)}, bf16[3,640,256]{2,1,0:T(8,128)(2,1)S(1)}, u32[]{:S(2)}, u32[]{:S(2)}) collective-permute-start(bf16[3,640,256]{2,1,0:T(8,128)(2,1)} %get-tuple-element.24.high), channel_id=1, source_target_pairs={{0,4},{4,8},{8,12},{12,16},{16,20},{20,24},{24,28},{28,32},{32,36}... | collective-permute-start | bytes 2949128 | tf_op jit(solution)/shard_map/ppermute | solution.py:230
  6.6 8.9 %collective-permute-start.1 = (bf16[3,640,256]{2,1,0:T(8,128)(2,1)S(1)}, bf16[3,640,256]{2,1,0:T(8,128)(2,1)S(1)}, u32[]{:S(2)}, u32[]{:S(2)}) collective-permute-start(bf16[3,640,256]{2,1,0:T(8,128)(2,1)S(1)} %get-tuple-element.25.low), channel_id=1, source_target_pairs={{0,252},{4,0},{8,4},{12,8},{16,12},{20,16},{24,20},{28,24},{32,28}... | collective-permute-start | bytes 2949128 | tf_op jit(solution)/shard_map/ppermute | solution.py:231
  15.4 0.0 copy-done.4
  15.4 0.0 copy-done.2
  15.4 50.3 %own.1 = (f32[9,160,128]{2,1,0:T(8,128)S(1)}, bf16[10,384,256]{2,1,0:T(8,128)(2,1)S(1)}, s32[10,128,128]{2,1,0:T(8,128)S(1)}, s32[10,128,128]{2,1,0:T(8,128)S(1)}) custom-call(bf16[3,640,256]{2,1,0:T(8,128)(2,1)} %get-tuple-element.24.high, bf16[3,640,256]{2,1,0:T(8,128)(2,1)S(1)} %get-tuple-element.25.low, f32[1,256]{1,0:T(1,128)S(1)} %bitcast.8, ...), custom_call_target="tpu_custom_call" | custom-call | flops 12000000000 | bytes 6291456 | tf_op jit(solution)/shard_map/own/pallas_call | solution.py:232
  65.7 0.0 collective-permute-done.below
  65.7 0.0 collective-permute-done.1.above
  65.7 0.0 copy-start.1
  65.8 0.0 copy-start.3
  65.8 0.0 copy-start.5
  65.8 19.3 %halo.1 = (bf16[9,40,128]{2,1,0:T(8,128)(2,1)S(1)}, bf16[9,40,128]{2,1,0:T(8,128)(2,1)S(1)}, bf16[9,40,128]{2,1,0:T(8,128)(2,1)S(1)}, bf16[9,40,128]{2,1,0:T(8,128)(2,1)S(1)}) custom-call(s32[1]{0:T(128)} %bitcast.mode_index, bf16[3,640,256]{2,1,0:T(8,128)(2,1)S(1)} %collective-permute-done.below, bf16[3,640,256]{2,1,0:T(8,128)(2,1)S(1)} %collective-permute-done.1.above, ...), custom_call_target="tpu_custom_call" | custom-call | flops 5000000000 | bytes 6291456 | tf_op jit(solution)/shard_map/halo/pallas_call | solution.py:249
  85.1 1.2 collective-permute-start.2
  86.3 1.2 collective-permute-start.3
  87.5 0.0 collective-permute-start.4
  87.5 0.0 copy-done.1
  87.5 0.0 copy-done.3
  87.5 0.0 copy-done.5
  87.5 0.0 copy-start.6
  87.5 3.7 %forward.1 = (bf16[5120,256]{1,0:T(8,128)(2,1)S(1)}, bf16[5120,256]{1,0:T(8,128)(2,1)S(1)}) custom-call(bf16[5120,128]{1,0:T(8,128)(2,1)S(1)} %copy-done.1, bf16[128,256]{1,0:T(8,128)(2,1)S(1)} %copy-done.3, f32[1,256]{1,0:T(1,128)S(1)} %bitcast.9), custom_call_target="tpu_custom_call" | custom-call | flops 4000000000 | bytes 7340032 | tf_op jit(solution)/shard_map/forward/pallas_call | solution.py:244
  91.3 0.0 copy-done.6
  91.3 0.0 collective-permute-done.2.p1
  91.3 0.5 collective-permute-done.3.p2
  91.8 0.6 collective-permute-done.4.p3
  92.4 6.2 %backward.1 = (bf16[5120,128]{1,0:T(8,128)(2,1)}, f32[80,128]{1,0:T(8,128)S(1)}, f32[80,128]{1,0:T(8,128)S(1)}, f32[80,128]{1,0:T(8,128)S(1)}, f32[80,128]{1,0:T(8,128)S(1)}) custom-call(s32[1]{0:T(128)} %bitcast.mode_index, bf16[9,40,128]{2,1,0:T(8,128)(2,1)S(1)} %get-tuple-element.30.p0, bf16[9,40,128]{2,1,0:T(8,128)(2,1)S(1)} %collective-permute-done.2.p1, ...), custom_call_target="tpu_custom_call" | custom-call | flops 2000000000 | bytes 9437184 | tf_op jit(solution)/shard_map/backward/pallas_call | solution.py:257
  98.6 0.7 collective-permute-start.5
  99.3 0.3 collective-permute-start.6
  99.6 0.1 collective-permute-start.7
  99.7 0.7 collective-permute-done.5
  100.4 2.2 %collective-permute-done.6 = f32[80,128]{1,0:T(8,128)S(1)} collective-permute-done((f32[80,128]{1,0:T(8,128)S(1)}, f32[80,128]{1,0:T(8,128)S(1)}, u32[]{:S(2)}, u32[]{:S(2)}) %collective-permute-start.6) | collective-permute-done | bytes 40992 | tf_op jit(solution)/shard_map/ppermute | solution.py:268
  102.6 0.4 collective-permute-done.7
  103.1 16.1 %all_to_all.10 = f32[8,80,128]{2,1,0:T(8,128)S(1)} all-to-all(f32[8,80,128]{2,1,0:T(8,128)S(1)} %broadcast_in_dim.4), channel_id=1, replica_groups={{0,4,8,12,16,20,24,28},{32,36,40,44,48,52,56,60},{64,68,72,76,80,84,88,..., dimensions={0} | all-to-all | bytes 655360 | tf_op jit(solution)/shard_map/all_to_all | solution.py:273
  119.3 14.0 %all_to_all.11 = f32[8,80,128]{2,1,0:T(8,128)S(1)} all-to-all(f32[8,80,128]{2,1,0:T(8,128)S(1)} %broadcast_in_dim.5), channel_id=1, replica_groups={{0,32,64,96,128,160,192,224},{4,36,68,100,132,164,196,228},{8,40,72,104..., dimensions={0} | all-to-all | bytes 655360 | tf_op jit(solution)/shard_map/all_to_all | solution.py:273
  133.3 1.8 %collective-permute-start.10 = (f32[80,128]{1,0:T(8,128)S(1)}, f32[80,128]{1,0:T(8,128)S(1)}, u32[]{:S(2)}, u32[]{:S(2)}) collective-permute-start(f32[80,128]{1,0:T(8,128)S(1)} %reduce_sum.19.c0), channel_id=1, source_target_pairs={{0,3},{1,0},{2,1},{3,2},{4,7},{5,4},{6,5},{7,6},{8,11},{9,8},{10,9... | collective-permute-start | bytes 122888 | tf_op jit(solution)/shard_map/ppermute | solution.py:275
  135.1 0.0 collective-permute-start.8
  135.2 1.4 %collective-permute-start.9 = (f32[80,128]{1,0:T(8,128)S(1)}, f32[80,128]{1,0:T(8,128)S(1)}, u32[]{:S(2)}, u32[]{:S(2)}) collective-permute-start(f32[80,128]{1,0:T(8,128)S(1)} %reduce_sum.19.c0), channel_id=1, source_target_pairs={{0,2},{1,3},{2,0},{3,1},{4,6},{5,7},{6,4},{7,5},{8,10},{9,11},{10,... | collective-permute-start | bytes 122888 | tf_op jit(solution)/shard_map/ppermute | solution.py:275
  136.5 0.3 collective-permute-done.10.c3
  136.8 0.0 collective-permute-done.8.c1
  136.8 1.5 %collective-permute-done.9.c2 = f32[80,128]{1,0:T(8,128)S(1)} collective-permute-done((f32[80,128]{1,0:T(8,128)S(1)}, f32[80,128]{1,0:T(8,128)S(1)}, u32[]{:S(2)}, u32[]{:S(2)}) %collective-permute-start.9) | collective-permute-done | bytes 40992 | tf_op jit(solution)/shard_map/ppermute | solution.py:275
  138.4 0.9 finish.1
  (6 shorter events, 0.1 us)
Async XLA Ops:
  0.6 14.8 %copy-start.4 = (f32[256]{0:T(256)S(1)}, f32[256]{0:T(256)}, u32[]{:S(2)}) copy-start(f32[256]{0:T(256)} %param.10) | copy-start | bytes 3076
  1.3 1.5 %copy-start = (bf16[1280,3,256]{2,0,1:T(8,128)(2,1)S(1)}, bf16[1280,3,256]{2,0,1:T(8,128)(2,1)}, u32[]{:S(2)}) copy-start(bf16[1280,3,256]{2,0,1:T(8,128)(2,1)} %param.8) | copy-start | bytes 5898244
  2.9 12.5 %copy-start.2 = (s32[1280,16]{0,1:T(8,128)S(1)}, s32[1280,16]{0,1:T(8,128)}, u32[]{:S(2)}) copy-start(s32[1280,16]{0,1:T(8,128)} %param.11) | copy-start | bytes 245764
  4.1 61.6 %collective-permute-start = (bf16[3,640,256]{2,1,0:T(8,128)(2,1)}, bf16[3,640,256]{2,1,0:T(8,128)(2,1)S(1)}, u32[]{:S(2)}, u32[]{:S(2)}) collective-permute-start(bf16[3,640,256]{2,1,0:T(8,128)(2,1)} %get-tuple-element.24.high), channel_id=1, source_target_pairs={{0,4},{4,8},{8,12},{12,16},{16,20},{20,24},{24,28},{28,32},{32,36}... | collective-permute-start | bytes 2949128 | tf_op jit(solution)/shard_map/ppermute | solution.py:230
  6.6 59.2 %collective-permute-start.1 = (bf16[3,640,256]{2,1,0:T(8,128)(2,1)S(1)}, bf16[3,640,256]{2,1,0:T(8,128)(2,1)S(1)}, u32[]{:S(2)}, u32[]{:S(2)}) collective-permute-start(bf16[3,640,256]{2,1,0:T(8,128)(2,1)S(1)} %get-tuple-element.25.low), channel_id=1, source_target_pairs={{0,252},{4,0},{8,4},{12,8},{16,12},{20,16},{24,20},{28,24},{32,28}... | collective-permute-start | bytes 2949128 | tf_op jit(solution)/shard_map/ppermute | solution.py:231
  65.7 21.8 %copy-start.1 = (bf16[5120,128]{1,0:T(8,128)(2,1)S(1)}, bf16[5120,128]{1,0:T(8,128)(2,1)}, u32[]{:S(2)}) copy-start(bf16[5120,128]{1,0:T(8,128)(2,1)} %features.3) | copy-start | bytes 3932164
  65.8 21.7 %copy-start.3 = (bf16[128,256]{1,0:T(8,128)(2,1)S(1)}, bf16[128,256]{1,0:T(8,128)(2,1)}, u32[]{:S(2)}) copy-start(bf16[128,256]{1,0:T(8,128)(2,1)} %w_in.3) | copy-start | bytes 196612
  65.8 21.7 %copy-start.5 = (f32[256]{0:T(256)S(1)}, f32[256]{0:T(256)}, u32[]{:S(2)}) copy-start(f32[256]{0:T(256)} %param.14) | copy-start | bytes 3076
  85.1 6.2 %collective-permute-start.2 = (bf16[9,40,128]{2,1,0:T(8,128)(2,1)S(1)}, bf16[9,40,128]{2,1,0:T(8,128)(2,1)S(1)}, u32[]{:S(2)}, u32[]{:S(2)}) collective-permute-start(bf16[9,40,128]{2,1,0:T(8,128)(2,1)S(1)} %get-tuple-element.31), channel_id=1, source_target_pairs={{0,1},{1,2},{2,3},{3,0},{4,5},{5,6},{6,7},{7,4},{8,9},{9,10},{10,1... | collective-permute-start | bytes 276488 | tf_op jit(solution)/shard_map/ppermute | solution.py:255
  86.3 5.4 %collective-permute-start.3 = (bf16[9,40,128]{2,1,0:T(8,128)(2,1)S(1)}, bf16[9,40,128]{2,1,0:T(8,128)(2,1)S(1)}, u32[]{:S(2)}, u32[]{:S(2)}) collective-permute-start(bf16[9,40,128]{2,1,0:T(8,128)(2,1)S(1)} %get-tuple-element.32), channel_id=1, source_target_pairs={{0,2},{1,3},{2,0},{3,1},{4,6},{5,7},{6,4},{7,5},{8,10},{9,11},{10,... | collective-permute-start | bytes 276488 | tf_op jit(solution)/shard_map/ppermute | solution.py:255
  87.5 4.9 %collective-permute-start.4 = (bf16[9,40,128]{2,1,0:T(8,128)(2,1)S(1)}, bf16[9,40,128]{2,1,0:T(8,128)(2,1)S(1)}, u32[]{:S(2)}, u32[]{:S(2)}) collective-permute-start(bf16[9,40,128]{2,1,0:T(8,128)(2,1)S(1)} %get-tuple-element.33), channel_id=1, source_target_pairs={{0,3},{1,0},{2,1},{3,2},{4,7},{5,4},{6,5},{7,6},{8,11},{9,8},{10,9... | collective-permute-start | bytes 276488 | tf_op jit(solution)/shard_map/ppermute | solution.py:255
  87.5 3.7 %copy-start.6 = (bf16[9,256]{1,0:T(8,128)(2,1)S(1)}, bf16[9,256]{1,0:T(8,128)(2,1)}, u32[]{:S(2)}) copy-start(bf16[9,256]{1,0:T(8,128)(2,1)} %param.15) | copy-start | bytes 13828
  98.6 1.8 %collective-permute-start.5 = (f32[80,128]{1,0:T(8,128)S(1)}, f32[80,128]{1,0:T(8,128)S(1)}, u32[]{:S(2)}, u32[]{:S(2)}) collective-permute-start(f32[80,128]{1,0:T(8,128)S(1)} %get-tuple-element.38), channel_id=1, source_target_pairs={{0,1},{1,2},{2,3},{3,0},{4,5},{5,6},{6,7},{7,4},{8,9},{9,10},{10,1... | collective-permute-start | bytes 122888 | tf_op jit(solution)/shard_map/ppermute | solution.py:268
  99.3 3.3 %collective-permute-start.6 = (f32[80,128]{1,0:T(8,128)S(1)}, f32[80,128]{1,0:T(8,128)S(1)}, u32[]{:S(2)}, u32[]{:S(2)}) collective-permute-start(f32[80,128]{1,0:T(8,128)S(1)} %get-tuple-element.39), channel_id=1, source_target_pairs={{0,2},{1,3},{2,0},{3,1},{4,6},{5,7},{6,4},{7,5},{8,10},{9,11},{10,... | collective-permute-start | bytes 122888 | tf_op jit(solution)/shard_map/ppermute | solution.py:268
  99.6 3.4 %collective-permute-start.7 = (f32[80,128]{1,0:T(8,128)S(1)}, f32[80,128]{1,0:T(8,128)S(1)}, u32[]{:S(2)}, u32[]{:S(2)}) collective-permute-start(f32[80,128]{1,0:T(8,128)S(1)} %get-tuple-element.40), channel_id=1, source_target_pairs={{0,3},{1,0},{2,1},{3,2},{4,7},{5,4},{6,5},{7,6},{8,11},{9,8},{10,9... | collective-permute-start | bytes 122888 | tf_op jit(solution)/shard_map/ppermute | solution.py:268
  133.3 3.5 %collective-permute-start.10 = (f32[80,128]{1,0:T(8,128)S(1)}, f32[80,128]{1,0:T(8,128)S(1)}, u32[]{:S(2)}, u32[]{:S(2)}) collective-permute-start(f32[80,128]{1,0:T(8,128)S(1)} %reduce_sum.19.c0), channel_id=1, source_target_pairs={{0,3},{1,0},{2,1},{3,2},{4,7},{5,4},{6,5},{7,6},{8,11},{9,8},{10,9... | collective-permute-start | bytes 122888 | tf_op jit(solution)/shard_map/ppermute | solution.py:275
  135.1 1.7 %collective-permute-start.8 = (f32[80,128]{1,0:T(8,128)S(1)}, f32[80,128]{1,0:T(8,128)S(1)}, u32[]{:S(2)}, u32[]{:S(2)}) collective-permute-start(f32[80,128]{1,0:T(8,128)S(1)} %reduce_sum.19.c0), channel_id=1, source_target_pairs={{0,1},{1,2},{2,3},{3,0},{4,5},{5,6},{6,7},{7,4},{8,9},{9,10},{10,1... | collective-permute-start | bytes 122888 | tf_op jit(solution)/shard_map/ppermute | solution.py:275
  135.2 3.2 %collective-permute-start.9 = (f32[80,128]{1,0:T(8,128)S(1)}, f32[80,128]{1,0:T(8,128)S(1)}, u32[]{:S(2)}, u32[]{:S(2)}) collective-permute-start(f32[80,128]{1,0:T(8,128)S(1)} %reduce_sum.19.c0), channel_id=1, source_target_pairs={{0,2},{1,3},{2,0},{3,1},{4,6},{5,7},{6,4},{7,5},{8,10},{9,11},{10,... | collective-permute-start | bytes 122888 | tf_op jit(solution)/shard_map/ppermute | solution.py:275

commit v2 on v1

--- a/solution.py
+++ b/solution.py
@@ -30,6 +30,9 @@
     return lax.dot_general(x, y, (((0,), (0,)), ((), ())), preferred_element_type=F32)
 
 
+STRIP = 3 * T
+
+
 def scale_kernel(eig, species, high, low):
     def half(base, out):
         for blk in range(REACH):
@@ -41,29 +44,90 @@
             inv = jnp.broadcast_to(lax.rsqrt(mass), (T, T)).T
             inv = jnp.concatenate([inv, inv], axis=1)
             for a in range(3):
-                out[a, blk * T:(blk + 1) * T, :] = (eig[a, rows, :].astype(F32) * inv).astype(BF16)
+                at = blk * STRIP + a * T
+                out[at:at + T, :] = (eig[a, rows, :].astype(F32) * inv).astype(BF16)
 
     half(RIM, high)
     half(0, low)
 
 
-def add_tile(left, right, tile, lane, where_tile, acc):
-    dense = nt_dot(left, right)
-    here = where_tile == tile
-    for a in range(3):
-        for b in range(3):
-            part = dense[a * T:(a + 1) * T, b * T:(b + 1) * T]
-            got = jnp.take_along_axis(part, lane, axis=1, mode="promise_in_bounds")
-            acc[3 * a + b] = jnp.where(here, got, acc[3 * a + b])
-
-
 def fold_matrix():
-    row = lax.broadcasted_iota(jnp.int32, (T // 8, T), 0)
-    col = lax.broadcasted_iota(jnp.int32, (T // 8, T), 1)
+    row = lax.broadcasted_iota(jnp.int32, (2 * T // 8, 2 * T), 0)
+    col = lax.broadcasted_iota(jnp.int32, (2 * T // 8, 2 * T), 1)
     return (col // 8 == row).astype(BF16)
 
 
-def own_kernel(high, low, mode_cot, nbr_t, out, weighted, lane_ref, tile_ref, stack, acc):
+def pick(dense, per, local, a, b, at):
+    place = local * 3 + b
+    return dense[place // per, pl.ds(a * T + at, 8), (place % per) * T:(place % per + 1) * T]
+
+
+def pipeline(jobs, weighted, lane_ref, tile_ref, dense, per, terms, with_self, pairs_of):
+    width = per * T
+
+    def multiply(job, out, c):
+        i, rows, first, _, _ = job
+        at = pl.ds(pl.multiple_of(first + c * width, T), width)
+        out[c] = nt_dot(weighted[i], rows[at, :])
+
+    def gather(job, src, step):
+        i, _, _, first_tile, tiles = job
+        found = []
+        for half in range(2):
+            at = pl.multiple_of(step * 16 + half * 8, 8)
+            lane, where_tile = lane_ref[i, pl.ds(at, 8), :], tile_ref[i, pl.ds(at, 8), :]
+            sums = [jnp.zeros((8, T), F32)] * 9
+            for local in range(tiles):
+                here = where_tile == first_tile + local
+                for a in range(3):
+                    for b in range(3):
+                        got = jnp.take_along_axis(pick(src, per, local, a, b, at), lane, axis=1,
+                                                  mode="promise_in_bounds")
+                        sums[3 * a + b] = jnp.where(here, got, sums[3 * a + b])
+            if with_self:
+                mine = lax.broadcasted_iota(jnp.int32, (8, T), 0) + at
+                live = where_tile >= 0
+                for a in range(3):
+                    for b in range(3):
+                        got = jnp.take_along_axis(pick(src, per, i + REACH - first_tile, a, b, at), mine, axis=1,
+                                                  mode="promise_in_bounds")
+                        sums[3 * a + b] = jnp.where(live, sums[3 * a + b] - got, 0.0)
+            found.append(sums)
+        place = pl.ds(pl.multiple_of(i * T + step * 16, 16), 16)
+        for c in range(9):
+            terms[c, place, :] = jnp.concatenate([found[0][c], found[1][c]], axis=0).astype(BF16)
+
+    def chunks(job):
+        return -(-job[4] * 3 // per)
+
+    for c in range(chunks(jobs[0])):
+        multiply(jobs[0], dense[0], c)
+    for k, job in enumerate(jobs):
+        src, other = dense[k % 2], dense[(k + 1) % 2]
+        ahead = chunks(jobs[k + 1]) if k + 1 < len(jobs) else 0
+        pairs = pairs_of(job[4])
+        turns = T // 16 // pairs
+        each = -(-ahead // turns)
+
+        def turn(step, carry, products, k=k, job=job, src=src, other=other, pairs=pairs):
+            for c in range(products):
+                multiply(jobs[k + 1], other, step * products + c)
+            for p in range(pairs):
+                gather(job, src, step * pairs + p)
+            return carry
+
+        full = ahead // each if each else 0
+        left = ahead - full * each
+        if full:
+            lax.fori_loop(0, full, functools.partial(turn, products=each), 0)
+        if left:
+            for c in range(left):
+                multiply(jobs[k + 1], other, full * each + c)
+        if full < turns:
+            lax.fori_loop(full, turns, functools.partial(turn, products=0), 0)
+
+
+def own_kernel(high, low, mode_cot, nbr_t, out, weighted, lane_ref, tile_ref, stack, dense0, dense1, terms):
     row = lax.broadcasted_iota(jnp.int32, (T, T), 0)
     col = lax.broadcasted_iota(jnp.int32, (T, T), 1)
     diagonal = (row % 8) == (col // 16)
@@ -74,68 +138,34 @@
         live = diagonal & (n < ATOMS + 2 * RIM)
         tile_ref[blk] = jnp.where(live, n >> 7, -1)
         lane_ref[blk] = n & (T - 1)
-        src, base = (low, blk * T) if blk < REACH else (high, blk * T - RIM)
-        for a in range(3):
-            s = src[a, base:base + T, :]
-            stack[blk, a * T:(a + 1) * T, :] = s
-            weighted[blk, a * T:(a + 1) * T, :] = (s.astype(F32) * cot).astype(BF16)
+        src = low if blk < REACH else high
+        s = src[blk % REACH * STRIP:(blk % REACH + 1) * STRIP, :]
+        stack[blk * STRIP:(blk + 1) * STRIP, :] = s
+        weighted[blk] = (s.astype(F32) * cot).astype(BF16)
+    stack[BLOCKS * STRIP:, :] = jnp.zeros((STRIP, 256), BF16)
+    jobs = []
+    for i in range(BLOCKS):
+        first, last = max(i - REACH, 0), min(i + REACH, BLOCKS - 1)
+        jobs.append((i, stack, first * STRIP, first + REACH, last - first + 1))
+    pipeline(jobs, weighted, lane_ref, tile_ref, (dense0, dense1), 6, terms, True, lambda tiles: 4)
     fold = fold_matrix()
-
-    def block(i, carry):
-        left = weighted[i]
-        lane, where_tile = lane_ref[i], tile_ref[i]
-        acc[...] = jnp.zeros_like(acc)
-
-        def tile(j, carry):
-            add_tile(left, stack[j], j + REACH, lane, where_tile, acc)
-            return carry
-
-        lax.fori_loop(jnp.maximum(i - REACH, 0), jnp.minimum(i + REACH, BLOCKS - 1) + 1, tile, 0)
-        mine = stack[i]
-        live = where_tile >= 0
-        for a in range(3):
-            for b in range(3):
-                both = left[a * T:(a + 1) * T].astype(F32) * mine[b * T:(b + 1) * T].astype(F32)
-                self_term = jnp.sum(both, axis=1, keepdims=True)
-                term = jnp.where(live, acc[3 * a + b] - self_term, 0.0)
-                folded = jnp.dot(fold, term.astype(BF16), preferred_element_type=F32)
-                out[3 * a + b, pl.ds(pl.multiple_of(i * 16, 16), 16), :] = folded
-        return carry
-
-    lax.fori_loop(0, BLOCKS, block, 0)
+    for h in range(BLOCKS // 2):
+        for c in range(9):
+            out[c, h * 32:(h + 1) * 32, :] = jnp.dot(
+                fold, terms[c, h * 2 * T:(h + 1) * 2 * T, :], preferred_element_type=F32)
 
 
 def halo_kernel(mode_index, below, above, weighted, lane_ref, tile_ref, own,
-                out0, out1, out2, out3, acc, total):
+                out0, out1, out2, out3, dense0, dense1, terms, total):
+    jobs = [(i, below, i * STRIP, i, REACH - i) for i in range(REACH)]
+    jobs += [(i, above, 0, 3 * REACH, i - REACH + 1) for i in range(REACH, BLOCKS)]
+    pipeline(jobs, weighted, lane_ref, tile_ref, (dense0, dense1), 3, terms, False, lambda tiles: 8)
     fold = fold_matrix()
-
-    def block(src, shift, lo, hi, i):
-        left = weighted[i]
-        lane, where_tile = lane_ref[i], tile_ref[i]
-        acc[...] = jnp.zeros_like(acc)
-
-        def tile(t, carry):
-            rows = pl.ds(pl.multiple_of((t - shift) * T, T), T)
-            right = jnp.concatenate([src[b, rows, :] for b in range(3)], axis=0)
-            add_tile(left, right, t, lane, where_tile, acc)
-            return carry
-
-        lax.fori_loop(lo, hi, tile, 0)
-        at = pl.ds(pl.multiple_of(i * 16, 16), 16)
+    for h in range(BLOCKS // 2):
         for c in range(9):
-            folded = jnp.dot(fold, acc[c].astype(BF16), preferred_element_type=F32)
-            total[c, at, :] = own[c, at, :] + folded
-
-    def low_block(i, carry):
-        block(below, 0, i, REACH, i)
-        return carry
-
-    def high_block(i, carry):
-        block(above, 3 * REACH, 3 * REACH, i + 2 * REACH + 1, i)
-        return carry
-
-    lax.fori_loop(0, REACH, low_block, 0)
-    lax.fori_loop(REACH, BLOCKS, high_block, 0)
+            at = slice(h * 32, (h + 1) * 32)
+            total[c, at, :] = own[c, at, :] + jnp.dot(
+                fold, terms[c, h * 2 * T:(h + 1) * 2 * T, :], preferred_element_type=F32)
     m = mode_index[0]
     for k, out in enumerate((out0, out1, out2, out3)):
         q = lax.rem(m + k, 4)
@@ -223,7 +253,7 @@
     eig = jnp.transpose(eigvec, (1, 0, 2))
     m = lax.axis_index("mode").astype(jnp.int32).reshape(1)
     high, low = pl.pallas_call(
-        scale_kernel, out_shape=[shape((3, RIM, 256), BF16)] * 2,
+        scale_kernel, out_shape=[shape((REACH * STRIP, 256), BF16)] * 2,
         in_specs=[VMEM] * 2, out_specs=[VMEM] * 2, compiler_params=PARAMS,
         cost_estimate=cost(1 << 20, 4 << 20), name="scale",
     )(eig, species.reshape(1, ATOMS))
@@ -234,7 +264,8 @@
         out_shape=[shape((9, GROUPS, T)), shape((BLOCKS, 3 * T, 256), BF16),
                    shape((BLOCKS, T, T), jnp.int32), shape((BLOCKS, T, T), jnp.int32)],
         in_specs=[VMEM] * 4, out_specs=[VMEM] * 4,
-        scratch_shapes=[pltpu.VMEM((BLOCKS, 3 * T, 256), BF16), pltpu.VMEM((9, T, T), F32)],
+        scratch_shapes=[pltpu.VMEM(((BLOCKS + 1) * STRIP, 256), BF16)]
+        + [pltpu.VMEM((5, STRIP, 6 * T), F32)] * 2 + [pltpu.VMEM((9, ATOMS, T), BF16)],
         compiler_params=PARAMS, cost_estimate=cost(12_000_000_000, 6 << 20), name="own",
     )(high, low, mode_cot.reshape(1, 256), neighbours.T)
     slots = pair_features.shape[0]
@@ -249,7 +280,8 @@
     parts = pl.pallas_call(
         halo_kernel, out_shape=[shape((9, QUARTER, T), BF16)] * 4,
         in_specs=[SMEM] + [VMEM] * 6, out_specs=[VMEM] * 4,
-        scratch_shapes=[pltpu.VMEM((9, T, T), F32), pltpu.VMEM((9, GROUPS, T), F32)],
+        scratch_shapes=[pltpu.VMEM((REACH, STRIP, 3 * T), F32)] * 2
+        + [pltpu.VMEM((9, ATOMS, T), BF16), pltpu.VMEM((9, GROUPS, T), F32)],
         compiler_params=PARAMS, cost_estimate=cost(5_000_000_000, 6 << 20), name="halo",
     )(m, below, above, weighted, lane, tile, own)
     parts = [parts[0]] + [lax.ppermute(parts[k], "mode", ring("mode", k)) for k in (1, 2, 3)]
@@ -269,9 +301,9 @@
     line = [[g * 8 + k for k in range(8)] for g in range(8)]
     plane = [[k * 8 + g for k in range(8)] for g in range(8)]
     for groups in (line, plane):
-        spread = jnp.broadcast_to(share[None], (8, ROWS, T))
+        spread = jnp.broadcast_to(share.astype(BF16)[None], (8, ROWS, T))
         got = lax.all_to_all(spread, "slab", 0, 0, axis_index_groups=groups, tiled=True)
-        share = jnp.sum(got, axis=0)
+        share = jnp.sum(got.astype(F32), axis=0)
     pieces = [share] + [lax.ppermute(share, "mode", ring("mode", k)) for k in (1, 2, 3)]
     grad_w_in, grad_b_in, grad_w_out = pl.pallas_call(
         finish_kernel, out_shape=[shape((128, 256)), shape((1, 256)), shape((9, 256))],

time: 139 us -> 95.1 us (0.68)
  Pallas kernels: 81.6 us -> 37 us
  blocking collectives: 30.2 us -> 27.5 us
  waiting for transfers between devices: 6.24 us -> 8.66 us
    pallas_call x1, Pallas kernels: 50.3 us -> 19.3 us  [shards(): pl.pallas_call(own_kernel, out_shape=[shape((9, GROUPS, T)), shape((BLOCK...]
    pallas_call x1, Pallas kernels: 19.3 us -> 5.77 us  [shards(): pl.pallas_call(halo_kernel, out_shape=[shape((9, QUARTER, T), BF16)] * 4,...]
    all_to_all x2, blocking collectives: 30.2 us -> 27.5 us  [shards(): lax.all_to_all(spread, 'slab', 0, 0, axis_index_groups=groups, tiled=True)]
    ppermute x1, waiting for transfers between devices: 0.01 us -> 2.42 us  [shards(): below = lax.ppermute(high, 'slab', ring('slab', 1))]
  transfers between devices with their start and end apart: 11 -> 11, of which waited for: 7 -> 8; matrix products, arithmetic and copies ran while one was open for 0% -> 0% of each run, Pallas kernels for 39% -> 24%
where the time goes in v2:
time: 95.1 us; the launch traced here: 94.8 us
  Pallas kernels  37 us (39%)
  blocking collectives  27.5 us (29%)
  starting transfers between devices  18.5 us (19%)
  waiting for transfers between devices  8.66 us (9%)
  local copies, waits for them, and re-layouts  2.33 us (2%)
    all_to_all x2, blocking collectives, shards(): lax.all_to_all(spread, 'slab', 0, 0, axis_index_groups=groups, tiled=True)  27.5 us
    pallas_call x1, Pallas kernels, shards(): pl.pallas_call(own_kernel, out_shape=[shape((9, GROUPS, T)), shape((BLOCK...  19.3 us
    ppermute x1, starting transfers between devices, shards(): above = lax.ppermute(low, 'slab', ring('slab', lax.axis_size('slab') - 1))  8.85 us
    pallas_call x1, Pallas kernels, shards(): pl.pallas_call(backward_kernel, out_shape=[shape((slots, 128), BF16)] + [...  6.22 us
    pallas_call x1, Pallas kernels, shards(): pl.pallas_call(halo_kernel, out_shape=[shape((9, QUARTER, T), BF16)] * 4,...  5.77 us
    pallas_call x1, Pallas kernels, shards(): pl.pallas_call(forward_kernel, out_shape=[shape((slots, 256), BF16)] * 2,...  3.72 us
    ppermute x3, starting transfers between devices, shards(): lax.ppermute(share, 'mode', ring('mode', k))  3.37 us
    ppermute x3, waiting for transfers between devices, shards(): share = share + lax.ppermute(sums[k], 'mode', ring('mode', k))  3.31 us
  transfers between devices with their start and end apart: 11, of which 8 were waited for; matrix products, arithmetic and copies ran while one was open for 0% of the time, Pallas kernels for 24%

profile of v2, /device:TPU:1, one launch (start us, length us, event | category | flops | bytes accessed | tf_op | source)
XLA Modules:
  0.0 94.8 jit_solution(9911399210415694574)
XLA Ops:
  0.6 0.0 copy-start.4
  0.6 0.7 reshape.26.species
  1.3 0.0 copy-start
  1.4 1.5 %copy-done = bf16[1280,3,256]{2,0,1:T(8,128)(2,1)S(1)} copy-done((bf16[1280,3,256]{2,0,1:T(8,128)(2,1)S(1)}, bf16[1280,3,256]{2,0,1:T(8,128)(2,1)}, u32[]{:S(2)}) %copy-start) | copy-done | bytes 1966104
  2.9 0.0 copy-start.2
  2.9 1.2 %scale.1 = (bf16[1920,256]{1,0:T(8,128)(2,1)}, bf16[1920,256]{1,0:T(8,128)(2,1)S(1)}) custom-call(bf16[3,1280,256]{2,1,0:T(8,128)(2,1)S(1)} %bitcast.6, s32[1,1280]{1,0:T(1,128)S(1)} %reshape.26.species), custom_call_target="tpu_custom_call" | custom-call | flops 1048576 | bytes 4194304 | tf_op jit(solution)/shard_map/scale/pallas_call | solution.py:255
  4.1 2.5 %collective-permute-start = (bf16[1920,256]{1,0:T(8,128)(2,1)}, bf16[1920,256]{1,0:T(8,128)(2,1)S(1)}, u32[]{:S(2)}, u32[]{:S(2)}) collective-permute-start(bf16[1920,256]{1,0:T(8,128)(2,1)} %get-tuple-element.24.high), channel_id=1, source_target_pairs={{0,4},{4,8},{8,12},{12,16},{16,20},{20,24},{24,28},{28,32},{32,36}... | collective-permute-start | bytes 2949128 | tf_op jit(solution)/shard_map/ppermute | solution.py:260
  6.6 8.9 %collective-permute-start.1 = (bf16[1920,256]{1,0:T(8,128)(2,1)S(1)}, bf16[1920,256]{1,0:T(8,128)(2,1)S(1)}, u32[]{:S(2)}, u32[]{:S(2)}) collective-permute-start(bf16[1920,256]{1,0:T(8,128)(2,1)S(1)} %get-tuple-element.25.low), channel_id=1, source_target_pairs={{0,252},{4,0},{8,4},{12,8},{16,12},{20,16},{24,20},{28,24},{32,28}... | collective-permute-start | bytes 2949128 | tf_op jit(solution)/shard_map/ppermute | solution.py:261
  15.4 0.0 copy-done.4
  15.4 0.0 copy-done.2
  15.4 19.3 %own.1 = (f32[9,160,128]{2,1,0:T(8,128)S(1)}, bf16[10,384,256]{2,1,0:T(8,128)(2,1)S(1)}, s32[10,128,128]{2,1,0:T(8,128)S(1)}, s32[10,128,128]{2,1,0:T(8,128)S(1)}) custom-call(bf16[1920,256]{1,0:T(8,128)(2,1)} %get-tuple-element.24.high, bf16[1920,256]{1,0:T(8,128)(2,1)S(1)} %get-tuple-element.25.low, f32[1,256]{1,0:T(1,128)S(1)} %bitcast.8, ...), custom_call_target="tpu_custom_call" | custom-call | flops 12000000000 | bytes 6291456 | tf_op jit(solution)/shard_map/own/pallas_call | solution.py:262
  34.7 2.4 %collective-permute-done.below = bf16[1920,256]{1,0:T(8,128)(2,1)S(1)} collective-permute-done((bf16[1920,256]{1,0:T(8,128)(2,1)}, bf16[1920,256]{1,0:T(8,128)(2,1)S(1)}, u32[]{:S(2)}, u32[]{:S(2)}) %collective-permute-start) | collective-permute-done | bytes 983072 | tf_op jit(solution)/shard_map/ppermute | solution.py:260
  37.1 0.0 collective-permute-done.1.above
  37.1 0.0 copy-start.1
  37.1 0.0 copy-start.3
  37.1 0.0 copy-start.5
  37.1 5.8 %halo.1 = (bf16[9,40,128]{2,1,0:T(8,128)(2,1)S(1)}, bf16[9,40,128]{2,1,0:T(8,128)(2,1)S(1)}, bf16[9,40,128]{2,1,0:T(8,128)(2,1)S(1)}, bf16[9,40,128]{2,1,0:T(8,128)(2,1)S(1)}) custom-call(s32[1]{0:T(128)} %bitcast.mode_index, bf16[1920,256]{1,0:T(8,128)(2,1)S(1)} %collective-permute-done.below, bf16[1920,256]{1,0:T(8,128)(2,1)S(1)} %collective-permute-done.1.above, ...), custom_call_target="tpu_custom_call" | custom-call | flops 5000000000 | bytes 6291456 | tf_op jit(solution)/shard_map/halo/pallas_call | solution.py:280
  42.9 1.5 %collective-permute-start.2 = (bf16[9,40,128]{2,1,0:T(8,128)(2,1)S(1)}, bf16[9,40,128]{2,1,0:T(8,128)(2,1)S(1)}, u32[]{:S(2)}, u32[]{:S(2)}) collective-permute-start(bf16[9,40,128]{2,1,0:T(8,128)(2,1)S(1)} %get-tuple-element.31), channel_id=1, source_target_pairs={{0,1},{1,2},{2,3},{3,0},{4,5},{5,6},{6,7},{7,4},{8,9},{9,10},{10,1... | collective-permute-start | bytes 276488 | tf_op jit(solution)/shard_map/ppermute | solution.py:287
  44.4 1.2 %collective-permute-start.3 = (bf16[9,40,128]{2,1,0:T(8,128)(2,1)S(1)}, bf16[9,40,128]{2,1,0:T(8,128)(2,1)S(1)}, u32[]{:S(2)}, u32[]{:S(2)}) collective-permute-start(bf16[9,40,128]{2,1,0:T(8,128)(2,1)S(1)} %get-tuple-element.32), channel_id=1, source_target_pairs={{0,2},{1,3},{2,0},{3,1},{4,6},{5,7},{6,4},{7,5},{8,10},{9,11},{10,... | collective-permute-start | bytes 276488 | tf_op jit(solution)/shard_map/ppermute | solution.py:287
  45.6 0.0 collective-permute-start.4
  45.6 0.0 copy-done.1
  45.6 0.0 copy-done.3
  45.6 0.0 copy-done.5
  45.6 0.0 copy-start.6
  45.6 3.7 %forward.1 = (bf16[5120,256]{1,0:T(8,128)(2,1)S(1)}, bf16[5120,256]{1,0:T(8,128)(2,1)S(1)}) custom-call(bf16[5120,128]{1,0:T(8,128)(2,1)S(1)} %copy-done.1, bf16[128,256]{1,0:T(8,128)(2,1)S(1)} %copy-done.3, f32[1,256]{1,0:T(1,128)S(1)} %bitcast.9), custom_call_target="tpu_custom_call" | custom-call | flops 4000000000 | bytes 7340032 | tf_op jit(solution)/shard_map/forward/pallas_call | solution.py:275
  49.3 0.0 copy-done.6
  49.4 0.0 collective-permute-done.2.p1
  49.4 0.5 collective-permute-done.3.p2
  49.8 0.6 collective-permute-done.4.p3
  50.5 6.2 %backward.1 = (bf16[5120,128]{1,0:T(8,128)(2,1)}, f32[80,128]{1,0:T(8,128)S(1)}, f32[80,128]{1,0:T(8,128)S(1)}, f32[80,128]{1,0:T(8,128)S(1)}, f32[80,128]{1,0:T(8,128)S(1)}) custom-call(s32[1]{0:T(128)} %bitcast.mode_index, bf16[9,40,128]{2,1,0:T(8,128)(2,1)S(1)} %get-tuple-element.30.p0, bf16[9,40,128]{2,1,0:T(8,128)(2,1)S(1)} %collective-permute-done.2.p1, ...), custom_call_target="tpu_custom_call" | custom-call | flops 2000000000 | bytes 9437184 | tf_op jit(solution)/shard_map/backward/pallas_call | solution.py:289
  56.7 0.7 collective-permute-start.5
  57.4 0.3 collective-permute-start.6
  57.7 0.1 collective-permute-start.7
  57.8 0.7 collective-permute-done.5
  58.5 2.2 %collective-permute-done.6 = f32[80,128]{1,0:T(8,128)S(1)} collective-permute-done((f32[80,128]{1,0:T(8,128)S(1)}, f32[80,128]{1,0:T(8,128)S(1)}, u32[]{:S(2)}, u32[]{:S(2)}) %collective-permute-start.6) | collective-permute-done | bytes 40992 | tf_op jit(solution)/shard_map/ppermute | solution.py:300
  60.7 0.4 collective-permute-done.7
  61.2 11.8 %all_to_all.10 = bf16[8,80,128]{2,1,0:T(8,128)(2,1)S(1)} all-to-all(bf16[8,80,128]{2,1,0:T(8,128)(2,1)S(1)} %broadcast_in_dim.4), channel_id=1, replica_groups={{0,4,8,12,16,20,24,28},{32,36,40,44,48,52,56,60},{64,68,72,76,80,84,88,..., dimensions={0} | all-to-all | bytes 327680 | tf_op jit(solution)/shard_map/all_to_all | solution.py:305
  73.0 15.7 %all_to_all.11 = bf16[8,80,128]{2,1,0:T(8,128)(2,1)S(1)} all-to-all(bf16[8,80,128]{2,1,0:T(8,128)(2,1)S(1)} %broadcast_in_dim.5), channel_id=1, replica_groups={{0,32,64,96,128,160,192,224},{4,36,68,100,132,164,196,228},{8,40,72,104..., dimensions={0} | all-to-all | bytes 327680 | tf_op jit(solution)/shard_map/all_to_all | solution.py:305
  88.7 1.9 %collective-permute-start.10 = (f32[80,128]{1,0:T(8,128)S(1)}, f32[80,128]{1,0:T(8,128)S(1)}, u32[]{:S(2)}, u32[]{:S(2)}) collective-permute-start(f32[80,128]{1,0:T(8,128)S(1)} %convert_reduce_fusion.c0), channel_id=1, source_target_pairs={{0,3},{1,0},{2,1},{3,2},{4,7},{5,4},{6,5},{7,6},{8,11},{9,8},{10,9... | collective-permute-start | bytes 122888 | tf_op jit(solution)/shard_map/ppermute | solution.py:307
  90.7 0.0 collective-permute-start.8
  90.7 1.4 %collective-permute-start.9 = (f32[80,128]{1,0:T(8,128)S(1)}, f32[80,128]{1,0:T(8,128)S(1)}, u32[]{:S(2)}, u32[]{:S(2)}) collective-permute-start(f32[80,128]{1,0:T(8,128)S(1)} %convert_reduce_fusion.c0), channel_id=1, source_target_pairs={{0,2},{1,3},{2,0},{3,1},{4,6},{5,7},{6,4},{7,5},{8,10},{9,11},{10,... | collective-permute-start | bytes 122888 | tf_op jit(solution)/shard_map/ppermute | solution.py:307
  92.1 0.1 collective-permute-done.10.c3
  92.2 0.0 collective-permute-done.8.c1
  92.2 1.7 %collective-permute-done.9.c2 = f32[80,128]{1,0:T(8,128)S(1)} collective-permute-done((f32[80,128]{1,0:T(8,128)S(1)}, f32[80,128]{1,0:T(8,128)S(1)}, u32[]{:S(2)}, u32[]{:S(2)}) %collective-permute-start.9) | collective-permute-done | bytes 40992 | tf_op jit(solution)/shard_map/ppermute | solution.py:307
  93.9 0.9 finish.1
  (6 shorter events, 0.1 us)
Async XLA Ops:
  0.6 14.8 %copy-start.4 = (f32[256]{0:T(256)S(1)}, f32[256]{0:T(256)}, u32[]{:S(2)}) copy-start(f32[256]{0:T(256)} %param.10) | copy-start | bytes 3076
  1.3 1.5 %copy-start = (bf16[1280,3,256]{2,0,1:T(8,128)(2,1)S(1)}, bf16[1280,3,256]{2,0,1:T(8,128)(2,1)}, u32[]{:S(2)}) copy-start(bf16[1280,3,256]{2,0,1:T(8,128)(2,1)} %param.8) | copy-start | bytes 5898244
  2.9 12.5 %copy-start.2 = (s32[1280,16]{0,1:T(8,128)S(1)}, s32[1280,16]{0,1:T(8,128)}, u32[]{:S(2)}) copy-start(s32[1280,16]{0,1:T(8,128)} %param.11) | copy-start | bytes 245764
  4.1 33.0 %collective-permute-start = (bf16[1920,256]{1,0:T(8,128)(2,1)}, bf16[1920,256]{1,0:T(8,128)(2,1)S(1)}, u32[]{:S(2)}, u32[]{:S(2)}) collective-permute-start(bf16[1920,256]{1,0:T(8,128)(2,1)} %get-tuple-element.24.high), channel_id=1, source_target_pairs={{0,4},{4,8},{8,12},{12,16},{16,20},{20,24},{24,28},{28,32},{32,36}... | collective-permute-start | bytes 2949128 | tf_op jit(solution)/shard_map/ppermute | solution.py:260
  6.6 30.5 %collective-permute-start.1 = (bf16[1920,256]{1,0:T(8,128)(2,1)S(1)}, bf16[1920,256]{1,0:T(8,128)(2,1)S(1)}, u32[]{:S(2)}, u32[]{:S(2)}) collective-permute-start(bf16[1920,256]{1,0:T(8,128)(2,1)S(1)} %get-tuple-element.25.low), channel_id=1, source_target_pairs={{0,252},{4,0},{8,4},{12,8},{16,12},{20,16},{24,20},{28,24},{32,28}... | collective-permute-start | bytes 2949128 | tf_op jit(solution)/shard_map/ppermute | solution.py:261
  37.1 8.5 %copy-start.1 = (bf16[5120,128]{1,0:T(8,128)(2,1)S(1)}, bf16[5120,128]{1,0:T(8,128)(2,1)}, u32[]{:S(2)}) copy-start(bf16[5120,128]{1,0:T(8,128)(2,1)} %features.3) | copy-start | bytes 3932164
  37.1 8.5 %copy-start.3 = (bf16[128,256]{1,0:T(8,128)(2,1)S(1)}, bf16[128,256]{1,0:T(8,128)(2,1)}, u32[]{:S(2)}) copy-start(bf16[128,256]{1,0:T(8,128)(2,1)} %w_in.3) | copy-start | bytes 196612
  37.1 8.5 %copy-start.5 = (f32[256]{0:T(256)S(1)}, f32[256]{0:T(256)}, u32[]{:S(2)}) copy-start(f32[256]{0:T(256)} %param.14) | copy-start | bytes 3076
  42.9 6.4 %collective-permute-start.2 = (bf16[9,40,128]{2,1,0:T(8,128)(2,1)S(1)}, bf16[9,40,128]{2,1,0:T(8,128)(2,1)S(1)}, u32[]{:S(2)}, u32[]{:S(2)}) collective-permute-start(bf16[9,40,128]{2,1,0:T(8,128)(2,1)S(1)} %get-tuple-element.31), channel_id=1, source_target_pairs={{0,1},{1,2},{2,3},{3,0},{4,5},{5,6},{6,7},{7,4},{8,9},{9,10},{10,1... | collective-permute-start | bytes 276488 | tf_op jit(solution)/shard_map/ppermute | solution.py:287
  44.4 5.4 %collective-permute-start.3 = (bf16[9,40,128]{2,1,0:T(8,128)(2,1)S(1)}, bf16[9,40,128]{2,1,0:T(8,128)(2,1)S(1)}, u32[]{:S(2)}, u32[]{:S(2)}) collective-permute-start(bf16[9,40,128]{2,1,0:T(8,128)(2,1)S(1)} %get-tuple-element.32), channel_id=1, source_target_pairs={{0,2},{1,3},{2,0},{3,1},{4,6},{5,7},{6,4},{7,5},{8,10},{9,11},{10,... | collective-permute-start | bytes 276488 | tf_op jit(solution)/shard_map/ppermute | solution.py:287
  45.6 4.9 %collective-permute-start.4 = (bf16[9,40,128]{2,1,0:T(8,128)(2,1)S(1)}, bf16[9,40,128]{2,1,0:T(8,128)(2,1)S(1)}, u32[]{:S(2)}, u32[]{:S(2)}) collective-permute-start(bf16[9,40,128]{2,1,0:T(8,128)(2,1)S(1)} %get-tuple-element.33), channel_id=1, source_target_pairs={{0,3},{1,0},{2,1},{3,2},{4,7},{5,4},{6,5},{7,6},{8,11},{9,8},{10,9... | collective-permute-start | bytes 276488 | tf_op jit(solution)/shard_map/ppermute | solution.py:287
  45.6 3.7 %copy-start.6 = (bf16[9,256]{1,0:T(8,128)(2,1)S(1)}, bf16[9,256]{1,0:T(8,128)(2,1)}, u32[]{:S(2)}) copy-start(bf16[9,256]{1,0:T(8,128)(2,1)} %param.15) | copy-start | bytes 13828
  56.7 1.8 %collective-permute-start.5 = (f32[80,128]{1,0:T(8,128)S(1)}, f32[80,128]{1,0:T(8,128)S(1)}, u32[]{:S(2)}, u32[]{:S(2)}) collective-permute-start(f32[80,128]{1,0:T(8,128)S(1)} %get-tuple-element.38), channel_id=1, source_target_pairs={{0,1},{1,2},{2,3},{3,0},{4,5},{5,6},{6,7},{7,4},{8,9},{9,10},{10,1... | collective-permute-start | bytes 122888 | tf_op jit(solution)/shard_map/ppermute | solution.py:300
  57.4 3.3 %collective-permute-start.6 = (f32[80,128]{1,0:T(8,128)S(1)}, f32[80,128]{1,0:T(8,128)S(1)}, u32[]{:S(2)}, u32[]{:S(2)}) collective-permute-start(f32[80,128]{1,0:T(8,128)S(1)} %get-tuple-element.39), channel_id=1, source_target_pairs={{0,2},{1,3},{2,0},{3,1},{4,6},{5,7},{6,4},{7,5},{8,10},{9,11},{10,... | collective-permute-start | bytes 122888 | tf_op jit(solution)/shard_map/ppermute | solution.py:300
  57.7 3.4 %collective-permute-start.7 = (f32[80,128]{1,0:T(8,128)S(1)}, f32[80,128]{1,0:T(8,128)S(1)}, u32[]{:S(2)}, u32[]{:S(2)}) collective-permute-start(f32[80,128]{1,0:T(8,128)S(1)} %get-tuple-element.40), channel_id=1, source_target_pairs={{0,3},{1,0},{2,1},{3,2},{4,7},{5,4},{6,5},{7,6},{8,11},{9,8},{10,9... | collective-permute-start | bytes 122888 | tf_op jit(solution)/shard_map/ppermute | solution.py:300
  88.7 3.5 %collective-permute-start.10 = (f32[80,128]{1,0:T(8,128)S(1)}, f32[80,128]{1,0:T(8,128)S(1)}, u32[]{:S(2)}, u32[]{:S(2)}) collective-permute-start(f32[80,128]{1,0:T(8,128)S(1)} %convert_reduce_fusion.c0), channel_id=1, source_target_pairs={{0,3},{1,0},{2,1},{3,2},{4,7},{5,4},{6,5},{7,6},{8,11},{9,8},{10,9... | collective-permute-start | bytes 122888 | tf_op jit(solution)/shard_map/ppermute | solution.py:307
  90.7 1.6 %collective-permute-start.8 = (f32[80,128]{1,0:T(8,128)S(1)}, f32[80,128]{1,0:T(8,128)S(1)}, u32[]{:S(2)}, u32[]{:S(2)}) collective-permute-start(f32[80,128]{1,0:T(8,128)S(1)} %convert_reduce_fusion.c0), channel_id=1, source_target_pairs={{0,1},{1,2},{2,3},{3,0},{4,5},{5,6},{6,7},{7,4},{8,9},{9,10},{10,1... | collective-permute-start | bytes 122888 | tf_op jit(solution)/shard_map/ppermute | solution.py:307
  90.7 3.3 %collective-permute-start.9 = (f32[80,128]{1,0:T(8,128)S(1)}, f32[80,128]{1,0:T(8,128)S(1)}, u32[]{:S(2)}, u32[]{:S(2)}) collective-permute-start(f32[80,128]{1,0:T(8,128)S(1)} %convert_reduce_fusion.c0), channel_id=1, source_target_pairs={{0,2},{1,3},{2,0},{3,1},{4,6},{5,7},{6,4},{7,5},{8,10},{9,11},{10,... | collective-permute-start | bytes 122888 | tf_op jit(solution)/shard_map/ppermute | solution.py:307

commit v3 on v2

--- a/solution.py
+++ b/solution.py
@@ -37,7 +37,7 @@
     def half(base, out):
         for blk in range(REACH):
             rows = slice(base + blk * T, base + (blk + 1) * T)
-            kind = species[:, rows]
+            kind = species[rows].reshape(1, T)
             mass = jnp.full(kind.shape, MASS_TABLE[3], F32)
             for k in range(3):
                 mass = jnp.where(kind == k, MASS_TABLE[k], mass)
@@ -147,7 +147,7 @@
     for i in range(BLOCKS):
         first, last = max(i - REACH, 0), min(i + REACH, BLOCKS - 1)
         jobs.append((i, stack, first * STRIP, first + REACH, last - first + 1))
-    pipeline(jobs, weighted, lane_ref, tile_ref, (dense0, dense1), 6, terms, True, lambda tiles: 4)
+    pipeline(jobs, weighted, lane_ref, tile_ref, (dense0, dense1), 6, terms, True, lambda tiles: 8)
     fold = fold_matrix()
     for h in range(BLOCKS // 2):
         for c in range(9):
@@ -155,7 +155,7 @@
                 fold, terms[c, h * 2 * T:(h + 1) * 2 * T, :], preferred_element_type=F32)
 
 
-def halo_kernel(mode_index, below, above, weighted, lane_ref, tile_ref, own,
+def halo_kernel(mode_index, below, above, weighted, lane_ref, tile_ref, own, _after,
                 out0, out1, out2, out3, dense0, dense1, terms, total):
     jobs = [(i, below, i * STRIP, i, REACH - i) for i in range(REACH)]
     jobs += [(i, above, 0, 3 * REACH, i - REACH + 1) for i in range(REACH, BLOCKS)]
@@ -173,47 +173,49 @@
 
 
 CHUNK = 512
-
-
-def forward_kernel(features, w_in, b_in, hidden, slope):
-    pre = jnp.dot(features[...], w_in[...], preferred_element_type=F32) + b_in[...]
+EXT = 144
+
+
+def forward_kernel(features, w_in, b_in, hidden, slope, turned):
+    x = features[...]
+    pre = jnp.dot(x, w_in[...], preferred_element_type=F32) + b_in[...]
     sig = 1.0 / (1.0 + jnp.exp(-pre))
     hidden[...] = (pre * sig).astype(BF16)
     slope[...] = (sig * (1.0 + pre * (1.0 - sig))).astype(BF16)
-
-
-def backward_kernel(mode_index, p0, p1, p2, p3, features, hidden, slope, w_in, w_out,
-                    grad, g0, g1, g2, g3, cot, sums):
-    step = pl.program_id(0)
-
-    @pl.when(step == 0)
-    def _():
-        whole = sum(p[...].astype(F32) for p in (p0, p1, p2, p3))
-        whole = jnp.concatenate([whole, jnp.zeros((7, QUARTER, T), F32)], axis=0)
-        cot[...] = jnp.swapaxes(whole, 0, 1).astype(BF16)
-        sums[...] = jnp.zeros_like(sums)
-
+    turned[0:128, :] = x.T
+    row = lax.broadcasted_iota(jnp.int32, (EXT - 128, CHUNK), 0)
+    turned[128:EXT, :] = (row == 0).astype(BF16)
+
+
+def gradient_kernel(mode_index, p0, p1, p2, p3, turned, hidden, slope, w_out,
+                    pre_cot, g0, g1, g2, g3, cot, sums):
+    whole = sum(p[...].astype(F32) for p in (p0, p1, p2, p3))
+    whole = jnp.concatenate([whole, jnp.zeros((7, QUARTER, T), F32)], axis=0)
+    cot[...] = jnp.swapaxes(whole, 0, 1).astype(BF16)
+    sums[...] = jnp.zeros_like(sums)
+    w_out16 = jnp.concatenate([w_out[...].astype(F32), jnp.zeros((7, 256), F32)], axis=0).astype(BF16)
     per = CHUNK // T
-    pair_cot = jnp.concatenate([cot[step * per + g] for g in range(per)], axis=1)
-    pre_cot32 = tn_dot(pair_cot, w_out[...]) * slope[...].astype(F32)
-    pre_cot = pre_cot32.astype(BF16)
-    grad[...] = nt_dot(pre_cot, w_in[...]).astype(BF16)
-    part_in = tn_dot(features[...], pre_cot)
-    part_out = jnp.dot(pair_cot, hidden[...], preferred_element_type=F32)
-    part_b = jnp.sum(pre_cot.astype(F32), axis=0, keepdims=True)
-    part_b = jnp.concatenate([part_b, jnp.zeros((7, 256), F32)], axis=0)
+    total_in, total_out = jnp.zeros((EXT, 256), F32), jnp.zeros((16, 256), F32)
+    for step in range(hidden.shape[0] // CHUNK):
+        rows = slice(step * CHUNK, (step + 1) * CHUNK)
+        pair_cot = jnp.concatenate([cot[step * per + g] for g in range(per)], axis=1)
+        part = (tn_dot(pair_cot, w_out16) * slope[rows, :].astype(F32)).astype(BF16)
+        pre_cot[rows, :] = part
+        total_in += jnp.dot(turned[:, rows], part, preferred_element_type=F32)
+        total_out += jnp.dot(pair_cot, hidden[rows, :], preferred_element_type=F32)
     for h in range(2):
         cols = slice(h * T, (h + 1) * T)
-        sums[h * 152:h * 152 + 128, :] += part_in[:, cols]
-        sums[h * 152 + 128:h * 152 + 144, :] += part_out[:, cols]
-        sums[h * 152 + 144:h * 152 + 152, :] += part_b[:, cols]
-
-    @pl.when(step == pl.num_programs(0) - 1)
-    def _():
-        m = mode_index[0]
-        for k, out in enumerate((g0, g1, g2, g3)):
-            q = lax.rem(m + k, 4)
-            out[...] = sums[pl.ds(pl.multiple_of(q * ROWS, 8), ROWS), :]
+        sums[h * 152:h * 152 + 128, :] = total_in[0:128, cols]
+        sums[h * 152 + 128:h * 152 + 144, :] = total_out[:, cols]
+        sums[h * 152 + 144:h * 152 + 152, :] = total_in[128:136, cols]
+    m = mode_index[0]
+    for k, out in enumerate((g0, g1, g2, g3)):
+        q = lax.rem(m + k, 4)
+        out[...] = sums[pl.ds(pl.multiple_of(q * ROWS, 8), ROWS), :]
+
+
+def features_kernel(pre_cot, w_in, grad):
+    grad[...] = nt_dot(pre_cot[...], w_in[...]).astype(BF16)
 
 
 SUM_ROWS = 320
@@ -256,7 +258,7 @@
         scale_kernel, out_shape=[shape((REACH * STRIP, 256), BF16)] * 2,
         in_specs=[VMEM] * 2, out_specs=[VMEM] * 2, compiler_params=PARAMS,
         cost_estimate=cost(1 << 20, 4 << 20), name="scale",
-    )(eig, species.reshape(1, ATOMS))
+    )(eig, species)
     below = lax.ppermute(high, "slab", ring("slab", 1))
     above = lax.ppermute(low, "slab", ring("slab", lax.axis_size("slab") - 1))
     own, weighted, lane, tile = pl.pallas_call(
@@ -272,29 +274,33 @@
     steps = slots // CHUNK
     rows_spec = lambda width: pl.BlockSpec((CHUNK, width), lambda s: (s, 0))
     full = lambda *dims: pl.BlockSpec(dims, lambda s: (0,) * len(dims))
-    hidden, slope = pl.pallas_call(
-        forward_kernel, out_shape=[shape((slots, 256), BF16)] * 2, grid=(steps,),
-        in_specs=[rows_spec(128), full(128, 256), full(1, 256)], out_specs=[rows_spec(256)] * 2,
-        compiler_params=PARAMS, cost_estimate=cost(4_000_000_000, 7 << 20), name="forward",
+    hidden, slope, turned = pl.pallas_call(
+        forward_kernel, out_shape=[shape((slots, 256), BF16)] * 2 + [shape((EXT, slots), BF16)], grid=(steps,),
+        in_specs=[rows_spec(128), full(128, 256), full(1, 256)],
+        out_specs=[rows_spec(256)] * 2 + [pl.BlockSpec((EXT, CHUNK), lambda s: (0, s))],
+        compiler_params=PARAMS, cost_estimate=cost(4_000_000_000, 8 << 20), name="forward",
     )(pair_features, w_in, b_in.reshape(1, 256))
     parts = pl.pallas_call(
         halo_kernel, out_shape=[shape((9, QUARTER, T), BF16)] * 4,
-        in_specs=[SMEM] + [VMEM] * 6, out_specs=[VMEM] * 4,
+        in_specs=[SMEM] + [VMEM] * 6 + [pl.BlockSpec(memory_space=pl.ANY)], out_specs=[VMEM] * 4,
         scratch_shapes=[pltpu.VMEM((REACH, STRIP, 3 * T), F32)] * 2
         + [pltpu.VMEM((9, ATOMS, T), BF16), pltpu.VMEM((9, GROUPS, T), F32)],
         compiler_params=PARAMS, cost_estimate=cost(5_000_000_000, 6 << 20), name="halo",
-    )(m, below, above, weighted, lane, tile, own)
+    )(m, below, above, weighted, lane, tile, own, turned)
     parts = [parts[0]] + [lax.ppermute(parts[k], "mode", ring("mode", k)) for k in (1, 2, 3)]
-    w_out16 = jnp.concatenate([w_out, jnp.zeros((7, 256), BF16)], axis=0)
-    features_grad, *sums = pl.pallas_call(
-        backward_kernel,
-        out_shape=[shape((slots, 128), BF16)] + [shape((ROWS, T))] * 4, grid=(steps,),
-        in_specs=[SMEM] + [full(9, QUARTER, T)] * 4
-        + [rows_spec(128), rows_spec(256), rows_spec(256), full(128, 256), full(16, 256)],
-        out_specs=[rows_spec(128)] + [full(ROWS, T)] * 4,
+    pre_cot, *sums = pl.pallas_call(
+        gradient_kernel,
+        out_shape=[shape((slots, 256), BF16)] + [shape((ROWS, T))] * 4,
+        in_specs=[SMEM] + [VMEM] * 8, out_specs=[VMEM] * 5,
         scratch_shapes=[pltpu.VMEM((QUARTER, 16, T), BF16), pltpu.VMEM((SUM_ROWS, T), F32)],
-        compiler_params=PARAMS, cost_estimate=cost(2_000_000_000, 9 << 20), name="backward",
-    )(m, *parts, pair_features, hidden, slope, w_in, w_out16)
+        compiler_params=PARAMS, cost_estimate=cost(2_000_000_000, 9 << 20), name="gradient",
+    )(m, *parts, turned, hidden, slope, w_out)
+    features_grad = pl.pallas_call(
+        features_kernel, out_shape=shape((slots, 128), BF16), grid=(steps // 2,),
+        in_specs=[pl.BlockSpec((2 * CHUNK, 256), lambda s: (s, 0)), full(128, 256)],
+        out_specs=pl.BlockSpec((2 * CHUNK, 128), lambda s: (s, 0)),
+        compiler_params=PARAMS, cost_estimate=cost(2_000_000_000, 5 << 20), name="features",
+    )(pre_cot, w_in)
     share = sums[0]
     for k in (1, 2, 3):
         share = share + lax.ppermute(sums[k], "mode", ring("mode", k))

time: 95.1 us -> 92.4 us (0.972)
  Pallas kernels: 37 us -> 35.2 us
  blocking collectives: 27.5 us -> 26.2 us
  starting transfers between devices: 18.5 us -> 19.6 us
    ppermute x3, waiting for transfers between devices: 1.11 us -> 4.89 us  [shards(): lax.ppermute(parts[k], 'mode', ring('mode', k))]
    ppermute x1, waiting for transfers between devices: 2.42 us -> 0.01 us  [shards(): below = lax.ppermute(high, 'slab', ring('slab', 1))]
    ppermute x3, waiting for transfers between devices: 1.82 us -> 0.01 us  [shards(): lax.ppermute(share, 'mode', ring('mode', k))]
    all_to_all x2, blocking collectives: 27.5 us -> 26.2 us  [shards(): lax.all_to_all(spread, 'slab', 0, 0, axis_index_groups=groups, tiled=True)]
    ppermute x3, starting transfers between devices: 3.37 us -> 4.68 us  [shards(): lax.ppermute(share, 'mode', ring('mode', k))]
    pallas_call x1, Pallas kernels: 19.3 us -> 18 us  [shards(): pl.pallas_call(own_kernel, out_shape=[shape((9, GROUPS, T)), shape((BLOCK...]
    pallas_call x2 -> x3, Pallas kernels: 9.94 us -> 9.08 us  [the longest x1 4 us: shards(): pl.pallas_call(forward_kernel, out_shape=[shape((slots, 256), BF16)] * 2...]
    unnamed x14 -> x16, local copies, waits for them, and re-layouts: 1.57 us -> 2.27 us
  transfers between devices with their start and end apart: 11 -> 11, of which waited for: 8 -> 6; matrix products, arithmetic and copies ran while one was open for 0% -> 0% of each run, Pallas kernels for 24% -> 27%
where the time goes in v3:
time: 92.4 us; the launch traced here: 92.1 us
  Pallas kernels  35.2 us (38%)
  blocking collectives  26.2 us (28%)
  starting transfers between devices  19.6 us (21%)
  waiting for transfers between devices  8.05 us (9%)
  local copies, waits for them, and re-layouts  2.31 us (2%)
    all_to_all x2, blocking collectives, shards(): lax.all_to_all(spread, 'slab', 0, 0, axis_index_groups=groups, tiled=True)  26.2 us
    pallas_call x1, Pallas kernels, shards(): pl.pallas_call(own_kernel, out_shape=[shape((9, GROUPS, T)), shape((BLOCK...  18 us
    ppermute x1, starting transfers between devices, shards(): above = lax.ppermute(low, 'slab', ring('slab', lax.axis_size('slab') - 1))  8.85 us
    pallas_call x1, Pallas kernels, shards(): pl.pallas_call(halo_kernel, out_shape=[shape((9, QUARTER, T), BF16)] * 4,...  5.72 us
    ppermute x3, waiting for transfers between devices, shards(): lax.ppermute(parts[k], 'mode', ring('mode', k))  4.89 us
    ppermute x3, starting transfers between devices, shards(): lax.ppermute(share, 'mode', ring('mode', k))  4.68 us
    pallas_call x1, Pallas kernels, shards(): pl.pallas_call(forward_kernel, out_shape=[shape((slots, 256), BF16)] * 2...  4 us
    ppermute x3, waiting for transfers between devices, shards(): share = share + lax.ppermute(sums[k], 'mode', ring('mode', k))  3.13 us
  transfers between devices with their start and end apart: 11, of which 6 were waited for; matrix products, arithmetic and copies ran while one was open for 0% of the time, Pallas kernels for 27%

profile of v3, /device:TPU:1, one launch (start us, length us, event | category | flops | bytes accessed | tf_op | source)
XLA Modules:
  0.0 92.1 jit_solution(16716856108805770232)
XLA Ops:
  0.6 0.0 copy-start.6
  0.6 0.0 copy-start
  0.7 1.5 %copy-done = bf16[1280,3,256]{2,0,1:T(8,128)(2,1)S(1)} copy-done((bf16[1280,3,256]{2,0,1:T(8,128)(2,1)S(1)}, bf16[1280,3,256]{2,0,1:T(8,128)(2,1)}, u32[]{:S(2)}) %copy-start) | copy-done | bytes 1966104
  2.2 0.0 copy-start.1
  2.2 0.7 copy-done.1
  2.9 0.0 copy-start.2
  2.9 0.0 copy-start.4
  2.9 1.6 %scale.1 = (bf16[1920,256]{1,0:T(8,128)(2,1)}, bf16[1920,256]{1,0:T(8,128)(2,1)}) custom-call(bf16[3,1280,256]{2,1,0:T(8,128)(2,1)S(1)} %bitcast.6, s32[1280]{0:T(1024)S(1)} %copy-done.1), custom_call_target="tpu_custom_call" | custom-call | flops 1048576 | bytes 4194304 | tf_op jit(solution)/shard_map/scale/pallas_call | solution.py:257
  4.5 2.5 %collective-permute-start = (bf16[1920,256]{1,0:T(8,128)(2,1)}, bf16[1920,256]{1,0:T(8,128)(2,1)S(1)}, u32[]{:S(2)}, u32[]{:S(2)}) collective-permute-start(bf16[1920,256]{1,0:T(8,128)(2,1)} %get-tuple-element.25.high), channel_id=1, source_target_pairs={{0,4},{4,8},{8,12},{12,16},{16,20},{20,24},{24,28},{28,32},{32,36}... | collective-permute-start | bytes 2949128 | tf_op jit(solution)/shard_map/ppermute | solution.py:262
  6.9 8.9 %collective-permute-start.1 = (bf16[1920,256]{1,0:T(8,128)(2,1)}, bf16[1920,256]{1,0:T(8,128)(2,1)S(1)}, u32[]{:S(2)}, u32[]{:S(2)}) collective-permute-start(bf16[1920,256]{1,0:T(8,128)(2,1)} %get-tuple-element.26.low), channel_id=1, source_target_pairs={{0,252},{4,0},{8,4},{12,8},{16,12},{20,16},{24,20},{28,24},{32,28}... | collective-permute-start | bytes 2949128 | tf_op jit(solution)/shard_map/ppermute | solution.py:263
  15.8 0.0 copy-done.6
  15.8 0.0 copy-done.2
  15.8 0.0 copy-done.4
  15.8 0.0 copy-start.3
  15.8 0.0 copy-start.7
  15.8 4.0 %forward.1 = (bf16[5120,256]{1,0:T(8,128)(2,1)S(1)}, bf16[5120,256]{1,0:T(8,128)(2,1)S(1)}, bf16[144,5120]{1,0:T(8,128)(2,1)S(1)}) custom-call(bf16[5120,128]{1,0:T(8,128)(2,1)S(1)} %copy-done.2, bf16[128,256]{1,0:T(8,128)(2,1)S(1)} %copy-done.4, f32[1,256]{1,0:T(1,128)S(1)} %bitcast.8), custom_call_target="tpu_custom_call" | custom-call | flops 4000000000 | bytes 8388608 | tf_op jit(solution)/shard_map/forward/pallas_call | solution.py:277
  19.8 0.0 copy-done.3
  19.8 0.0 copy-done.7
  19.8 18.0 %own.1 = (f32[9,160,128]{2,1,0:T(8,128)S(1)}, bf16[10,384,256]{2,1,0:T(8,128)(2,1)S(1)}, s32[10,128,128]{2,1,0:T(8,128)S(1)}, s32[10,128,128]{2,1,0:T(8,128)S(1)}) custom-call(bf16[1920,256]{1,0:T(8,128)(2,1)} %get-tuple-element.25.high, bf16[1920,256]{1,0:T(8,128)(2,1)} %get-tuple-element.26.low, f32[1,256]{1,0:T(1,128)S(1)} %bitcast.9, s32[16,1280]{1,0:T(8,128)S(1)} %bitcast.7), custom_call_target="tpu_custom_call" | custom-call | flops 12000000000 | bytes 6291456 | tf_op jit(solution)/shard_map/own/pallas_call | solution.py:264
  37.8 0.0 collective-permute-done.below
  37.8 0.0 collective-permute-done.1.above
  37.8 0.0 copy-start.5
  37.8 5.7 %halo.1 = (bf16[9,40,128]{2,1,0:T(8,128)(2,1)S(1)}, bf16[9,40,128]{2,1,0:T(8,128)(2,1)S(1)}, bf16[9,40,128]{2,1,0:T(8,128)(2,1)S(1)}, bf16[9,40,128]{2,1,0:T(8,128)(2,1)S(1)}) custom-call(s32[1]{0:T(128)} %bitcast.mode_index, bf16[1920,256]{1,0:T(8,128)(2,1)S(1)} %collective-permute-done.below, bf16[1920,256]{1,0:T(8,128)(2,1)S(1)} %collective-permute-done.1.above, ...), custom_call_target="tpu_custom_call" | custom-call | flops 5000000000 | bytes 6291456 | tf_op jit(solution)/shard_map/halo/pallas_call | solution.py:283
  43.6 1.2 %collective-permute-start.2 = (bf16[9,40,128]{2,1,0:T(8,128)(2,1)S(1)}, bf16[9,40,128]{2,1,0:T(8,128)(2,1)S(1)}, u32[]{:S(2)}, u32[]{:S(2)}) collective-permute-start(bf16[9,40,128]{2,1,0:T(8,128)(2,1)S(1)} %get-tuple-element.33), channel_id=1, source_target_pairs={{0,1},{1,2},{2,3},{3,0},{4,5},{5,6},{6,7},{7,4},{8,9},{9,10},{10,1... | collective-permute-start | bytes 276488 | tf_op jit(solution)/shard_map/ppermute | solution.py:290
  44.8 1.2 %collective-permute-start.3 = (bf16[9,40,128]{2,1,0:T(8,128)(2,1)S(1)}, bf16[9,40,128]{2,1,0:T(8,128)(2,1)S(1)}, u32[]{:S(2)}, u32[]{:S(2)}) collective-permute-start(bf16[9,40,128]{2,1,0:T(8,128)(2,1)S(1)} %get-tuple-element.34), channel_id=1, source_target_pairs={{0,2},{1,3},{2,0},{3,1},{4,6},{5,7},{6,4},{7,5},{8,10},{9,11},{10,... | collective-permute-start | bytes 276488 | tf_op jit(solution)/shard_map/ppermute | solution.py:290
  45.9 0.0 collective-permute-start.4
  46.0 0.7 collective-permute-done.2.p1
  46.6 3.6 %collective-permute-done.3.p2 = bf16[9,40,128]{2,1,0:T(8,128)(2,1)S(1)} collective-permute-done((bf16[9,40,128]{2,1,0:T(8,128)(2,1)S(1)}, bf16[9,40,128]{2,1,0:T(8,128)(2,1)S(1)}, u32[]{:S(2)}, u32[]{:S(2)}) %collective-permute-start.3) | collective-permute-done | bytes 92192 | tf_op jit(solution)/shard_map/ppermute | solution.py:290
  50.2 0.6 collective-permute-done.4.p3
  50.8 0.0 copy-done.5
  50.8 2.1 %gradient.1 = (bf16[5120,256]{1,0:T(8,128)(2,1)S(1)}, f32[80,128]{1,0:T(8,128)S(1)}, f32[80,128]{1,0:T(8,128)S(1)}, f32[80,128]{1,0:T(8,128)S(1)}, f32[80,128]{1,0:T(8,128)S(1)}) custom-call(s32[1]{0:T(128)} %bitcast.mode_index, bf16[9,40,128]{2,1,0:T(8,128)(2,1)S(1)} %get-tuple-element.32.p0, bf16[9,40,128]{2,1,0:T(8,128)(2,1)S(1)} %collective-permute-done.2.p1, ...), custom_call_target="tpu_custom_call" | custom-call | flops 2000000000 | bytes 9437184 | tf_op jit(solution)/shard_map/gradient/pallas_call | solution.py:291
  52.9 0.1 collective-permute-start.5
  53.0 0.7 collective-permute-start.6
  53.7 0.4 collective-permute-start.7
  54.1 0.1 collective-permute-done.5
  54.2 1.7 %collective-permute-done.6 = f32[80,128]{1,0:T(8,128)S(1)} collective-permute-done((f32[80,128]{1,0:T(8,128)S(1)}, f32[80,128]{1,0:T(8,128)S(1)}, u32[]{:S(2)}, u32[]{:S(2)}) %collective-permute-start.6) | collective-permute-done | bytes 40992 | tf_op jit(solution)/shard_map/ppermute | solution.py:306
  56.0 1.3 %collective-permute-done.7 = f32[80,128]{1,0:T(8,128)S(1)} collective-permute-done((f32[80,128]{1,0:T(8,128)S(1)}, f32[80,128]{1,0:T(8,128)S(1)}, u32[]{:S(2)}, u32[]{:S(2)}) %collective-permute-start.7) | collective-permute-done | bytes 40992 | tf_op jit(solution)/shard_map/ppermute | solution.py:306
  57.3 11.8 %all_to_all.10 = bf16[8,80,128]{2,1,0:T(8,128)(2,1)S(1)} all-to-all(bf16[8,80,128]{2,1,0:T(8,128)(2,1)S(1)} %broadcast_in_dim.4), channel_id=1, replica_groups={{0,4,8,12,16,20,24,28},{32,36,40,44,48,52,56,60},{64,68,72,76,80,84,88,..., dimensions={0} | all-to-all | bytes 327680 | tf_op jit(solution)/shard_map/all_to_all | solution.py:311
  69.2 14.4 %all_to_all.11 = bf16[8,80,128]{2,1,0:T(8,128)(2,1)S(1)} all-to-all(bf16[8,80,128]{2,1,0:T(8,128)(2,1)S(1)} %broadcast_in_dim.5), channel_id=1, replica_groups={{0,32,64,96,128,160,192,224},{4,36,68,100,132,164,196,228},{8,40,72,104..., dimensions={0} | all-to-all | bytes 327680 | tf_op jit(solution)/shard_map/all_to_all | solution.py:311
  83.6 2.9 %collective-permute-start.10 = (f32[80,128]{1,0:T(8,128)S(1)}, f32[80,128]{1,0:T(8,128)S(1)}, u32[]{:S(2)}, u32[]{:S(2)}) collective-permute-start(f32[80,128]{1,0:T(8,128)S(1)} %convert_reduce_fusion.c0), channel_id=1, source_target_pairs={{0,3},{1,0},{2,1},{3,2},{4,7},{5,4},{6,5},{7,6},{8,11},{9,8},{10,9... | collective-permute-start | bytes 122888 | tf_op jit(solution)/shard_map/ppermute | solution.py:313
  86.5 0.1 collective-permute-start.9
  86.7 1.6 %collective-permute-start.8 = (f32[80,128]{1,0:T(8,128)S(1)}, f32[80,128]{1,0:T(8,128)S(1)}, u32[]{:S(2)}, u32[]{:S(2)}) collective-permute-start(f32[80,128]{1,0:T(8,128)S(1)} %convert_reduce_fusion.c0), channel_id=1, source_target_pairs={{0,1},{1,2},{2,3},{3,0},{4,5},{5,6},{6,7},{7,4},{8,9},{9,10},{10,1... | collective-permute-start | bytes 122888 | tf_op jit(solution)/shard_map/ppermute | solution.py:313
  88.3 3.0 %features.3 = bf16[5120,128]{1,0:T(8,128)(2,1)} custom-call(bf16[5120,256]{1,0:T(8,128)(2,1)S(1)} %get-tuple-element.38.pre_cot, bf16[128,256]{1,0:T(8,128)(2,1)S(1)} %copy-done.4), custom_call_target="tpu_custom_call" | custom-call | flops 2000000000 | bytes 5242880 | tf_op jit(solution)/shard_map/features/pallas_call | solution.py:298
  91.3 0.0 collective-permute-done.10.c3
  91.3 0.0 collective-permute-done.9.c2
  91.3 0.0 collective-permute-done.8.c1
  91.3 0.9 finish.1
  (5 shorter events, 0.1 us)
Async XLA Ops:
  0.6 15.1 %copy-start.6 = (f32[256]{0:T(256)S(1)}, f32[256]{0:T(256)}, u32[]{:S(2)}) copy-start(f32[256]{0:T(256)} %param.14) | copy-start | bytes 3076
  0.6 1.6 %copy-start = (bf16[1280,3,256]{2,0,1:T(8,128)(2,1)S(1)}, bf16[1280,3,256]{2,0,1:T(8,128)(2,1)}, u32[]{:S(2)}) copy-start(bf16[1280,3,256]{2,0,1:T(8,128)(2,1)} %param.8) | copy-start | bytes 5898244
  2.2 0.7 copy-start.1
  2.9 12.9 %copy-start.2 = (bf16[5120,128]{1,0:T(8,128)(2,1)S(1)}, bf16[5120,128]{1,0:T(8,128)(2,1)}, u32[]{:S(2)}) copy-start(bf16[5120,128]{1,0:T(8,128)(2,1)} %features.2) | copy-start | bytes 3932164
  2.9 12.9 %copy-start.4 = (bf16[128,256]{1,0:T(8,128)(2,1)S(1)}, bf16[128,256]{1,0:T(8,128)(2,1)}, u32[]{:S(2)}) copy-start(bf16[128,256]{1,0:T(8,128)(2,1)} %w_in.3) | copy-start | bytes 196612
  4.5 33.4 %collective-permute-start = (bf16[1920,256]{1,0:T(8,128)(2,1)}, bf16[1920,256]{1,0:T(8,128)(2,1)S(1)}, u32[]{:S(2)}, u32[]{:S(2)}) collective-permute-start(bf16[1920,256]{1,0:T(8,128)(2,1)} %get-tuple-element.25.high), channel_id=1, source_target_pairs={{0,4},{4,8},{8,12},{12,16},{16,20},{20,24},{24,28},{28,32},{32,36}... | collective-permute-start | bytes 2949128 | tf_op jit(solution)/shard_map/ppermute | solution.py:262
  6.9 30.9 %collective-permute-start.1 = (bf16[1920,256]{1,0:T(8,128)(2,1)}, bf16[1920,256]{1,0:T(8,128)(2,1)S(1)}, u32[]{:S(2)}, u32[]{:S(2)}) collective-permute-start(bf16[1920,256]{1,0:T(8,128)(2,1)} %get-tuple-element.26.low), channel_id=1, source_target_pairs={{0,252},{4,0},{8,4},{12,8},{16,12},{20,16},{24,20},{28,24},{32,28}... | collective-permute-start | bytes 2949128 | tf_op jit(solution)/shard_map/ppermute | solution.py:263
  15.8 4.0 %copy-start.3 = (s32[1280,16]{0,1:T(8,128)S(1)}, s32[1280,16]{0,1:T(8,128)}, u32[]{:S(2)}) copy-start(s32[1280,16]{0,1:T(8,128)} %param.11) | copy-start | bytes 245764
  15.8 4.0 %copy-start.7 = (f32[256]{0:T(256)S(1)}, f32[256]{0:T(256)}, u32[]{:S(2)}) copy-start(f32[256]{0:T(256)} %param.10) | copy-start | bytes 3076
  37.8 13.0 %copy-start.5 = (bf16[9,256]{1,0:T(8,128)(2,1)S(1)}, bf16[9,256]{1,0:T(8,128)(2,1)}, u32[]{:S(2)}) copy-start(bf16[9,256]{1,0:T(8,128)(2,1)} %w_out.1) | copy-start | bytes 13828
  43.6 3.1 %collective-permute-start.2 = (bf16[9,40,128]{2,1,0:T(8,128)(2,1)S(1)}, bf16[9,40,128]{2,1,0:T(8,128)(2,1)S(1)}, u32[]{:S(2)}, u32[]{:S(2)}) collective-permute-start(bf16[9,40,128]{2,1,0:T(8,128)(2,1)S(1)} %get-tuple-element.33), channel_id=1, source_target_pairs={{0,1},{1,2},{2,3},{3,0},{4,5},{5,6},{6,7},{7,4},{8,9},{9,10},{10,1... | collective-permute-start | bytes 276488 | tf_op jit(solution)/shard_map/ppermute | solution.py:290
  44.8 5.4 %collective-permute-start.3 = (bf16[9,40,128]{2,1,0:T(8,128)(2,1)S(1)}, bf16[9,40,128]{2,1,0:T(8,128)(2,1)S(1)}, u32[]{:S(2)}, u32[]{:S(2)}) collective-permute-start(bf16[9,40,128]{2,1,0:T(8,128)(2,1)S(1)} %get-tuple-element.34), channel_id=1, source_target_pairs={{0,2},{1,3},{2,0},{3,1},{4,6},{5,7},{6,4},{7,5},{8,10},{9,11},{10,... | collective-permute-start | bytes 276488 | tf_op jit(solution)/shard_map/ppermute | solution.py:290
  45.9 4.9 %collective-permute-start.4 = (bf16[9,40,128]{2,1,0:T(8,128)(2,1)S(1)}, bf16[9,40,128]{2,1,0:T(8,128)(2,1)S(1)}, u32[]{:S(2)}, u32[]{:S(2)}) collective-permute-start(bf16[9,40,128]{2,1,0:T(8,128)(2,1)S(1)} %get-tuple-element.35), channel_id=1, source_target_pairs={{0,3},{1,0},{2,1},{3,2},{4,7},{5,4},{6,5},{7,6},{8,11},{9,8},{10,9... | collective-permute-start | bytes 276488 | tf_op jit(solution)/shard_map/ppermute | solution.py:290
  52.9 1.3 %collective-permute-start.5 = (f32[80,128]{1,0:T(8,128)S(1)}, f32[80,128]{1,0:T(8,128)S(1)}, u32[]{:S(2)}, u32[]{:S(2)}) collective-permute-start(f32[80,128]{1,0:T(8,128)S(1)} %get-tuple-element.40), channel_id=1, source_target_pairs={{0,1},{1,2},{2,3},{3,0},{4,5},{5,6},{6,7},{7,4},{8,9},{9,10},{10,1... | collective-permute-start | bytes 122888 | tf_op jit(solution)/shard_map/ppermute | solution.py:306
  53.0 2.9 %collective-permute-start.6 = (f32[80,128]{1,0:T(8,128)S(1)}, f32[80,128]{1,0:T(8,128)S(1)}, u32[]{:S(2)}, u32[]{:S(2)}) collective-permute-start(f32[80,128]{1,0:T(8,128)S(1)} %get-tuple-element.41), channel_id=1, source_target_pairs={{0,2},{1,3},{2,0},{3,1},{4,6},{5,7},{6,4},{7,5},{8,10},{9,11},{10,... | collective-permute-start | bytes 122888 | tf_op jit(solution)/shard_map/ppermute | solution.py:306
  53.7 3.6 %collective-permute-start.7 = (f32[80,128]{1,0:T(8,128)S(1)}, f32[80,128]{1,0:T(8,128)S(1)}, u32[]{:S(2)}, u32[]{:S(2)}) collective-permute-start(f32[80,128]{1,0:T(8,128)S(1)} %get-tuple-element.42), channel_id=1, source_target_pairs={{0,3},{1,0},{2,1},{3,2},{4,7},{5,4},{6,5},{7,6},{8,11},{9,8},{10,9... | collective-permute-start | bytes 122888 | tf_op jit(solution)/shard_map/ppermute | solution.py:306
  83.6 7.7 %collective-permute-start.10 = (f32[80,128]{1,0:T(8,128)S(1)}, f32[80,128]{1,0:T(8,128)S(1)}, u32[]{:S(2)}, u32[]{:S(2)}) collective-permute-start(f32[80,128]{1,0:T(8,128)S(1)} %convert_reduce_fusion.c0), channel_id=1, source_target_pairs={{0,3},{1,0},{2,1},{3,2},{4,7},{5,4},{6,5},{7,6},{8,11},{9,8},{10,9... | collective-permute-start | bytes 122888 | tf_op jit(solution)/shard_map/ppermute | solution.py:313
  86.5 4.7 %collective-permute-start.9 = (f32[80,128]{1,0:T(8,128)S(1)}, f32[80,128]{1,0:T(8,128)S(1)}, u32[]{:S(2)}, u32[]{:S(2)}) collective-permute-start(f32[80,128]{1,0:T(8,128)S(1)} %convert_reduce_fusion.c0), channel_id=1, source_target_pairs={{0,2},{1,3},{2,0},{3,1},{4,6},{5,7},{6,4},{7,5},{8,10},{9,11},{10,... | collective-permute-start | bytes 122888 | tf_op jit(solution)/shard_map/ppermute | solution.py:313
  86.7 4.6 %collective-permute-start.8 = (f32[80,128]{1,0:T(8,128)S(1)}, f32[80,128]{1,0:T(8,128)S(1)}, u32[]{:S(2)}, u32[]{:S(2)}) collective-permute-start(f32[80,128]{1,0:T(8,128)S(1)} %convert_reduce_fusion.c0), channel_id=1, source_target_pairs={{0,1},{1,2},{2,3},{3,0},{4,5},{5,6},{6,7},{7,4},{8,9},{9,10},{10,1... | collective-permute-start | bytes 122888 | tf_op jit(solution)/shard_map/ppermute | solution.py:313

commit v4 on v3

v4 whole, which is shorter than its diff:
```python
import functools

import jax
import jax.numpy as jnp
from jax import lax
from jax.experimental import pallas as pl
from jax.experimental.pallas import tpu as pltpu
from jax.sharding import PartitionSpec as P

MASS_TABLE = (1.35, 2.94, 2.79, 2.95)
CLIP_NORM = 100.0
T = 128
ATOMS = 1280
RIM = 640
BLOCKS = ATOMS // T
REACH = RIM // T
GROUPS = ATOMS // 8
QUARTER = GROUPS // 4
F32, BF16 = jnp.float32, jnp.bfloat16
VMEM = pl.BlockSpec(memory_space=pltpu.VMEM)
SMEM = pl.BlockSpec(memory_space=pltpu.SMEM)
PARAMS = pltpu.CompilerParams(vmem_limit_bytes=40 << 20)


def nt_dot(x, y):
    return lax.dot_general(x, y, (((1,), (1,)), ((), ())), preferred_element_type=F32)


def tn_dot(x, y):
    return lax.dot_general(x, y, (((0,), (0,)), ((), ())), preferred_element_type=F32)


STRIP = 3 * T


NEAR = 3


def scale_kernel(eig, species, high_near, high_far, low_near, low_far):
    order = [blk for t in range(REACH) for blk in (BLOCKS - 1 - t, t)]
    for blk in order:
        rows = slice(blk * T, (blk + 1) * T)
        kind = species[rows].reshape(1, T)
        mass = jnp.full(kind.shape, MASS_TABLE[3], F32)
        for k in range(3):
            mass = jnp.where(kind == k, MASS_TABLE[k], mass)
        inv = jnp.broadcast_to(lax.rsqrt(mass), (T, T)).T
        inv = jnp.concatenate([inv, inv], axis=1)
        out, tile = place_of(blk, high_near, high_far, low_near, low_far)
        for a in range(3):
            at = tile * STRIP + a * T
            out[at:at + T, :] = (eig[a, rows, :].astype(F32) * inv).astype(BF16)


def place_of(blk, high_near, high_far, low_near, low_far):
    if blk < NEAR:
        return low_near, blk
    if blk < REACH:
        return low_far, blk - NEAR
    if blk < BLOCKS - NEAR:
        return high_far, blk - REACH
    return high_near, blk - (BLOCKS - NEAR)


def fold_matrix():
    row = lax.broadcasted_iota(jnp.int32, (2 * T // 8, 2 * T), 0)
    col = lax.broadcasted_iota(jnp.int32, (2 * T // 8, 2 * T), 1)
    return (col // 8 == row).astype(BF16)


def pick(dense, local, a, b, at):
    place = (local * 3 + b) * T
    return dense[a * T + at:a * T + at + 16, place:place + T]


def lane_gather(values, lane):
    numbers = lax.GatherDimensionNumbers(
        offset_dims=(), collapsed_slice_dims=(1,), start_index_map=(1,),
        operand_batching_dims=(0,), start_indices_batching_dims=(0,))
    return lax.gather(values, lane[..., None], numbers, slice_sizes=(1, 1),
                      mode=lax.GatherScatterMode.PROMISE_IN_BOUNDS)


def pipeline(jobs, weighted, lane_ref, tile_ref, dense, terms, with_self):
    def multiply(job, out):
        i, rows, first, _, tiles = job
        left = weighted[i]
        for start in range(0, tiles * STRIP, 2 * STRIP):
            stop = min(start + 2 * STRIP, tiles * STRIP)
            out[:, start:stop] = nt_dot(left, rows[first + start:first + stop, :]).astype(BF16)

    def gather(job, src, at):
        i, _, _, first_tile, tiles = job
        lane, where_tile = lane_ref[i, at:at + 16, :], tile_ref[i, at:at + 16, :]
        sums = [jnp.zeros((16, T), BF16)] * 9
        for local in range(tiles):
            here = where_tile == jnp.int16(first_tile + local)
            for a in range(3):
                for b in range(3):
                    got = lane_gather(pick(src, local, a, b, at), lane)
                    sums[3 * a + b] = jnp.where(here, got, sums[3 * a + b])
        if with_self:
            mine = (lax.broadcasted_iota(jnp.int32, (16, T), 0) + at).astype(jnp.int16)
            live = where_tile.astype(jnp.int32) >= 0
            for a in range(3):
                for b in range(3):
                    got = lane_gather(pick(src, i + REACH - first_tile, a, b, at), mine)
                    term = sums[3 * a + b].astype(F32) - got.astype(F32)
                    sums[3 * a + b] = jnp.where(live, term, 0.0).astype(BF16)
        for c in range(9):
            terms[c, i * T + at:i * T + at + 16, :] = sums[c]

    multiply(jobs[0], dense[0])
    for k, job in enumerate(jobs):

        def turn(step, carry, k=k, job=job):
            if k + 1 < len(jobs):
                multiply(jobs[k + 1], dense[(k + 1) % 2])
            for at in range(0, T, 16):
                gather(job, dense[k % 2], at)
            return carry

        turn(0, 0)


def own_kernel(high_near, high_far, low_near, low_far, mode_cot, nbr_t, out, weighted, lane_ref, tile_ref, stack, dense0, dense1, terms):
    row = lax.broadcasted_iota(jnp.int32, (T, T), 0)
    col = lax.broadcasted_iota(jnp.int32, (T, T), 1)
    diagonal = (row % 8) == (col // 16)
    cot = mode_cot[...]
    for blk in range(BLOCKS):
        n = nbr_t[:, blk * T:(blk + 1) * T].astype(F32)
        n = jnp.concatenate([n] * 8, axis=0).T.astype(jnp.int32)
        live = diagonal & (n < ATOMS + 2 * RIM)
        tile_ref[blk] = jnp.where(live, n >> 7, -1).astype(jnp.int16)
        lane_ref[blk] = (n & (T - 1)).astype(jnp.int16)
        src, tile = place_of(blk, high_near, high_far, low_near, low_far)
        s = src[tile * STRIP:(tile + 1) * STRIP, :]
        stack[blk * STRIP:(blk + 1) * STRIP, :] = s
        weighted[blk] = (s.astype(F32) * cot).astype(BF16)
    jobs = []
    for i in range(BLOCKS):
        first, last = max(i - REACH, 0), min(i + REACH, BLOCKS - 1)
        jobs.append((i, stack, first * STRIP, first + REACH, last - first + 1))
    pipeline(jobs, weighted, lane_ref, tile_ref, (dense0, dense1), terms, True)
    fold = fold_matrix()
    for h in range(BLOCKS // 2):
        for c in range(9):
            out[c, h * 32:(h + 1) * 32, :] = jnp.dot(
                fold, terms[c, h * 2 * T:(h + 1) * 2 * T, :], preferred_element_type=F32)


def near_kernel(below, above, weighted, lane_ref, tile_ref, own, total, dense0, dense1, terms):
    skip = REACH - NEAR
    jobs = []
    for i in reversed(range(REACH)):
        first = max(i, skip)
        jobs.append((i, below, (first - skip) * STRIP, first, REACH - first))
    for i in reversed(range(REACH, BLOCKS)):
        jobs.append((i, above, 0, 3 * REACH, min(i - REACH + 1, NEAR)))
    pipeline(jobs, weighted, lane_ref, tile_ref, (dense0, dense1), terms, False)
    fold = fold_matrix()
    for h in range(BLOCKS // 2):
        for c in range(9):
            at = slice(h * 32, (h + 1) * 32)
            total[c, at, :] = own[c, at, :] + jnp.dot(
                fold, terms[c, h * 2 * T:(h + 1) * 2 * T, :], preferred_element_type=F32)


def far_kernel(mode_index, below, above, weighted, lane_ref, tile_ref, before, _after,
               out0, out1, out2, out3, dense0, dense1, terms, total):
    skip = REACH - NEAR
    jobs = [(i, below, i * STRIP, i, skip - i) for i in reversed(range(skip))]
    jobs += [(i, above, 0, 3 * REACH + NEAR, i - REACH - NEAR + 1) for i in range(REACH + NEAR, BLOCKS)]
    pipeline(jobs, weighted, lane_ref, tile_ref, (dense0, dense1), terms, False)
    total[...] = before[...]
    fold = fold_matrix()
    for h in (0, BLOCKS // 2 - 1):
        for c in range(9):
            at = slice(h * 32, (h + 1) * 32)
            total[c, at, :] += jnp.dot(
                fold, terms[c, h * 2 * T:(h + 1) * 2 * T, :], preferred_element_type=F32)
    m = mode_index[0]
    for k, out in enumerate((out0, out1, out2, out3)):
        q = lax.rem(m + k, 4)
        out[...] = total[:, pl.ds(pl.multiple_of(q * QUARTER, 8), QUARTER), :].astype(BF16)


CHUNK = 512
EXT = 144


def forward_kernel(features, w_in, b_in, _after, hidden, slope, turned):
    x = features[...]
    pre = jnp.dot(x, w_in[...], preferred_element_type=F32) + b_in[...]
    sig = 1.0 / (1.0 + jnp.exp(-pre))
    hidden[...] = (pre * sig).astype(BF16)
    slope[...] = (sig * (1.0 + pre * (1.0 - sig))).astype(BF16)
    turned[0:128, :] = x.T
    row = lax.broadcasted_iota(jnp.int32, (EXT - 128, CHUNK), 0)
    turned[128:EXT, :] = (row == 0).astype(BF16)


def gradient_kernel(mode_index, p0, p1, p2, p3, turned, hidden, slope, w_out,
                    pre_cot, g0, g1, g2, g3, cot, sums):
    whole = sum(p[...].astype(F32) for p in (p0, p1, p2, p3))
    whole = jnp.concatenate([whole, jnp.zeros((7, QUARTER, T), F32)], axis=0)
    cot[...] = jnp.swapaxes(whole, 0, 1).astype(BF16)
    sums[...] = jnp.zeros_like(sums)
    w_out16 = jnp.concatenate([w_out[...].astype(F32), jnp.zeros((7, 256), F32)], axis=0).astype(BF16)
    per = CHUNK // T
    total_in, total_out = jnp.zeros((EXT, 256), F32), jnp.zeros((16, 256), F32)
    for step in range(hidden.shape[0] // CHUNK):
        rows = slice(step * CHUNK, (step + 1) * CHUNK)
        pair_cot = jnp.concatenate([cot[step * per + g] for g in range(per)], axis=1)
        part = (tn_dot(pair_cot, w_out16) * slope[rows, :].astype(F32)).astype(BF16)
        pre_cot[rows, :] = part
        total_in += jnp.dot(turned[:, rows], part, preferred_element_type=F32)
        total_out += jnp.dot(pair_cot, hidden[rows, :], preferred_element_type=F32)
    for h in range(2):
        cols = slice(h * T, (h + 1) * T)
        sums[h * 152:h * 152 + 128, :] = total_in[0:128, cols]
        sums[h * 152 + 128:h * 152 + 144, :] = total_out[:, cols]
        sums[h * 152 + 144:h * 152 + 152, :] = total_in[128:136, cols]
    m = mode_index[0]
    for k, out in enumerate((g0, g1, g2, g3)):
        q = lax.rem(m + k, 4)
        out[...] = sums[pl.ds(pl.multiple_of(q * ROWS, 8), ROWS), :]


def features_kernel(pre_cot, w_in, grad):
    grad[...] = nt_dot(pre_cot[...], w_in[...]).astype(BF16)


SUM_ROWS = 320
ROWS = SUM_ROWS // 4


def finish_kernel(mode_index, c0, c1, c2, c3, grad_w_in, grad_b_in, grad_w_out, whole):
    m = mode_index[0]
    for k, part in enumerate((c0, c1, c2, c3)):
        q = lax.rem(m + 4 - k, 4)
        whole[pl.ds(pl.multiple_of(q * ROWS, 8), ROWS), :] = part[...]
    both = []
    for start, rows in ((0, 128), (128, 9), (144, 1)):
        both.append(jnp.concatenate([whole[h * 152 + start:h * 152 + start + rows, :] for h in range(2)], axis=1))
    w, o, b = both
    norm_sq = jnp.sum(w * w) + jnp.sum(b * b) + jnp.sum(o * o)
    factor = jnp.minimum(1.0, CLIP_NORM / jnp.sqrt(jnp.broadcast_to(norm_sq + 1e-06, (1, 256))))
    grad_w_in[...] = w * factor
    grad_b_in[...] = b * factor
    grad_w_out[...] = o * factor


def shape(dims, dtype=F32):
    return jax.ShapeDtypeStruct(dims, dtype)


def cost(flops, moved):
    return pl.CostEstimate(flops=flops, bytes_accessed=moved, transcendentals=0)


def ring(axis, k):
    n = lax.axis_size(axis)
    return [(i, (i + k) % n) for i in range(n)]


def shards(eigvec, species, mode_cot, neighbours, pair_features, w_in, b_in, w_out):
    eig = jnp.transpose(eigvec, (1, 0, 2))
    m = lax.axis_index("mode").astype(jnp.int32).reshape(1)
    near, far = NEAR * STRIP, (REACH - NEAR) * STRIP
    anywhere = pl.BlockSpec(memory_space=pl.ANY)
    halves = pl.pallas_call(
        scale_kernel, out_shape=[shape((near, 256), BF16), shape((far, 256), BF16)] * 2,
        in_specs=[VMEM] * 2, out_specs=[VMEM] * 4,
        compiler_params=PARAMS, cost_estimate=cost(1 << 20, 4 << 20), name="scale",
    )(eig, species)
    high_near, high_far, low_near, low_far = halves
    up, down = ring("slab", 1), ring("slab", lax.axis_size("slab") - 1)
    below_near = lax.ppermute(high_near, "slab", up)
    above_near = lax.ppermute(low_near, "slab", down)
    own, weighted, lane, tile = pl.pallas_call(
        own_kernel,
        out_shape=[shape((9, GROUPS, T)), shape((BLOCKS, 3 * T, 256), BF16),
                   shape((BLOCKS, T, T), jnp.int16), shape((BLOCKS, T, T), jnp.int16)],
        in_specs=[VMEM] * 6, out_specs=[VMEM] * 4,
        scratch_shapes=[pltpu.VMEM((BLOCKS * STRIP, 256), BF16)]
        + [pltpu.VMEM((STRIP, BLOCKS * STRIP), BF16)] * 2 + [pltpu.VMEM((9, ATOMS, T), BF16)],
        compiler_params=PARAMS, cost_estimate=cost(12_000_000_000, 6 << 20), name="own",
    )(*halves, mode_cot.reshape(1, 256), neighbours.T)
    high_far, low_far, own = lax.optimization_barrier((high_far, low_far, own))
    below_far = lax.ppermute(high_far, "slab", up)
    above_far = lax.ppermute(low_far, "slab", down)
    slots = pair_features.shape[0]
    steps = slots // CHUNK
    rows_spec = lambda width: pl.BlockSpec((CHUNK, width), lambda s: (s, 0))
    full = lambda *dims: pl.BlockSpec(dims, lambda s: (0,) * len(dims))
    hidden, slope, turned = pl.pallas_call(
        forward_kernel, out_shape=[shape((slots, 256), BF16)] * 2 + [shape((EXT, slots), BF16)], grid=(steps,),
        in_specs=[rows_spec(128), full(128, 256), full(1, 256), anywhere],
        out_specs=[rows_spec(256)] * 2 + [pl.BlockSpec((EXT, CHUNK), lambda s: (0, s))],
        compiler_params=PARAMS, cost_estimate=cost(4_000_000_000, 8 << 20), name="forward",
    )(pair_features, w_in, b_in.reshape(1, 256), own)
    total = pl.pallas_call(
        near_kernel, out_shape=shape((9, GROUPS, T)), in_specs=[VMEM] * 6, out_specs=VMEM,
        scratch_shapes=[pltpu.VMEM((STRIP, NEAR * STRIP), BF16)] * 2 + [pltpu.VMEM((9, ATOMS, T), BF16)],
        compiler_params=PARAMS, cost_estimate=cost(4_000_000_000, 6 << 20), name="near",
    )(below_near, above_near, weighted, lane, tile, own)
    parts = pl.pallas_call(
        far_kernel, out_shape=[shape((9, QUARTER, T), BF16)] * 4,
        in_specs=[SMEM] + [VMEM] * 6 + [anywhere], out_specs=[VMEM] * 4,
        scratch_shapes=[pltpu.VMEM((STRIP, (REACH - NEAR) * STRIP), BF16)] * 2
        + [pltpu.VMEM((9, ATOMS, T), BF16), pltpu.VMEM((9, GROUPS, T), F32)],
        compiler_params=PARAMS, cost_estimate=cost(1_000_000_000, 5 << 20), name="far",
    )(m, below_far, above_far, weighted, lane, tile, total, turned)
    parts = [parts[0]] + [lax.ppermute(parts[k], "mode", ring("mode", k)) for k in (1, 2, 3)]
    pre_cot, *sums = pl.pallas_call(
        gradient_kernel,
        out_shape=[shape((slots, 256), BF16)] + [shape((ROWS, T))] * 4,
        in_specs=[SMEM] + [VMEM] * 8, out_specs=[VMEM] * 5,
        scratch_shapes=[pltpu.VMEM((QUARTER, 16, T), BF16), pltpu.VMEM((SUM_ROWS, T), F32)],
        compiler_params=PARAMS, cost_estimate=cost(2_000_000_000, 9 << 20), name="gradient",
    )(m, *parts, turned, hidden, slope, w_out)
    features_grad = pl.pallas_call(
        features_kernel, out_shape=shape((slots, 128), BF16), grid=(steps // 2,),
        in_specs=[pl.BlockSpec((2 * CHUNK, 256), lambda s: (s, 0)), full(128, 256)],
        out_specs=pl.BlockSpec((2 * CHUNK, 128), lambda s: (s, 0)),
        compiler_params=PARAMS, cost_estimate=cost(2_000_000_000, 5 << 20), name="features",
    )(pre_cot, w_in)
    share = sums[0]
    for k in (1, 2, 3):
        share = share + lax.ppermute(sums[k], "mode", ring("mode", k))
    share, features_grad = lax.optimization_barrier((share, features_grad))
    line = [[g * 8 + k for k in range(8)] for g in range(8)]
    plane = [[k * 8 + g for k in range(8)] for g in range(8)]
    for groups in (line, plane):
        spread = jnp.broadcast_to(share.astype(BF16)[None], (8, ROWS, T))
        got = lax.all_to_all(spread, "slab", 0, 0, axis_index_groups=groups, tiled=True)
        share = jnp.sum(got.astype(F32), axis=0)
    pieces = [share] + [lax.ppermute(share, "mode", ring("mode", k)) for k in (1, 2, 3)]
    grad_w_in, grad_b_in, grad_w_out = pl.pallas_call(
        finish_kernel, out_shape=[shape((128, 256)), shape((1, 256)), shape((9, 256))],
        in_specs=[SMEM] + [VMEM] * 4, out_specs=[VMEM] * 3,
        scratch_shapes=[pltpu.VMEM((SUM_ROWS, T), F32)],
        compiler_params=PARAMS, name="finish",
    )(m, *pieces)
    return (features_grad, grad_w_in, grad_b_in.reshape(256), grad_w_out)


def solution(mesh):
    return jax.shard_map(
        shards,
        mesh=mesh,
        in_specs=(
            P("slab", None, "mode"),
            P("slab"),
            P("mode"),
            P("slab", None),
            P(("slab", "mode"), None),
            P(),
            P(),
            P(),
        ),
        out_specs=(P(("slab", "mode"), None), P(), P(), P()),
        check_vma=False,
    )
```

time: 92.4 us -> 98 us (1.061)
  starting transfers between devices: 19.6 us -> 27.6 us
  local copies, waits for them, and re-layouts: 2.31 us -> 9.88 us
  blocking collectives: 26.2 us -> 20.4 us
  Pallas kernels: 35.2 us -> 30.5 us
    unnamed x16 -> x36, local copies, waits for them, and re-layouts: 2.27 us -> 9.83 us
    ppermute x2 -> x4, starting transfers between devices: 11.3 us -> 18.5 us  [the longest x1 8.85 us: shards(): above_near = lax.ppermute(low_near, 'slab', down)]
    pallas_call x1, Pallas kernels: 18 us -> 11.5 us  [shards(): pl.pallas_call(own_kernel, out_shape=[shape((9, GROUPS, T)), shape((BLOCK...]
    all_to_all x2, blocking collectives: 26.2 us -> 20.4 us  [shards(): lax.all_to_all(spread, 'slab', 0, 0, axis_index_groups=groups, tiled=True)]
    ppermute x3, waiting for transfers between devices: 0.01 us -> 3.38 us  [shards(): lax.ppermute(share, 'mode', ring('mode', k))]
    ppermute x3, waiting for transfers between devices: 3.13 us -> 0.14 us  [shards(): share = share + lax.ppermute(sums[k], 'mode', ring('mode', k))]
    pallas_call x2 -> x3, Pallas kernels: 7.27 us -> 9.23 us  [the longest x1 4.95 us: shards(): pl.pallas_call(near_kernel, out_shape=shape((9, GROUPS, T)), in_specs=[VM...]
  transfers between devices with their start and end apart: 11 -> 13, of which waited for: 6 -> 7; matrix products, arithmetic and copies ran while one was open for 0% -> 0% of each run, Pallas kernels for 27% -> 24%
where the time goes in v4:
time: 98 us; the launch traced here: 97.6 us
  Pallas kernels  30.5 us (31%)
  starting transfers between devices  27.6 us (28%)
  blocking collectives  20.4 us (21%)
  local copies, waits for them, and re-layouts  9.88 us (10%)
  waiting for transfers between devices  8.43 us (9%)
    all_to_all x2, blocking collectives, shards(): lax.all_to_all(spread, 'slab', 0, 0, axis_index_groups=groups, tiled=True)  20.4 us
    pallas_call x1, Pallas kernels, shards(): pl.pallas_call(own_kernel, out_shape=[shape((9, GROUPS, T)), shape((BLOCK...  11.5 us
    unnamed x36, local copies, waits for them, and re-layouts  9.83 us
    ppermute x1, starting transfers between devices, shards(): above_near = lax.ppermute(low_near, 'slab', down)  8.85 us
    ppermute x1, starting transfers between devices, shards(): above_far = lax.ppermute(low_far, 'slab', down)  7.19 us
    pallas_call x1, Pallas kernels, shards(): pl.pallas_call(near_kernel, out_shape=shape((9, GROUPS, T)), in_specs=[VM...  4.95 us
    ppermute x3, starting transfers between devices, shards(): lax.ppermute(share, 'mode', ring('mode', k))  4.9 us
    ppermute x3, waiting for transfers between devices, shards(): lax.ppermute(parts[k], 'mode', ring('mode', k))  4.89 us
  transfers between devices with their start and end apart: 13, of which 7 were waited for; matrix products, arithmetic and copies ran while one was open for 0% of the time, Pallas kernels for 24%

profile of v4, /device:TPU:1, one launch (start us, length us, event | category | flops | bytes accessed | tf_op | source)
XLA Modules:
  0.0 97.6 jit_solution(8218353305038749994)
XLA Ops:
  0.6 0.0 copy-start.10
  0.6 0.0 copy-start
  0.7 1.5 %copy-done = bf16[1280,3,256]{2,0,1:T(8,128)(2,1)S(1)} copy-done((bf16[1280,3,256]{2,0,1:T(8,128)(2,1)S(1)}, bf16[1280,3,256]{2,0,1:T(8,128)(2,1)}, u32[]{:S(2)}) %copy-start) | copy-done | bytes 1966104
  2.2 0.0 copy-start.5
  2.2 0.7 copy-done.5
  2.9 0.0 copy-start.7
  2.9 1.6 %scale.1 = (bf16[1152,256]{1,0:T(8,128)(2,1)}, bf16[768,256]{1,0:T(8,128)(2,1)}, bf16[1152,256]{1,0:T(8,128)(2,1)}, bf16[768,256]{1,0:T(8,128)(2,1)}) custom-call(bf16[3,1280,256]{2,1,0:T(8,128)(2,1)S(1)} %bitcast.6, s32[1280]{0:T(1024)S(1)} %copy-done.5), custom_call_target="tpu_custom_call" | custom-call | flops 1048576 | bytes 4194304 | tf_op jit(solution)/shard_map/scale/pallas_call | solution.py:273
  4.5 2.5 %collective-permute-start.2 = (bf16[1152,256]{1,0:T(8,128)(2,1)}, bf16[1152,256]{1,0:T(8,128)(2,1)}, u32[]{:S(2)}, u32[]{:S(2)}) collective-permute-start(bf16[1152,256]{1,0:T(8,128)(2,1)} %get-tuple-element.34.high_near), channel_id=1, source_target_pairs={{0,4},{4,8},{8,12},{12,16},{16,20},{20,24},{24,28},{28,32},{32,36}... | collective-permute-start | bytes 1769480 | tf_op jit(solution)/shard_map/ppermute | solution.py:280
  7.0 8.9 %collective-permute-start.3 = (bf16[1152,256]{1,0:T(8,128)(2,1)}, bf16[1152,256]{1,0:T(8,128)(2,1)}, u32[]{:S(2)}, u32[]{:S(2)}) collective-permute-start(bf16[1152,256]{1,0:T(8,128)(2,1)} %get-tuple-element.35.low_near), channel_id=1, source_target_pairs={{0,252},{4,0},{8,4},{12,8},{16,12},{20,16},{24,20},{28,24},{32,28}... | collective-permute-start | bytes 1769480 | tf_op jit(solution)/shard_map/ppermute | solution.py:281
  15.9 0.0 copy-done.10
  15.9 0.0 copy-done.7
  15.9 0.0 copy-start.6
  15.9 0.0 copy-start.11
  15.9 11.5 %own.1 = (f32[9,160,128]{2,1,0:T(8,128)S(1)}, bf16[10,384,256]{2,1,0:T(8,128)(2,1)S(1)}, s16[10,128,128]{2,1,0:T(8,128)(2,1)S(1)}, s16[10,128,128]{2,1,0:T(8,128)(2,1)S(1)}) custom-call(bf16[1152,256]{1,0:T(8,128)(2,1)} %get-tuple-element.34.high_near, bf16[768,256]{1,0:T(8,128)(2,1)} %get-tuple-element.37.high_far, ...), custom_call_target="tpu_custom_call" | custom-call | flops 12000000000 | bytes 6291456 | tf_op jit(solution)/shard_map/own/pallas_call | solution.py:282
  27.4 0.7 copy-done.1
  28.1 0.7 copy-done.3
  28.8 0.0 collective-permute-start
  28.8 7.2 %collective-permute-start.1 = (bf16[768,256]{1,0:T(8,128)(2,1)}, bf16[768,256]{1,0:T(8,128)(2,1)}, u32[]{:S(2)}, u32[]{:S(2)}) collective-permute-start(bf16[768,256]{1,0:T(8,128)(2,1)} %get-tuple-element.38.low_far), channel_id=1, source_target_pairs={{0,252},{4,0},{8,4},{12,8},{16,12},{20,16},{24,20},{28,24},{32,28}... | collective-permute-start | bytes 1179656 | tf_op jit(solution)/shard_map/ppermute | solution.py:293
  36.0 0.0 copy-done.6
  36.0 0.0 copy-done.8
  36.0 0.0 copy-done.11
  36.0 3.8 %forward.1 = (bf16[5120,256]{1,0:T(8,128)(2,1)S(1)}, bf16[5120,256]{1,0:T(8,128)(2,1)S(1)}, bf16[144,5120]{1,0:T(8,128)(2,1)S(1)}) custom-call(bf16[5120,128]{1,0:T(8,128)(2,1)S(1)} %copy-done.6, bf16[128,256]{1,0:T(8,128)(2,1)S(1)} %copy-done.8, f32[1,256]{1,0:T(1,128)S(1)} %bitcast.9, f32[9,160,128]{2,1,0:T(8,128)S(1)} %get-tuple-element.42.own._after), custom_call_target="tpu_custom_call" | custom-call | flops 4000000000 | bytes 8388608 | tf_op jit(solution)/shard_map/forward/pallas_call | solution.py:298
  39.9 0.0 copy-done.16
  39.9 0.0 copy-start.12
  39.9 1.5 %copy-done.12 = bf16[5120,256]{1,0:T(8,128)(2,1)} copy-done((bf16[5120,256]{1,0:T(8,128)(2,1)}, bf16[5120,256]{1,0:T(8,128)(2,1)S(1)}, u32[]{:S(2)}) %copy-start.12) | copy-done | bytes 2621464
  41.4 1.5 %copy-done.14 = bf16[5120,256]{1,0:T(8,128)(2,1)} copy-done((bf16[5120,256]{1,0:T(8,128)(2,1)}, bf16[5120,256]{1,0:T(8,128)(2,1)S(1)}, u32[]{:S(2)}) %copy-start.14) | copy-done | bytes 2621464
  42.9 0.0 collective-permute-done.2.below
  42.9 0.0 collective-permute-done.3.above
  42.9 1.0 copy-done.2
  43.9 1.0 copy-done.4
  44.9 1.1 %copy-done.17 = f32[9,160,128]{2,1,0:T(8,128)S(1)} copy-done((f32[9,160,128]{2,1,0:T(8,128)S(1)}, f32[9,160,128]{2,1,0:T(8,128)}, u32[]{:S(2)}) %copy-start.17) | copy-done | bytes 737304
  46.0 4.9 %near.1.before = f32[9,160,128]{2,1,0:T(8,128)S(1)} custom-call(bf16[1152,256]{1,0:T(8,128)(2,1)} %collective-permute-done.2.below, bf16[1152,256]{1,0:T(8,128)(2,1)} %collective-permute-done.3.above, bf16[10,384,256]{2,1,0:T(8,128)(2,1)S(1)} %get-tuple-element.39.weighted, s16[10,128,128]{2,1,0:T(8,128)(2,1)S(1)} %copy-done.2, ...), custom_call_target="tpu_custom_call" | custom-call | flops 4000000000 | bytes 6291456 | tf_op jit(solution)/shard_map/near/pallas_call | solution.py:304
  50.9 0.0 collective-permute-done.below
  51.0 0.0 collective-permute-done.1.above
  51.0 0.0 copy-start.9
  51.0 0.0 copy-start.13
  51.0 0.0 copy-start.15
  51.0 2.6 %far.1 = (bf16[9,40,128]{2,1,0:T(8,128)(2,1)S(1)}, bf16[9,40,128]{2,1,0:T(8,128)(2,1)S(1)}, bf16[9,40,128]{2,1,0:T(8,128)(2,1)S(1)}, bf16[9,40,128]{2,1,0:T(8,128)(2,1)S(1)}) custom-call(s32[1]{0:T(128)} %bitcast.mode_index, bf16[768,256]{1,0:T(8,128)(2,1)} %collective-permute-done.below, bf16[768,256]{1,0:T(8,128)(2,1)} %collective-permute-done.1.above, ...), custom_call_target="tpu_custom_call" | custom-call | flops 1000000000 | bytes 5242880 | tf_op jit(solution)/shard_map/far/pallas_call | solution.py:309
  53.6 1.8 %collective-permute-start.4 = (bf16[9,40,128]{2,1,0:T(8,128)(2,1)S(1)}, bf16[9,40,128]{2,1,0:T(8,128)(2,1)S(1)}, u32[]{:S(2)}, u32[]{:S(2)}) collective-permute-start(bf16[9,40,128]{2,1,0:T(8,128)(2,1)S(1)} %get-tuple-element.45), channel_id=1, source_target_pairs={{0,1},{1,2},{2,3},{3,0},{4,5},{5,6},{6,7},{7,4},{8,9},{9,10},{10,1... | collective-permute-start | bytes 276488 | tf_op jit(solution)/shard_map/ppermute | solution.py:316
  55.4 1.2 %collective-permute-start.5 = (bf16[9,40,128]{2,1,0:T(8,128)(2,1)S(1)}, bf16[9,40,128]{2,1,0:T(8,128)(2,1)S(1)}, u32[]{:S(2)}, u32[]{:S(2)}) collective-permute-start(bf16[9,40,128]{2,1,0:T(8,128)(2,1)S(1)} %get-tuple-element.46), channel_id=1, source_target_pairs={{0,2},{1,3},{2,0},{3,1},{4,6},{5,7},{6,4},{7,5},{8,10},{9,11},{10,... | collective-permute-start | bytes 276488 | tf_op jit(solution)/shard_map/ppermute | solution.py:316
  56.6 0.0 collective-permute-start.6
  56.6 0.7 collective-permute-done.4.p1
  57.3 3.6 %collective-permute-done.5.p2 = bf16[9,40,128]{2,1,0:T(8,128)(2,1)S(1)} collective-permute-done((bf16[9,40,128]{2,1,0:T(8,128)(2,1)S(1)}, bf16[9,40,128]{2,1,0:T(8,128)(2,1)S(1)}, u32[]{:S(2)}, u32[]{:S(2)}) %collective-permute-start.5) | collective-permute-done | bytes 92192 | tf_op jit(solution)/shard_map/ppermute | solution.py:316
  60.9 0.6 collective-permute-done.6.p3
  61.5 0.0 copy-done.9
  61.5 0.0 copy-done.13
  61.5 0.0 copy-done.15
  61.5 2.1 %gradient.1 = (bf16[5120,256]{1,0:T(8,128)(2,1)S(1)}, f32[80,128]{1,0:T(8,128)S(1)}, f32[80,128]{1,0:T(8,128)S(1)}, f32[80,128]{1,0:T(8,128)S(1)}, f32[80,128]{1,0:T(8,128)S(1)}) custom-call(s32[1]{0:T(128)} %bitcast.mode_index, bf16[9,40,128]{2,1,0:T(8,128)(2,1)S(1)} %get-tuple-element.44.p0, bf16[9,40,128]{2,1,0:T(8,128)(2,1)S(1)} %collective-permute-done.4.p1, ...), custom_call_target="tpu_custom_call" | custom-call | flops 2000000000 | bytes 9437184 | tf_op jit(solution)/shard_map/gradient/pallas_call | solution.py:317
  63.6 0.1 collective-permute-start.7
  63.7 0.7 collective-permute-start.8
  64.4 0.4 collective-permute-start.9
  64.8 3.0 %features.3 = bf16[5120,128]{1,0:T(8,128)(2,1)} custom-call(bf16[5120,256]{1,0:T(8,128)(2,1)S(1)} %get-tuple-element.54.pre_cot, bf16[128,256]{1,0:T(8,128)(2,1)S(1)} %copy-done.8), custom_call_target="tpu_custom_call" | custom-call | flops 2000000000 | bytes 5242880 | tf_op jit(solution)/shard_map/features/pallas_call | solution.py:324
  67.8 0.0 collective-permute-done.7
  67.8 0.0 collective-permute-done.8
  67.8 0.1 collective-permute-done.9
  68.0 10.7 %all_to_all.10 = bf16[8,80,128]{2,1,0:T(8,128)(2,1)S(1)} all-to-all(bf16[8,80,128]{2,1,0:T(8,128)(2,1)S(1)} %broadcast_in_dim.4), channel_id=1, replica_groups={{0,4,8,12,16,20,24,28},{32,36,40,44,48,52,56,60},{64,68,72,76,80,84,88,..., dimensions={0} | all-to-all | bytes 327680 | tf_op jit(solution)/shard_map/all_to_all | solution.py:338
  78.8 9.7 %all_to_all.11 = bf16[8,80,128]{2,1,0:T(8,128)(2,1)S(1)} all-to-all(bf16[8,80,128]{2,1,0:T(8,128)(2,1)S(1)} %broadcast_in_dim.5), channel_id=1, replica_groups={{0,32,64,96,128,160,192,224},{4,36,68,100,132,164,196,228},{8,40,72,104..., dimensions={0} | all-to-all | bytes 327680 | tf_op jit(solution)/shard_map/all_to_all | solution.py:338
  88.5 4.4 %collective-permute-start.10 = (f32[80,128]{1,0:T(8,128)S(1)}, f32[80,128]{1,0:T(8,128)S(1)}, u32[]{:S(2)}, u32[]{:S(2)}) collective-permute-start(f32[80,128]{1,0:T(8,128)S(1)} %convert_reduce_fusion.c0), channel_id=1, source_target_pairs={{0,1},{1,2},{2,3},{3,0},{4,5},{5,6},{6,7},{7,4},{8,9},{9,10},{10,1... | collective-permute-start | bytes 122888 | tf_op jit(solution)/shard_map/ppermute | solution.py:340
  92.9 0.5 collective-permute-start.11
  93.3 0.0 collective-permute-start.12
  93.4 0.6 collective-permute-done.10.c1
  94.0 1.8 %collective-permute-done.11.c2 = f32[80,128]{1,0:T(8,128)S(1)} collective-permute-done((f32[80,128]{1,0:T(8,128)S(1)}, f32[80,128]{1,0:T(8,128)S(1)}, u32[]{:S(2)}, u32[]{:S(2)}) %collective-permute-start.11) | collective-permute-done | bytes 40992 | tf_op jit(solution)/shard_map/ppermute | solution.py:340
  95.8 0.9 collective-permute-done.12.c3
  96.8 0.9 finish.1
  (13 shorter events, 0.1 us)
Async XLA Ops:
  0.6 15.2 %copy-start.10 = (f32[256]{0:T(256)S(1)}, f32[256]{0:T(256)}, u32[]{:S(2)}) copy-start(f32[256]{0:T(256)} %param.10) | copy-start | bytes 3076
  0.6 1.6 %copy-start = (bf16[1280,3,256]{2,0,1:T(8,128)(2,1)S(1)}, bf16[1280,3,256]{2,0,1:T(8,128)(2,1)}, u32[]{:S(2)}) copy-start(bf16[1280,3,256]{2,0,1:T(8,128)(2,1)} %param.8) | copy-start | bytes 5898244
  2.2 0.7 copy-start.5
  2.9 13.0 %copy-start.7 = (s32[1280,16]{0,1:T(8,128)S(1)}, s32[1280,16]{0,1:T(8,128)}, u32[]{:S(2)}) copy-start(s32[1280,16]{0,1:T(8,128)} %param.11) | copy-start | bytes 245764
  4.5 38.4 %collective-permute-start.2 = (bf16[1152,256]{1,0:T(8,128)(2,1)}, bf16[1152,256]{1,0:T(8,128)(2,1)}, u32[]{:S(2)}, u32[]{:S(2)}) collective-permute-start(bf16[1152,256]{1,0:T(8,128)(2,1)} %get-tuple-element.34.high_near), channel_id=1, source_target_pairs={{0,4},{4,8},{8,12},{12,16},{16,20},{20,24},{24,28},{28,32},{32,36}... | collective-permute-start | bytes 1769480 | tf_op jit(solution)/shard_map/ppermute | solution.py:280
  7.0 35.9 %collective-permute-start.3 = (bf16[1152,256]{1,0:T(8,128)(2,1)}, bf16[1152,256]{1,0:T(8,128)(2,1)}, u32[]{:S(2)}, u32[]{:S(2)}) collective-permute-start(bf16[1152,256]{1,0:T(8,128)(2,1)} %get-tuple-element.35.low_near), channel_id=1, source_target_pairs={{0,252},{4,0},{8,4},{12,8},{16,12},{20,16},{24,20},{28,24},{32,28}... | collective-permute-start | bytes 1769480 | tf_op jit(solution)/shard_map/ppermute | solution.py:281
  15.9 20.2 %copy-start.6 = (bf16[5120,128]{1,0:T(8,128)(2,1)S(1)}, bf16[5120,128]{1,0:T(8,128)(2,1)}, u32[]{:S(2)}) copy-start(bf16[5120,128]{1,0:T(8,128)(2,1)} %features.2) | copy-start | bytes 3932164
  15.9 20.2 %copy-start.8 = (bf16[128,256]{1,0:T(8,128)(2,1)S(1)}, bf16[128,256]{1,0:T(8,128)(2,1)}, u32[]{:S(2)}) copy-start(bf16[128,256]{1,0:T(8,128)(2,1)} %w_in.3) | copy-start | bytes 196612
  15.9 20.2 %copy-start.11 = (f32[256]{0:T(256)S(1)}, f32[256]{0:T(256)}, u32[]{:S(2)}) copy-start(f32[256]{0:T(256)} %param.14) | copy-start | bytes 3076
  27.4 0.7 copy-start.1
  28.1 0.7 copy-start.3
  28.8 11.0 %copy-start.16 = (f32[9,160,128]{2,1,0:T(8,128)}, f32[9,160,128]{2,1,0:T(8,128)S(1)}, u32[]{:S(2)}) copy-start(f32[9,160,128]{2,1,0:T(8,128)S(1)} %get-tuple-element.42.own._after) | copy-start | bytes 2211844
  28.8 22.1 %collective-permute-start = (bf16[768,256]{1,0:T(8,128)(2,1)}, bf16[768,256]{1,0:T(8,128)(2,1)}, u32[]{:S(2)}, u32[]{:S(2)}) collective-permute-start(bf16[768,256]{1,0:T(8,128)(2,1)} %get-tuple-element.37.high_far), channel_id=1, source_target_pairs={{0,4},{4,8},{8,12},{12,16},{16,20},{20,24},{24,28},{28,32},{32,36}... | collective-permute-start | bytes 1179656 | tf_op jit(solution)/shard_map/ppermute | solution.py:292
  28.8 22.1 %collective-permute-start.1 = (bf16[768,256]{1,0:T(8,128)(2,1)}, bf16[768,256]{1,0:T(8,128)(2,1)}, u32[]{:S(2)}, u32[]{:S(2)}) collective-permute-start(bf16[768,256]{1,0:T(8,128)(2,1)} %get-tuple-element.38.low_far), channel_id=1, source_target_pairs={{0,252},{4,0},{8,4},{12,8},{16,12},{20,16},{24,20},{28,24},{32,28}... | collective-permute-start | bytes 1179656 | tf_op jit(solution)/shard_map/ppermute | solution.py:293
  39.9 1.5 %copy-start.12 = (bf16[5120,256]{1,0:T(8,128)(2,1)}, bf16[5120,256]{1,0:T(8,128)(2,1)S(1)}, u32[]{:S(2)}) copy-start(bf16[5120,256]{1,0:T(8,128)(2,1)S(1)} %get-tuple-element.48.hidden) | copy-start | bytes 7864324
  41.4 1.5 %copy-start.14 = (bf16[5120,256]{1,0:T(8,128)(2,1)}, bf16[5120,256]{1,0:T(8,128)(2,1)S(1)}, u32[]{:S(2)}) copy-start(bf16[5120,256]{1,0:T(8,128)(2,1)S(1)} %get-tuple-element.49.slope) | copy-start | bytes 7864324
  42.9 1.0 copy-start.2
  43.9 1.0 copy-start.4
  44.9 1.1 %copy-start.17 = (f32[9,160,128]{2,1,0:T(8,128)S(1)}, f32[9,160,128]{2,1,0:T(8,128)}, u32[]{:S(2)}) copy-start(f32[9,160,128]{2,1,0:T(8,128)} %copy-done.16) | copy-start | bytes 2211844
  51.0 10.5 %copy-start.9 = (bf16[9,256]{1,0:T(8,128)(2,1)S(1)}, bf16[9,256]{1,0:T(8,128)(2,1)}, u32[]{:S(2)}) copy-start(bf16[9,256]{1,0:T(8,128)(2,1)} %w_out.1) | copy-start | bytes 13828
  51.0 10.5 %copy-start.13 = (bf16[5120,256]{1,0:T(8,128)(2,1)S(1)}, bf16[5120,256]{1,0:T(8,128)(2,1)}, u32[]{:S(2)}) copy-start(bf16[5120,256]{1,0:T(8,128)(2,1)} %copy-done.12) | copy-start | bytes 7864324
  51.0 10.5 %copy-start.15 = (bf16[5120,256]{1,0:T(8,128)(2,1)S(1)}, bf16[5120,256]{1,0:T(8,128)(2,1)}, u32[]{:S(2)}) copy-start(bf16[5120,256]{1,0:T(8,128)(2,1)} %copy-done.14) | copy-start | bytes 7864324
  53.6 3.6 %collective-permute-start.4 = (bf16[9,40,128]{2,1,0:T(8,128)(2,1)S(1)}, bf16[9,40,128]{2,1,0:T(8,128)(2,1)S(1)}, u32[]{:S(2)}, u32[]{:S(2)}) collective-permute-start(bf16[9,40,128]{2,1,0:T(8,128)(2,1)S(1)} %get-tuple-element.45), channel_id=1, source_target_pairs={{0,1},{1,2},{2,3},{3,0},{4,5},{5,6},{6,7},{7,4},{8,9},{9,10},{10,1... | collective-permute-start | bytes 276488 | tf_op jit(solution)/shard_map/ppermute | solution.py:316
  55.4 5.4 %collective-permute-start.5 = (bf16[9,40,128]{2,1,0:T(8,128)(2,1)S(1)}, bf16[9,40,128]{2,1,0:T(8,128)(2,1)S(1)}, u32[]{:S(2)}, u32[]{:S(2)}) collective-permute-start(bf16[9,40,128]{2,1,0:T(8,128)(2,1)S(1)} %get-tuple-element.46), channel_id=1, source_target_pairs={{0,2},{1,3},{2,0},{3,1},{4,6},{5,7},{6,4},{7,5},{8,10},{9,11},{10,... | collective-permute-start | bytes 276488 | tf_op jit(solution)/shard_map/ppermute | solution.py:316
  56.6 4.9 %collective-permute-start.6 = (bf16[9,40,128]{2,1,0:T(8,128)(2,1)S(1)}, bf16[9,40,128]{2,1,0:T(8,128)(2,1)S(1)}, u32[]{:S(2)}, u32[]{:S(2)}) collective-permute-start(bf16[9,40,128]{2,1,0:T(8,128)(2,1)S(1)} %get-tuple-element.47), channel_id=1, source_target_pairs={{0,3},{1,0},{2,1},{3,2},{4,7},{5,4},{6,5},{7,6},{8,11},{9,8},{10,9... | collective-permute-start | bytes 276488 | tf_op jit(solution)/shard_map/ppermute | solution.py:316
  63.6 4.2 %collective-permute-start.7 = (f32[80,128]{1,0:T(8,128)S(1)}, f32[80,128]{1,0:T(8,128)S(1)}, u32[]{:S(2)}, u32[]{:S(2)}) collective-permute-start(f32[80,128]{1,0:T(8,128)S(1)} %get-tuple-element.51), channel_id=1, source_target_pairs={{0,1},{1,2},{2,3},{3,0},{4,5},{5,6},{6,7},{7,4},{8,9},{9,10},{10,1... | collective-permute-start | bytes 122888 | tf_op jit(solution)/shard_map/ppermute | solution.py:332
  63.7 4.1 %collective-permute-start.8 = (f32[80,128]{1,0:T(8,128)S(1)}, f32[80,128]{1,0:T(8,128)S(1)}, u32[]{:S(2)}, u32[]{:S(2)}) collective-permute-start(f32[80,128]{1,0:T(8,128)S(1)} %get-tuple-element.52), channel_id=1, source_target_pairs={{0,2},{1,3},{2,0},{3,1},{4,6},{5,7},{6,4},{7,5},{8,10},{9,11},{10,... | collective-permute-start | bytes 122888 | tf_op jit(solution)/shard_map/ppermute | solution.py:332
  64.4 3.6 %collective-permute-start.9 = (f32[80,128]{1,0:T(8,128)S(1)}, f32[80,128]{1,0:T(8,128)S(1)}, u32[]{:S(2)}, u32[]{:S(2)}) collective-permute-start(f32[80,128]{1,0:T(8,128)S(1)} %get-tuple-element.53), channel_id=1, source_target_pairs={{0,3},{1,0},{2,1},{3,2},{4,7},{5,4},{6,5},{7,6},{8,11},{9,8},{10,9... | collective-permute-start | bytes 122888 | tf_op jit(solution)/shard_map/ppermute | solution.py:332
  88.5 5.5 %collective-permute-start.10 = (f32[80,128]{1,0:T(8,128)S(1)}, f32[80,128]{1,0:T(8,128)S(1)}, u32[]{:S(2)}, u32[]{:S(2)}) collective-permute-start(f32[80,128]{1,0:T(8,128)S(1)} %convert_reduce_fusion.c0), channel_id=1, source_target_pairs={{0,1},{1,2},{2,3},{3,0},{4,5},{5,6},{6,7},{7,4},{8,9},{9,10},{10,1... | collective-permute-start | bytes 122888 | tf_op jit(solution)/shard_map/ppermute | solution.py:340
  92.9 3.0 %collective-permute-start.11 = (f32[80,128]{1,0:T(8,128)S(1)}, f32[80,128]{1,0:T(8,128)S(1)}, u32[]{:S(2)}, u32[]{:S(2)}) collective-permute-start(f32[80,128]{1,0:T(8,128)S(1)} %convert_reduce_fusion.c0), channel_id=1, source_target_pairs={{0,2},{1,3},{2,0},{3,1},{4,6},{5,7},{6,4},{7,5},{8,10},{9,11},{10,... | collective-permute-start | bytes 122888 | tf_op jit(solution)/shard_map/ppermute | solution.py:340
  93.3 3.4 %collective-permute-start.12 = (f32[80,128]{1,0:T(8,128)S(1)}, f32[80,128]{1,0:T(8,128)S(1)}, u32[]{:S(2)}, u32[]{:S(2)}) collective-permute-start(f32[80,128]{1,0:T(8,128)S(1)} %convert_reduce_fusion.c0), channel_id=1, source_target_pairs={{0,3},{1,0},{2,1},{3,2},{4,7},{5,4},{6,5},{7,6},{8,11},{9,8},{10,9... | collective-permute-start | bytes 122888 | tf_op jit(solution)/shard_map/ppermute | solution.py:340

commit v5 on v4

--- a/solution.py
+++ b/solution.py
@@ -19,7 +19,7 @@
 F32, BF16 = jnp.float32, jnp.bfloat16
 VMEM = pl.BlockSpec(memory_space=pltpu.VMEM)
 SMEM = pl.BlockSpec(memory_space=pltpu.SMEM)
-PARAMS = pltpu.CompilerParams(vmem_limit_bytes=40 << 20)
+PARAMS = pltpu.CompilerParams(vmem_limit_bytes=24 << 20)
 
 
 def nt_dot(x, y):
@@ -123,7 +123,7 @@
         turn(0, 0)
 
 
-def own_kernel(high_near, high_far, low_near, low_far, mode_cot, nbr_t, out, weighted, lane_ref, tile_ref, stack, dense0, dense1, terms):
+def own_kernel(high_near, high_far, low_near, low_far, mode_cot, nbr_t, _after, out, weighted, lane_ref, tile_ref, stack, dense0, dense1, terms):
     row = lax.broadcasted_iota(jnp.int32, (T, T), 0)
     col = lax.broadcasted_iota(jnp.int32, (T, T), 1)
     diagonal = (row % 8) == (col // 16)
@@ -167,7 +167,7 @@
                 fold, terms[c, h * 2 * T:(h + 1) * 2 * T, :], preferred_element_type=F32)
 
 
-def far_kernel(mode_index, below, above, weighted, lane_ref, tile_ref, before, _after,
+def far_kernel(mode_index, below, above, weighted, lane_ref, tile_ref, before,
                out0, out1, out2, out3, dense0, dense1, terms, total):
     skip = REACH - NEAR
     jobs = [(i, below, i * STRIP, i, skip - i) for i in reversed(range(skip))]
@@ -190,7 +190,7 @@
 EXT = 144
 
 
-def forward_kernel(features, w_in, b_in, _after, hidden, slope, turned):
+def forward_kernel(features, w_in, b_in, hidden, slope, turned):
     x = features[...]
     pre = jnp.dot(x, w_in[...], preferred_element_type=F32) + b_in[...]
     sig = 1.0 / (1.0 + jnp.exp(-pre))
@@ -279,28 +279,28 @@
     up, down = ring("slab", 1), ring("slab", lax.axis_size("slab") - 1)
     below_near = lax.ppermute(high_near, "slab", up)
     above_near = lax.ppermute(low_near, "slab", down)
-    own, weighted, lane, tile = pl.pallas_call(
-        own_kernel,
-        out_shape=[shape((9, GROUPS, T)), shape((BLOCKS, 3 * T, 256), BF16),
-                   shape((BLOCKS, T, T), jnp.int16), shape((BLOCKS, T, T), jnp.int16)],
-        in_specs=[VMEM] * 6, out_specs=[VMEM] * 4,
-        scratch_shapes=[pltpu.VMEM((BLOCKS * STRIP, 256), BF16)]
-        + [pltpu.VMEM((STRIP, BLOCKS * STRIP), BF16)] * 2 + [pltpu.VMEM((9, ATOMS, T), BF16)],
-        compiler_params=PARAMS, cost_estimate=cost(12_000_000_000, 6 << 20), name="own",
-    )(*halves, mode_cot.reshape(1, 256), neighbours.T)
-    high_far, low_far, own = lax.optimization_barrier((high_far, low_far, own))
-    below_far = lax.ppermute(high_far, "slab", up)
-    above_far = lax.ppermute(low_far, "slab", down)
     slots = pair_features.shape[0]
     steps = slots // CHUNK
     rows_spec = lambda width: pl.BlockSpec((CHUNK, width), lambda s: (s, 0))
     full = lambda *dims: pl.BlockSpec(dims, lambda s: (0,) * len(dims))
     hidden, slope, turned = pl.pallas_call(
         forward_kernel, out_shape=[shape((slots, 256), BF16)] * 2 + [shape((EXT, slots), BF16)], grid=(steps,),
-        in_specs=[rows_spec(128), full(128, 256), full(1, 256), anywhere],
+        in_specs=[rows_spec(128), full(128, 256), full(1, 256)],
         out_specs=[rows_spec(256)] * 2 + [pl.BlockSpec((EXT, CHUNK), lambda s: (0, s))],
         compiler_params=PARAMS, cost_estimate=cost(4_000_000_000, 8 << 20), name="forward",
-    )(pair_features, w_in, b_in.reshape(1, 256), own)
+    )(pair_features, w_in, b_in.reshape(1, 256))
+    high_far, low_far, turned = lax.optimization_barrier((high_far, low_far, turned))
+    below_far = lax.ppermute(high_far, "slab", up)
+    above_far = lax.ppermute(low_far, "slab", down)
+    own, weighted, lane, tile = pl.pallas_call(
+        own_kernel,
+        out_shape=[shape((9, GROUPS, T)), shape((BLOCKS, 3 * T, 256), BF16),
+                   shape((BLOCKS, T, T), jnp.int16), shape((BLOCKS, T, T), jnp.int16)],
+        in_specs=[VMEM] * 6 + [anywhere], out_specs=[VMEM] * 4,
+        scratch_shapes=[pltpu.VMEM((BLOCKS * STRIP, 256), BF16)]
+        + [pltpu.VMEM((STRIP, BLOCKS * STRIP), BF16)] * 2 + [pltpu.VMEM((9, ATOMS, T), BF16)],
+        compiler_params=PARAMS, cost_estimate=cost(12_000_000_000, 6 << 20), name="own",
+    )(high_near, high_far, low_near, low_far, mode_cot.reshape(1, 256), neighbours.T, turned)
     total = pl.pallas_call(
         near_kernel, out_shape=shape((9, GROUPS, T)), in_specs=[VMEM] * 6, out_specs=VMEM,
         scratch_shapes=[pltpu.VMEM((STRIP, NEAR * STRIP), BF16)] * 2 + [pltpu.VMEM((9, ATOMS, T), BF16)],
@@ -308,11 +308,11 @@
     )(below_near, above_near, weighted, lane, tile, own)
     parts = pl.pallas_call(
         far_kernel, out_shape=[shape((9, QUARTER, T), BF16)] * 4,
-        in_specs=[SMEM] + [VMEM] * 6 + [anywhere], out_specs=[VMEM] * 4,
+        in_specs=[SMEM] + [VMEM] * 6, out_specs=[VMEM] * 4,
         scratch_shapes=[pltpu.VMEM((STRIP, (REACH - NEAR) * STRIP), BF16)] * 2
         + [pltpu.VMEM((9, ATOMS, T), BF16), pltpu.VMEM((9, GROUPS, T), F32)],
         compiler_params=PARAMS, cost_estimate=cost(1_000_000_000, 5 << 20), name="far",
-    )(m, below_far, above_far, weighted, lane, tile, total, turned)
+    )(m, below_far, above_far, weighted, lane, tile, total)
     parts = [parts[0]] + [lax.ppermute(parts[k], "mode", ring("mode", k)) for k in (1, 2, 3)]
     pre_cot, *sums = pl.pallas_call(
         gradient_kernel,
@@ -330,7 +330,6 @@
     share = sums[0]
     for k in (1, 2, 3):
         share = share + lax.ppermute(sums[k], "mode", ring("mode", k))
-    share, features_grad = lax.optimization_barrier((share, features_grad))
     line = [[g * 8 + k for k in range(8)] for g in range(8)]
     plane = [[k * 8 + g for k in range(8)] for g in range(8)]
     for groups in (line, plane):

time: 98 us -> 94.3 us (0.962)
  local copies, waits for them, and re-layouts: 9.88 us -> 7.37 us
  Pallas kernels: 30.5 us -> 29.4 us
  starting transfers between devices: 27.6 us -> 26.5 us
  blocking collectives: 20.4 us -> 21.4 us
    ppermute x3, waiting for transfers between devices: 0.14 us -> 3.13 us  [shards(): share = share + lax.ppermute(sums[k], 'mode', ring('mode', k))]
    ppermute x3, waiting for transfers between devices: 3.38 us -> 0.41 us  [shards(): lax.ppermute(share, 'mode', ring('mode', k))]
    unnamed x36 -> x32, local copies, waits for them, and re-layouts: 9.83 us -> 7.32 us
    pallas_call x1, Pallas kernels: 2.64 us -> 1.37 us  [shards(): pl.pallas_call(far_kernel, out_shape=[shape((9, QUARTER, T), BF16)] * 4,...]
    ppermute x3, starting transfers between devices: 4.9 us -> 3.9 us  [shards(): lax.ppermute(share, 'mode', ring('mode', k))]
  transfers between devices with their start and end apart: 13 -> 13, of which waited for: 7 -> 7; matrix products, arithmetic and copies ran while one was open for 0% -> 0% of each run, Pallas kernels for 24% -> 25%
where the time goes in v5:
time: 94.3 us; the launch traced here: 94 us
  Pallas kernels  29.4 us (31%)
  starting transfers between devices  26.5 us (28%)
  blocking collectives  21.4 us (23%)
  waiting for transfers between devices  8.45 us (9%)
  local copies, waits for them, and re-layouts  7.37 us (8%)
    all_to_all x2, blocking collectives, shards(): lax.all_to_all(spread, 'slab', 0, 0, axis_index_groups=groups, tiled=True)  21.4 us
    pallas_call x1, Pallas kernels, shards(): pl.pallas_call(own_kernel, out_shape=[shape((9, GROUPS, T)), shape((BLOCK...  11.4 us
    ppermute x1, starting transfers between devices, shards(): above_near = lax.ppermute(low_near, 'slab', down)  8.85 us
    unnamed x32, local copies, waits for them, and re-layouts  7.32 us
    ppermute x1, starting transfers between devices, shards(): above_far = lax.ppermute(low_far, 'slab', down)  7.19 us
    pallas_call x1, Pallas kernels, shards(): pl.pallas_call(near_kernel, out_shape=shape((9, GROUPS, T)), in_specs=[VM...  5.34 us
    ppermute x3, waiting for transfers between devices, shards(): lax.ppermute(parts[k], 'mode', ring('mode', k))  4.89 us
    ppermute x3, starting transfers between devices, shards(): lax.ppermute(share, 'mode', ring('mode', k))  3.9 us
  transfers between devices with their start and end apart: 13, of which 7 were waited for; matrix products, arithmetic and copies ran while one was open for 0% of the time, Pallas kernels for 25%

profile of v5, /device:TPU:1, one launch (start us, length us, event | category | flops | bytes accessed | tf_op | source)
XLA Modules:
  0.0 94.0 jit_solution(8513071116959176465)
XLA Ops:
  0.6 0.0 copy-start.6
  0.6 0.0 copy-start
  0.7 1.5 %copy-done = bf16[1280,3,256]{2,0,1:T(8,128)(2,1)S(1)} copy-done((bf16[1280,3,256]{2,0,1:T(8,128)(2,1)S(1)}, bf16[1280,3,256]{2,0,1:T(8,128)(2,1)}, u32[]{:S(2)}) %copy-start) | copy-done | bytes 1966104
  2.2 0.0 copy-start.1
  2.2 0.7 copy-done.1
  2.9 0.0 copy-start.2
  2.9 0.0 copy-start.4
  2.9 1.5 %scale.1 = (bf16[1152,256]{1,0:T(8,128)(2,1)}, bf16[768,256]{1,0:T(8,128)(2,1)}, bf16[1152,256]{1,0:T(8,128)(2,1)}, bf16[768,256]{1,0:T(8,128)(2,1)}) custom-call(bf16[3,1280,256]{2,1,0:T(8,128)(2,1)S(1)} %bitcast.6, s32[1280]{0:T(1024)S(1)} %copy-done.1), custom_call_target="tpu_custom_call" | custom-call | flops 1048576 | bytes 4194304 | tf_op jit(solution)/shard_map/scale/pallas_call | solution.py:273
  4.4 2.5 %collective-permute-start.2 = (bf16[1152,256]{1,0:T(8,128)(2,1)}, bf16[1152,256]{1,0:T(8,128)(2,1)}, u32[]{:S(2)}, u32[]{:S(2)}) collective-permute-start(bf16[1152,256]{1,0:T(8,128)(2,1)} %get-tuple-element.35.high_near), channel_id=1, source_target_pairs={{0,4},{4,8},{8,12},{12,16},{16,20},{20,24},{24,28},{28,32},{32,36}... | collective-permute-start | bytes 1769480 | tf_op jit(solution)/shard_map/ppermute | solution.py:280
  6.9 8.9 %collective-permute-start.3 = (bf16[1152,256]{1,0:T(8,128)(2,1)}, bf16[1152,256]{1,0:T(8,128)(2,1)}, u32[]{:S(2)}, u32[]{:S(2)}) collective-permute-start(bf16[1152,256]{1,0:T(8,128)(2,1)} %get-tuple-element.36.low_near), channel_id=1, source_target_pairs={{0,252},{4,0},{8,4},{12,8},{16,12},{20,16},{24,20},{28,24},{32,28}... | collective-permute-start | bytes 1769480 | tf_op jit(solution)/shard_map/ppermute | solution.py:281
  15.8 0.0 copy-done.6
  15.8 0.0 copy-done.2
  15.8 0.0 copy-done.4
  15.8 0.0 copy-start.3
  15.8 0.0 copy-start.7
  15.8 3.8 %forward.1 = (bf16[5120,256]{1,0:T(8,128)(2,1)S(1)}, bf16[5120,256]{1,0:T(8,128)(2,1)S(1)}, bf16[144,5120]{1,0:T(8,128)(2,1)S(1)}) custom-call(bf16[5120,128]{1,0:T(8,128)(2,1)S(1)} %copy-done.2, bf16[128,256]{1,0:T(8,128)(2,1)S(1)} %copy-done.4, f32[1,256]{1,0:T(1,128)S(1)} %bitcast.8), custom_call_target="tpu_custom_call" | custom-call | flops 4000000000 | bytes 8388608 | tf_op jit(solution)/shard_map/forward/pallas_call | solution.py:286
  19.6 0.0 copy-start.8
  19.6 1.5 %copy-done.8 = bf16[5120,256]{1,0:T(8,128)(2,1)} copy-done((bf16[5120,256]{1,0:T(8,128)(2,1)}, bf16[5120,256]{1,0:T(8,128)(2,1)S(1)}, u32[]{:S(2)}) %copy-start.8) | copy-done | bytes 2621464
  21.1 0.0 copy-start.10
  21.1 1.5 %copy-done.10 = bf16[5120,256]{1,0:T(8,128)(2,1)} copy-done((bf16[5120,256]{1,0:T(8,128)(2,1)}, bf16[5120,256]{1,0:T(8,128)(2,1)S(1)}, u32[]{:S(2)}) %copy-start.10) | copy-done | bytes 2621464
  22.7 0.0 collective-permute-start
  22.7 7.2 %collective-permute-start.1 = (bf16[768,256]{1,0:T(8,128)(2,1)}, bf16[768,256]{1,0:T(8,128)(2,1)S(1)}, u32[]{:S(2)}, u32[]{:S(2)}) collective-permute-start(bf16[768,256]{1,0:T(8,128)(2,1)} %get-tuple-element.34.low_far), channel_id=1, source_target_pairs={{0,252},{4,0},{8,4},{12,8},{16,12},{20,16},{24,20},{28,24},{32,28}... | collective-permute-start | bytes 1179656 | tf_op jit(solution)/shard_map/ppermute | solution.py:294
  29.9 0.0 copy-done.3
  29.9 0.0 copy-done.7
  29.9 11.4 %own.1 = (f32[9,160,128]{2,1,0:T(8,128)S(1)}, bf16[10,384,256]{2,1,0:T(8,128)(2,1)S(1)}, s16[10,128,128]{2,1,0:T(8,128)(2,1)S(1)}, s16[10,128,128]{2,1,0:T(8,128)(2,1)S(1)}) custom-call(bf16[1152,256]{1,0:T(8,128)(2,1)} %get-tuple-element.35.high_near, bf16[768,256]{1,0:T(8,128)(2,1)} %get-tuple-element.33.high_far, ...), custom_call_target="tpu_custom_call" | custom-call | flops 12000000000 | bytes 6291456 | tf_op jit(solution)/shard_map/own/pallas_call | solution.py:295
  41.2 0.0 copy-done.12
  41.2 0.9 copy-done.14
  42.1 0.0 collective-permute-done.2.below
  42.1 0.0 collective-permute-done.3.above
  42.1 1.1 %copy-done.15 = f32[9,160,128]{2,1,0:T(8,128)S(1)} copy-done((f32[9,160,128]{2,1,0:T(8,128)S(1)}, f32[9,160,128]{2,1,0:T(8,128)}, u32[]{:S(2)}) %copy-start.15) | copy-done | bytes 737304
  43.2 5.3 %near.1.before = f32[9,160,128]{2,1,0:T(8,128)S(1)} custom-call(bf16[1152,256]{1,0:T(8,128)(2,1)} %collective-permute-done.2.below, bf16[1152,256]{1,0:T(8,128)(2,1)} %collective-permute-done.3.above, bf16[10,384,256]{2,1,0:T(8,128)(2,1)S(1)} %get-tuple-element.38.weighted, s16[10,128,128]{2,1,0:T(8,128)(2,1)S(1)} %get-tuple-element.39.lane_ref, ...), custom_call_target="tpu_custom_call" | custom-call | flops 4000000000 | bytes 6291456 | tf_op jit(solution)/shard_map/near/pallas_call | solution.py:304
  48.6 0.0 collective-permute-done.below
  48.6 0.0 collective-permute-done.1.above
  48.6 0.0 copy-start.5
  48.6 0.0 copy-start.9
  48.6 0.0 copy-start.13
  48.6 1.4 %far.1 = (bf16[9,40,128]{2,1,0:T(8,128)(2,1)S(1)}, bf16[9,40,128]{2,1,0:T(8,128)(2,1)S(1)}, bf16[9,40,128]{2,1,0:T(8,128)(2,1)S(1)}, bf16[9,40,128]{2,1,0:T(8,128)(2,1)S(1)}) custom-call(s32[1]{0:T(128)} %bitcast.mode_index, bf16[768,256]{1,0:T(8,128)(2,1)S(1)} %collective-permute-done.below, bf16[768,256]{1,0:T(8,128)(2,1)S(1)} %collective-permute-done.1.above, ...), custom_call_target="tpu_custom_call" | custom-call | flops 1000000000 | bytes 5242880 | tf_op jit(solution)/shard_map/far/pallas_call | solution.py:309
  50.0 1.8 %collective-permute-start.4 = (bf16[9,40,128]{2,1,0:T(8,128)(2,1)S(1)}, bf16[9,40,128]{2,1,0:T(8,128)(2,1)S(1)}, u32[]{:S(2)}, u32[]{:S(2)}) collective-permute-start(bf16[9,40,128]{2,1,0:T(8,128)(2,1)S(1)} %get-tuple-element.43), channel_id=1, source_target_pairs={{0,1},{1,2},{2,3},{3,0},{4,5},{5,6},{6,7},{7,4},{8,9},{9,10},{10,1... | collective-permute-start | bytes 276488 | tf_op jit(solution)/shard_map/ppermute | solution.py:316
  51.8 1.1 %collective-permute-start.5 = (bf16[9,40,128]{2,1,0:T(8,128)(2,1)S(1)}, bf16[9,40,128]{2,1,0:T(8,128)(2,1)S(1)}, u32[]{:S(2)}, u32[]{:S(2)}) collective-permute-start(bf16[9,40,128]{2,1,0:T(8,128)(2,1)S(1)} %get-tuple-element.44), channel_id=1, source_target_pairs={{0,2},{1,3},{2,0},{3,1},{4,6},{5,7},{6,4},{7,5},{8,10},{9,11},{10,... | collective-permute-start | bytes 276488 | tf_op jit(solution)/shard_map/ppermute | solution.py:316
  53.0 0.0 collective-permute-start.6
  53.0 0.7 collective-permute-done.4.p1
  53.7 3.6 %collective-permute-done.5.p2 = bf16[9,40,128]{2,1,0:T(8,128)(2,1)S(1)} collective-permute-done((bf16[9,40,128]{2,1,0:T(8,128)(2,1)S(1)}, bf16[9,40,128]{2,1,0:T(8,128)(2,1)S(1)}, u32[]{:S(2)}, u32[]{:S(2)}) %collective-permute-start.5) | collective-permute-done | bytes 92192 | tf_op jit(solution)/shard_map/ppermute | solution.py:316
  57.2 0.6 collective-permute-done.6.p3
  57.8 0.0 copy-done.11
  57.9 0.0 copy-done.5
  57.9 0.0 copy-done.9
  57.9 0.0 copy-done.13
  57.9 2.1 %gradient.1 = (bf16[5120,256]{1,0:T(8,128)(2,1)S(1)}, f32[80,128]{1,0:T(8,128)S(1)}, f32[80,128]{1,0:T(8,128)S(1)}, f32[80,128]{1,0:T(8,128)S(1)}, f32[80,128]{1,0:T(8,128)S(1)}) custom-call(s32[1]{0:T(128)} %bitcast.mode_index, bf16[9,40,128]{2,1,0:T(8,128)(2,1)S(1)} %get-tuple-element.42.p0, bf16[9,40,128]{2,1,0:T(8,128)(2,1)S(1)} %collective-permute-done.4.p1, ...), custom_call_target="tpu_custom_call" | custom-call | flops 2000000000 | bytes 9437184 | tf_op jit(solution)/shard_map/gradient/pallas_call | solution.py:317
  60.0 0.1 collective-permute-start.7
  60.1 0.7 collective-permute-start.8
  60.7 0.4 collective-permute-start.9
  61.2 0.1 collective-permute-done.7
  61.3 1.7 %collective-permute-done.8 = f32[80,128]{1,0:T(8,128)S(1)} collective-permute-done((f32[80,128]{1,0:T(8,128)S(1)}, f32[80,128]{1,0:T(8,128)S(1)}, u32[]{:S(2)}, u32[]{:S(2)}) %collective-permute-start.8) | collective-permute-done | bytes 40992 | tf_op jit(solution)/shard_map/ppermute | solution.py:332
  63.0 1.3 %collective-permute-done.9 = f32[80,128]{1,0:T(8,128)S(1)} collective-permute-done((f32[80,128]{1,0:T(8,128)S(1)}, f32[80,128]{1,0:T(8,128)S(1)}, u32[]{:S(2)}, u32[]{:S(2)}) %collective-permute-start.9) | collective-permute-done | bytes 40992 | tf_op jit(solution)/shard_map/ppermute | solution.py:332
  64.4 11.8 %all_to_all.10 = bf16[8,80,128]{2,1,0:T(8,128)(2,1)S(1)} all-to-all(bf16[8,80,128]{2,1,0:T(8,128)(2,1)S(1)} %broadcast_in_dim.4), channel_id=1, replica_groups={{0,4,8,12,16,20,24,28},{32,36,40,44,48,52,56,60},{64,68,72,76,80,84,88,..., dimensions={0} | all-to-all | bytes 327680 | tf_op jit(solution)/shard_map/all_to_all | solution.py:337
  76.2 9.6 %all_to_all.11 = bf16[8,80,128]{2,1,0:T(8,128)(2,1)S(1)} all-to-all(bf16[8,80,128]{2,1,0:T(8,128)(2,1)S(1)} %broadcast_in_dim.5), channel_id=1, replica_groups={{0,32,64,96,128,160,192,224},{4,36,68,100,132,164,196,228},{8,40,72,104..., dimensions={0} | all-to-all | bytes 327680 | tf_op jit(solution)/shard_map/all_to_all | solution.py:337
  85.8 3.2 %collective-permute-start.10 = (f32[80,128]{1,0:T(8,128)S(1)}, f32[80,128]{1,0:T(8,128)S(1)}, u32[]{:S(2)}, u32[]{:S(2)}) collective-permute-start(f32[80,128]{1,0:T(8,128)S(1)} %convert_reduce_fusion.c0), channel_id=1, source_target_pairs={{0,1},{1,2},{2,3},{3,0},{4,5},{5,6},{6,7},{7,4},{8,9},{9,10},{10,1... | collective-permute-start | bytes 122888 | tf_op jit(solution)/shard_map/ppermute | solution.py:339
  89.0 0.7 collective-permute-start.11
  89.7 0.0 collective-permute-start.12
  89.7 3.0 %features.3 = bf16[5120,128]{1,0:T(8,128)(2,1)} custom-call(bf16[5120,256]{1,0:T(8,128)(2,1)S(1)} %get-tuple-element.48.pre_cot, bf16[128,256]{1,0:T(8,128)(2,1)S(1)} %copy-done.4), custom_call_target="tpu_custom_call" | custom-call | flops 2000000000 | bytes 5242880 | tf_op jit(solution)/shard_map/features/pallas_call | solution.py:324
  92.7 0.0 collective-permute-done.10.c1
  92.7 0.0 collective-permute-done.11.c2
  92.7 0.4 collective-permute-done.12.c3
  93.1 0.9 finish.1
  (9 shorter events, 0.1 us)
Async XLA Ops:
  0.6 15.1 %copy-start.6 = (f32[256]{0:T(256)S(1)}, f32[256]{0:T(256)}, u32[]{:S(2)}) copy-start(f32[256]{0:T(256)} %param.14) | copy-start | bytes 3076
  0.6 1.6 %copy-start = (bf16[1280,3,256]{2,0,1:T(8,128)(2,1)S(1)}, bf16[1280,3,256]{2,0,1:T(8,128)(2,1)}, u32[]{:S(2)}) copy-start(bf16[1280,3,256]{2,0,1:T(8,128)(2,1)} %param.8) | copy-start | bytes 5898244
  2.2 0.7 copy-start.1
  2.9 12.9 %copy-start.2 = (bf16[5120,128]{1,0:T(8,128)(2,1)S(1)}, bf16[5120,128]{1,0:T(8,128)(2,1)}, u32[]{:S(2)}) copy-start(bf16[5120,128]{1,0:T(8,128)(2,1)} %features.2) | copy-start | bytes 3932164
  2.9 12.9 %copy-start.4 = (bf16[128,256]{1,0:T(8,128)(2,1)S(1)}, bf16[128,256]{1,0:T(8,128)(2,1)}, u32[]{:S(2)}) copy-start(bf16[128,256]{1,0:T(8,128)(2,1)} %w_in.3) | copy-start | bytes 196612
  4.4 37.7 %collective-permute-start.2 = (bf16[1152,256]{1,0:T(8,128)(2,1)}, bf16[1152,256]{1,0:T(8,128)(2,1)}, u32[]{:S(2)}, u32[]{:S(2)}) collective-permute-start(bf16[1152,256]{1,0:T(8,128)(2,1)} %get-tuple-element.35.high_near), channel_id=1, source_target_pairs={{0,4},{4,8},{8,12},{12,16},{16,20},{20,24},{24,28},{28,32},{32,36}... | collective-permute-start | bytes 1769480 | tf_op jit(solution)/shard_map/ppermute | solution.py:280
  6.9 35.2 %collective-permute-start.3 = (bf16[1152,256]{1,0:T(8,128)(2,1)}, bf16[1152,256]{1,0:T(8,128)(2,1)}, u32[]{:S(2)}, u32[]{:S(2)}) collective-permute-start(bf16[1152,256]{1,0:T(8,128)(2,1)} %get-tuple-element.36.low_near), channel_id=1, source_target_pairs={{0,252},{4,0},{8,4},{12,8},{16,12},{20,16},{24,20},{28,24},{32,28}... | collective-permute-start | bytes 1769480 | tf_op jit(solution)/shard_map/ppermute | solution.py:281
  15.8 14.1 %copy-start.3 = (s32[1280,16]{0,1:T(8,128)S(1)}, s32[1280,16]{0,1:T(8,128)}, u32[]{:S(2)}) copy-start(s32[1280,16]{0,1:T(8,128)} %param.11) | copy-start | bytes 245764
  15.8 14.1 %copy-start.7 = (f32[256]{0:T(256)S(1)}, f32[256]{0:T(256)}, u32[]{:S(2)}) copy-start(f32[256]{0:T(256)} %param.10) | copy-start | bytes 3076
  19.6 1.5 %copy-start.8 = (bf16[5120,256]{1,0:T(8,128)(2,1)}, bf16[5120,256]{1,0:T(8,128)(2,1)S(1)}, u32[]{:S(2)}) copy-start(bf16[5120,256]{1,0:T(8,128)(2,1)S(1)} %get-tuple-element.46.hidden) | copy-start | bytes 7864324
  21.1 1.5 %copy-start.10 = (bf16[5120,256]{1,0:T(8,128)(2,1)}, bf16[5120,256]{1,0:T(8,128)(2,1)S(1)}, u32[]{:S(2)}) copy-start(bf16[5120,256]{1,0:T(8,128)(2,1)S(1)} %get-tuple-element.47.slope) | copy-start | bytes 7864324
  22.7 18.6 %copy-start.12 = (bf16[144,5120]{1,0:T(8,128)(2,1)}, bf16[144,5120]{1,0:T(8,128)(2,1)S(1)}, u32[]{:S(2)}) copy-start(bf16[144,5120]{1,0:T(8,128)(2,1)S(1)} %get-tuple-element.37._after.turned) | copy-start | bytes 4423684
  22.7 25.9 %collective-permute-start = (bf16[768,256]{1,0:T(8,128)(2,1)}, bf16[768,256]{1,0:T(8,128)(2,1)S(1)}, u32[]{:S(2)}, u32[]{:S(2)}) collective-permute-start(bf16[768,256]{1,0:T(8,128)(2,1)} %get-tuple-element.33.high_far), channel_id=1, source_target_pairs={{0,4},{4,8},{8,12},{12,16},{16,20},{20,24},{24,28},{28,32},{32,36}... | collective-permute-start | bytes 1179656 | tf_op jit(solution)/shard_map/ppermute | solution.py:293
  22.7 25.9 %collective-permute-start.1 = (bf16[768,256]{1,0:T(8,128)(2,1)}, bf16[768,256]{1,0:T(8,128)(2,1)S(1)}, u32[]{:S(2)}, u32[]{:S(2)}) collective-permute-start(bf16[768,256]{1,0:T(8,128)(2,1)} %get-tuple-element.34.low_far), channel_id=1, source_target_pairs={{0,252},{4,0},{8,4},{12,8},{16,12},{20,16},{24,20},{28,24},{32,28}... | collective-permute-start | bytes 1179656 | tf_op jit(solution)/shard_map/ppermute | solution.py:294
  41.2 0.9 copy-start.14
  42.1 1.1 %copy-start.15 = (f32[9,160,128]{2,1,0:T(8,128)S(1)}, f32[9,160,128]{2,1,0:T(8,128)}, u32[]{:S(2)}) copy-start(f32[9,160,128]{2,1,0:T(8,128)} %copy-done.14) | copy-start | bytes 2211844
  43.2 14.6 %copy-start.11 = (bf16[5120,256]{1,0:T(8,128)(2,1)S(1)}, bf16[5120,256]{1,0:T(8,128)(2,1)}, u32[]{:S(2)}) copy-start(bf16[5120,256]{1,0:T(8,128)(2,1)} %copy-done.10) | copy-start | bytes 7864324
  48.6 9.2 %copy-start.5 = (bf16[9,256]{1,0:T(8,128)(2,1)S(1)}, bf16[9,256]{1,0:T(8,128)(2,1)}, u32[]{:S(2)}) copy-start(bf16[9,256]{1,0:T(8,128)(2,1)} %w_out.1) | copy-start | bytes 13828
  48.6 9.2 %copy-start.9 = (bf16[5120,256]{1,0:T(8,128)(2,1)S(1)}, bf16[5120,256]{1,0:T(8,128)(2,1)}, u32[]{:S(2)}) copy-start(bf16[5120,256]{1,0:T(8,128)(2,1)} %copy-done.8) | copy-start | bytes 7864324
  48.6 9.2 %copy-start.13 = (bf16[144,5120]{1,0:T(8,128)(2,1)S(1)}, bf16[144,5120]{1,0:T(8,128)(2,1)}, u32[]{:S(2)}) copy-start(bf16[144,5120]{1,0:T(8,128)(2,1)} %copy-done.12) | copy-start | bytes 4423684
  50.0 3.6 %collective-permute-start.4 = (bf16[9,40,128]{2,1,0:T(8,128)(2,1)S(1)}, bf16[9,40,128]{2,1,0:T(8,128)(2,1)S(1)}, u32[]{:S(2)}, u32[]{:S(2)}) collective-permute-start(bf16[9,40,128]{2,1,0:T(8,128)(2,1)S(1)} %get-tuple-element.43), channel_id=1, source_target_pairs={{0,1},{1,2},{2,3},{3,0},{4,5},{5,6},{6,7},{7,4},{8,9},{9,10},{10,1... | collective-permute-start | bytes 276488 | tf_op jit(solution)/shard_map/ppermute | solution.py:316
  51.8 5.4 %collective-permute-start.5 = (bf16[9,40,128]{2,1,0:T(8,128)(2,1)S(1)}, bf16[9,40,128]{2,1,0:T(8,128)(2,1)S(1)}, u32[]{:S(2)}, u32[]{:S(2)}) collective-permute-start(bf16[9,40,128]{2,1,0:T(8,128)(2,1)S(1)} %get-tuple-element.44), channel_id=1, source_target_pairs={{0,2},{1,3},{2,0},{3,1},{4,6},{5,7},{6,4},{7,5},{8,10},{9,11},{10,... | collective-permute-start | bytes 276488 | tf_op jit(solution)/shard_map/ppermute | solution.py:316
  53.0 4.9 %collective-permute-start.6 = (bf16[9,40,128]{2,1,0:T(8,128)(2,1)S(1)}, bf16[9,40,128]{2,1,0:T(8,128)(2,1)S(1)}, u32[]{:S(2)}, u32[]{:S(2)}) collective-permute-start(bf16[9,40,128]{2,1,0:T(8,128)(2,1)S(1)} %get-tuple-element.45), channel_id=1, source_target_pairs={{0,3},{1,0},{2,1},{3,2},{4,7},{5,4},{6,5},{7,6},{8,11},{9,8},{10,9... | collective-permute-start | bytes 276488 | tf_op jit(solution)/shard_map/ppermute | solution.py:316
  60.0 1.3 %collective-permute-start.7 = (f32[80,128]{1,0:T(8,128)S(1)}, f32[80,128]{1,0:T(8,128)S(1)}, u32[]{:S(2)}, u32[]{:S(2)}) collective-permute-start(f32[80,128]{1,0:T(8,128)S(1)} %get-tuple-element.50), channel_id=1, source_target_pairs={{0,1},{1,2},{2,3},{3,0},{4,5},{5,6},{6,7},{7,4},{8,9},{9,10},{10,1... | collective-permute-start | bytes 122888 | tf_op jit(solution)/shard_map/ppermute | solution.py:332
  60.1 2.9 %collective-permute-start.8 = (f32[80,128]{1,0:T(8,128)S(1)}, f32[80,128]{1,0:T(8,128)S(1)}, u32[]{:S(2)}, u32[]{:S(2)}) collective-permute-start(f32[80,128]{1,0:T(8,128)S(1)} %get-tuple-element.51), channel_id=1, source_target_pairs={{0,2},{1,3},{2,0},{3,1},{4,6},{5,7},{6,4},{7,5},{8,10},{9,11},{10,... | collective-permute-start | bytes 122888 | tf_op jit(solution)/shard_map/ppermute | solution.py:332
  60.7 3.6 %collective-permute-start.9 = (f32[80,128]{1,0:T(8,128)S(1)}, f32[80,128]{1,0:T(8,128)S(1)}, u32[]{:S(2)}, u32[]{:S(2)}) collective-permute-start(f32[80,128]{1,0:T(8,128)S(1)} %get-tuple-element.52), channel_id=1, source_target_pairs={{0,3},{1,0},{2,1},{3,2},{4,7},{5,4},{6,5},{7,6},{8,11},{9,8},{10,9... | collective-permute-start | bytes 122888 | tf_op jit(solution)/shard_map/ppermute | solution.py:332
  85.8 6.9 %collective-permute-start.10 = (f32[80,128]{1,0:T(8,128)S(1)}, f32[80,128]{1,0:T(8,128)S(1)}, u32[]{:S(2)}, u32[]{:S(2)}) collective-permute-start(f32[80,128]{1,0:T(8,128)S(1)} %convert_reduce_fusion.c0), channel_id=1, source_target_pairs={{0,1},{1,2},{2,3},{3,0},{4,5},{5,6},{6,7},{7,4},{8,9},{9,10},{10,1... | collective-permute-start | bytes 122888 | tf_op jit(solution)/shard_map/ppermute | solution.py:339
  89.0 3.8 %collective-permute-start.11 = (f32[80,128]{1,0:T(8,128)S(1)}, f32[80,128]{1,0:T(8,128)S(1)}, u32[]{:S(2)}, u32[]{:S(2)}) collective-permute-start(f32[80,128]{1,0:T(8,128)S(1)} %convert_reduce_fusion.c0), channel_id=1, source_target_pairs={{0,2},{1,3},{2,0},{3,1},{4,6},{5,7},{6,4},{7,5},{8,10},{9,11},{10,... | collective-permute-start | bytes 122888 | tf_op jit(solution)/shard_map/ppermute | solution.py:339
  89.7 3.4 %collective-permute-start.12 = (f32[80,128]{1,0:T(8,128)S(1)}, f32[80,128]{1,0:T(8,128)S(1)}, u32[]{:S(2)}, u32[]{:S(2)}) collective-permute-start(f32[80,128]{1,0:T(8,128)S(1)} %convert_reduce_fusion.c0), channel_id=1, source_target_pairs={{0,3},{1,0},{2,1},{3,2},{4,7},{5,4},{6,5},{7,6},{8,11},{9,8},{10,9... | collective-permute-start | bytes 122888 | tf_op jit(solution)/shard_map/ppermute | solution.py:339

commit v6 on v4

--- a/solution.py
+++ b/solution.py
@@ -19,7 +19,7 @@
 F32, BF16 = jnp.float32, jnp.bfloat16
 VMEM = pl.BlockSpec(memory_space=pltpu.VMEM)
 SMEM = pl.BlockSpec(memory_space=pltpu.SMEM)
-PARAMS = pltpu.CompilerParams(vmem_limit_bytes=40 << 20)
+PARAMS = pltpu.CompilerParams(vmem_limit_bytes=24 << 20)
 
 
 def nt_dot(x, y):
@@ -33,33 +33,22 @@
 STRIP = 3 * T
 
 
-NEAR = 3
-
-
-def scale_kernel(eig, species, high_near, high_far, low_near, low_far):
-    order = [blk for t in range(REACH) for blk in (BLOCKS - 1 - t, t)]
-    for blk in order:
-        rows = slice(blk * T, (blk + 1) * T)
-        kind = species[rows].reshape(1, T)
-        mass = jnp.full(kind.shape, MASS_TABLE[3], F32)
-        for k in range(3):
-            mass = jnp.where(kind == k, MASS_TABLE[k], mass)
-        inv = jnp.broadcast_to(lax.rsqrt(mass), (T, T)).T
-        inv = jnp.concatenate([inv, inv], axis=1)
-        out, tile = place_of(blk, high_near, high_far, low_near, low_far)
-        for a in range(3):
-            at = tile * STRIP + a * T
-            out[at:at + T, :] = (eig[a, rows, :].astype(F32) * inv).astype(BF16)
-
-
-def place_of(blk, high_near, high_far, low_near, low_far):
-    if blk < NEAR:
-        return low_near, blk
-    if blk < REACH:
-        return low_far, blk - NEAR
-    if blk < BLOCKS - NEAR:
-        return high_far, blk - REACH
-    return high_near, blk - (BLOCKS - NEAR)
+def scale_kernel(eig, species, high, low):
+    def half(base, out):
+        for blk in range(REACH):
+            rows = slice(base + blk * T, base + (blk + 1) * T)
+            kind = species[rows].reshape(1, T)
+            mass = jnp.full(kind.shape, MASS_TABLE[3], F32)
+            for k in range(3):
+                mass = jnp.where(kind == k, MASS_TABLE[k], mass)
+            inv = jnp.broadcast_to(lax.rsqrt(mass), (T, T)).T
+            inv = jnp.concatenate([inv, inv], axis=1)
+            for a in range(3):
+                at = blk * STRIP + a * T
+                out[at:at + T, :] = (eig[a, rows, :].astype(F32) * inv).astype(BF16)
+
+    half(RIM, high)
+    half(0, low)
 
 
 def fold_matrix():
@@ -123,7 +112,7 @@
         turn(0, 0)
 
 
-def own_kernel(high_near, high_far, low_near, low_far, mode_cot, nbr_t, out, weighted, lane_ref, tile_ref, stack, dense0, dense1, terms):
+def own_kernel(high, low, mode_cot, nbr_t, out, weighted, lane_ref, tile_ref, stack, dense0, dense1, terms):
     row = lax.broadcasted_iota(jnp.int32, (T, T), 0)
     col = lax.broadcasted_iota(jnp.int32, (T, T), 1)
     diagonal = (row % 8) == (col // 16)
@@ -134,8 +123,8 @@
         live = diagonal & (n < ATOMS + 2 * RIM)
         tile_ref[blk] = jnp.where(live, n >> 7, -1).astype(jnp.int16)
         lane_ref[blk] = (n & (T - 1)).astype(jnp.int16)
-        src, tile = place_of(blk, high_near, high_far, low_near, low_far)
-        s = src[tile * STRIP:(tile + 1) * STRIP, :]
+        src = low if blk < REACH else high
+        s = src[blk % REACH * STRIP:(blk % REACH + 1) * STRIP, :]
         stack[blk * STRIP:(blk + 1) * STRIP, :] = s
         weighted[blk] = (s.astype(F32) * cot).astype(BF16)
     jobs = []
@@ -150,14 +139,10 @@
                 fold, terms[c, h * 2 * T:(h + 1) * 2 * T, :], preferred_element_type=F32)
 
 
-def near_kernel(below, above, weighted, lane_ref, tile_ref, own, total, dense0, dense1, terms):
-    skip = REACH - NEAR
-    jobs = []
-    for i in reversed(range(REACH)):
-        first = max(i, skip)
-        jobs.append((i, below, (first - skip) * STRIP, first, REACH - first))
-    for i in reversed(range(REACH, BLOCKS)):
-        jobs.append((i, above, 0, 3 * REACH, min(i - REACH + 1, NEAR)))
+def halo_kernel(mode_index, below, above, weighted, lane_ref, tile_ref, own, _after,
+                out0, out1, out2, out3, dense0, dense1, terms, total):
+    jobs = [(i, below, i * STRIP, i, REACH - i) for i in reversed(range(REACH))]
+    jobs += [(i, above, 0, 3 * REACH, i - REACH + 1) for i in reversed(range(REACH, BLOCKS))]
     pipeline(jobs, weighted, lane_ref, tile_ref, (dense0, dense1), terms, False)
     fold = fold_matrix()
     for h in range(BLOCKS // 2):
@@ -165,21 +150,6 @@
             at = slice(h * 32, (h + 1) * 32)
             total[c, at, :] = own[c, at, :] + jnp.dot(
                 fold, terms[c, h * 2 * T:(h + 1) * 2 * T, :], preferred_element_type=F32)
-
-
-def far_kernel(mode_index, below, above, weighted, lane_ref, tile_ref, before, _after,
-               out0, out1, out2, out3, dense0, dense1, terms, total):
-    skip = REACH - NEAR
-    jobs = [(i, below, i * STRIP, i, skip - i) for i in reversed(range(skip))]
-    jobs += [(i, above, 0, 3 * REACH + NEAR, i - REACH - NEAR + 1) for i in range(REACH + NEAR, BLOCKS)]
-    pipeline(jobs, weighted, lane_ref, tile_ref, (dense0, dense1), terms, False)
-    total[...] = before[...]
-    fold = fold_matrix()
-    for h in (0, BLOCKS // 2 - 1):
-        for c in range(9):
-            at = slice(h * 32, (h + 1) * 32)
-            total[c, at, :] += jnp.dot(
-                fold, terms[c, h * 2 * T:(h + 1) * 2 * T, :], preferred_element_type=F32)
     m = mode_index[0]
     for k, out in enumerate((out0, out1, out2, out3)):
         q = lax.rem(m + k, 4)
@@ -190,7 +160,7 @@
 EXT = 144
 
 
-def forward_kernel(features, w_in, b_in, _after, hidden, slope, turned):
+def forward_kernel(features, w_in, b_in, hidden, slope, turned):
     x = features[...]
     pre = jnp.dot(x, w_in[...], preferred_element_type=F32) + b_in[...]
     sig = 1.0 / (1.0 + jnp.exp(-pre))
@@ -268,51 +238,39 @@
 def shards(eigvec, species, mode_cot, neighbours, pair_features, w_in, b_in, w_out):
     eig = jnp.transpose(eigvec, (1, 0, 2))
     m = lax.axis_index("mode").astype(jnp.int32).reshape(1)
-    near, far = NEAR * STRIP, (REACH - NEAR) * STRIP
-    anywhere = pl.BlockSpec(memory_space=pl.ANY)
-    halves = pl.pallas_call(
-        scale_kernel, out_shape=[shape((near, 256), BF16), shape((far, 256), BF16)] * 2,
-        in_specs=[VMEM] * 2, out_specs=[VMEM] * 4,
-        compiler_params=PARAMS, cost_estimate=cost(1 << 20, 4 << 20), name="scale",
+    high, low = pl.pallas_call(
+        scale_kernel, out_shape=[shape((REACH * STRIP, 256), BF16)] * 2,
+        in_specs=[VMEM] * 2, out_specs=[VMEM] * 2, compiler_params=PARAMS,
+        cost_estimate=cost(1 << 20, 4 << 20), name="scale",
     )(eig, species)
-    high_near, high_far, low_near, low_far = halves
-    up, down = ring("slab", 1), ring("slab", lax.axis_size("slab") - 1)
-    below_near = lax.ppermute(high_near, "slab", up)
-    above_near = lax.ppermute(low_near, "slab", down)
+    below = lax.ppermute(high, "slab", ring("slab", 1))
+    above = lax.ppermute(low, "slab", ring("slab", lax.axis_size("slab") - 1))
     own, weighted, lane, tile = pl.pallas_call(
         own_kernel,
         out_shape=[shape((9, GROUPS, T)), shape((BLOCKS, 3 * T, 256), BF16),
                    shape((BLOCKS, T, T), jnp.int16), shape((BLOCKS, T, T), jnp.int16)],
-        in_specs=[VMEM] * 6, out_specs=[VMEM] * 4,
+        in_specs=[VMEM] * 4, out_specs=[VMEM] * 4,
         scratch_shapes=[pltpu.VMEM((BLOCKS * STRIP, 256), BF16)]
         + [pltpu.VMEM((STRIP, BLOCKS * STRIP), BF16)] * 2 + [pltpu.VMEM((9, ATOMS, T), BF16)],
         compiler_params=PARAMS, cost_estimate=cost(12_000_000_000, 6 << 20), name="own",
-    )(*halves, mode_cot.reshape(1, 256), neighbours.T)
-    high_far, low_far, own = lax.optimization_barrier((high_far, low_far, own))
-    below_far = lax.ppermute(high_far, "slab", up)
-    above_far = lax.ppermute(low_far, "slab", down)
+    )(high, low, mode_cot.reshape(1, 256), neighbours.T)
     slots = pair_features.shape[0]
     steps = slots // CHUNK
     rows_spec = lambda width: pl.BlockSpec((CHUNK, width), lambda s: (s, 0))
     full = lambda *dims: pl.BlockSpec(dims, lambda s: (0,) * len(dims))
     hidden, slope, turned = pl.pallas_call(
         forward_kernel, out_shape=[shape((slots, 256), BF16)] * 2 + [shape((EXT, slots), BF16)], grid=(steps,),
-        in_specs=[rows_spec(128), full(128, 256), full(1, 256), anywhere],
+        in_specs=[rows_spec(128), full(128, 256), full(1, 256)],
         out_specs=[rows_spec(256)] * 2 + [pl.BlockSpec((EXT, CHUNK), lambda s: (0, s))],
         compiler_params=PARAMS, cost_estimate=cost(4_000_000_000, 8 << 20), name="forward",
-    )(pair_features, w_in, b_in.reshape(1, 256), own)
-    total = pl.pallas_call(
-        near_kernel, out_shape=shape((9, GROUPS, T)), in_specs=[VMEM] * 6, out_specs=VMEM,
-        scratch_shapes=[pltpu.VMEM((STRIP, NEAR * STRIP), BF16)] * 2 + [pltpu.VMEM((9, ATOMS, T), BF16)],
-        compiler_params=PARAMS, cost_estimate=cost(4_000_000_000, 6 << 20), name="near",
-    )(below_near, above_near, weighted, lane, tile, own)
+    )(pair_features, w_in, b_in.reshape(1, 256))
     parts = pl.pallas_call(
-        far_kernel, out_shape=[shape((9, QUARTER, T), BF16)] * 4,
-        in_specs=[SMEM] + [VMEM] * 6 + [anywhere], out_specs=[VMEM] * 4,
-        scratch_shapes=[pltpu.VMEM((STRIP, (REACH - NEAR) * STRIP), BF16)] * 2
+        halo_kernel, out_shape=[shape((9, QUARTER, T), BF16)] * 4,
+        in_specs=[SMEM] + [VMEM] * 6 + [pl.BlockSpec(memory_space=pl.ANY)], out_specs=[VMEM] * 4,
+        scratch_shapes=[pltpu.VMEM((STRIP, REACH * STRIP), BF16)] * 2
         + [pltpu.VMEM((9, ATOMS, T), BF16), pltpu.VMEM((9, GROUPS, T), F32)],
-        compiler_params=PARAMS, cost_estimate=cost(1_000_000_000, 5 << 20), name="far",
-    )(m, below_far, above_far, weighted, lane, tile, total, turned)
+        compiler_params=PARAMS, cost_estimate=cost(5_000_000_000, 6 << 20), name="halo",
+    )(m, below, above, weighted, lane, tile, own, turned)
     parts = [parts[0]] + [lax.ppermute(parts[k], "mode", ring("mode", k)) for k in (1, 2, 3)]
     pre_cot, *sums = pl.pallas_call(
         gradient_kernel,
@@ -330,7 +288,6 @@
     share = sums[0]
     for k in (1, 2, 3):
         share = share + lax.ppermute(sums[k], "mode", ring("mode", k))
-    share, features_grad = lax.optimization_barrier((share, features_grad))
     line = [[g * 8 + k for k in range(8)] for g in range(8)]
     plane = [[k * 8 + g for k in range(8)] for g in range(8)]
     for groups in (line, plane):

time: 98 us -> 91.7 us (0.936)
  starting transfers between devices: 27.6 us -> 19.9 us
  local copies, waits for them, and re-layouts: 9.88 us -> 2.31 us
  blocking collectives: 20.4 us -> 26.3 us
  waiting for transfers between devices: 8.43 us -> 13.9 us
  Pallas kernels: 30.5 us -> 28.3 us
    unnamed x36 -> x16, local copies, waits for them, and re-layouts: 9.83 us -> 2.27 us
    ppermute x4 -> x2, starting transfers between devices: 18.5 us -> 11.3 us  [the longest x1 8.85 us: shards(): above = lax.ppermute(low, 'slab', ring('slab', lax.axis_size('slab') - 1))]
    ppermute x4 -> x2, waiting for transfers between devices: 0.01 us -> 5.91 us  [the longest x1 5.91 us: shards(): below = lax.ppermute(high, 'slab', ring('slab', 1))]
    all_to_all x2, blocking collectives: 20.4 us -> 26.3 us  [shards(): lax.all_to_all(spread, 'slab', 0, 0, axis_index_groups=groups, tiled=True)]
    ppermute x3, waiting for transfers between devices: 3.38 us -> 0.01 us  [shards(): lax.ppermute(share, 'mode', ring('mode', k))]
    ppermute x3, waiting for transfers between devices: 0.14 us -> 3.13 us  [shards(): share = share + lax.ppermute(sums[k], 'mode', ring('mode', k))]
    pallas_call x3 -> x2, Pallas kernels: 9.23 us -> 6.61 us  [the longest x1 5.06 us: shards(): pl.pallas_call(halo_kernel, out_shape=[shape((9, QUARTER, T), BF16)] * 4,...]
  transfers between devices with their start and end apart: 13 -> 11, of which waited for: 7 -> 7; matrix products, arithmetic and copies ran while one was open for 0% -> 0% of each run, Pallas kernels for 24% -> 20%
where the time goes in v6:
time: 91.7 us; the launch traced here: 91.5 us
  Pallas kernels  28.3 us (31%)
  blocking collectives  26.3 us (29%)
  starting transfers between devices  19.9 us (22%)
  waiting for transfers between devices  13.9 us (15%)
  local copies, waits for them, and re-layouts  2.31 us (3%)
    all_to_all x2, blocking collectives, shards(): lax.all_to_all(spread, 'slab', 0, 0, axis_index_groups=groups, tiled=True)  26.3 us
    pallas_call x1, Pallas kernels, shards(): pl.pallas_call(own_kernel, out_shape=[shape((9, GROUPS, T)), shape((BLOCK...  11.7 us
    ppermute x1, starting transfers between devices, shards(): above = lax.ppermute(low, 'slab', ring('slab', lax.axis_size('slab') - 1))  8.85 us
    ppermute x1, waiting for transfers between devices, shards(): below = lax.ppermute(high, 'slab', ring('slab', 1))  5.91 us
    pallas_call x1, Pallas kernels, shards(): pl.pallas_call(halo_kernel, out_shape=[shape((9, QUARTER, T), BF16)] * 4,...  5.06 us
    ppermute x3, waiting for transfers between devices, shards(): lax.ppermute(parts[k], 'mode', ring('mode', k))  4.89 us
    ppermute x3, starting transfers between devices, shards(): lax.ppermute(share, 'mode', ring('mode', k))  4.68 us
    pallas_call x1, Pallas kernels, shards(): pl.pallas_call(forward_kernel, out_shape=[shape((slots, 256), BF16)] * 2...  4 us
  transfers between devices with their start and end apart: 11, of which 7 were waited for; matrix products, arithmetic and copies ran while one was open for 0% of the time, Pallas kernels for 20%

profile of v6, /device:TPU:1, one launch (start us, length us, event | category | flops | bytes accessed | tf_op | source)
XLA Modules:
  0.0 91.5 jit_solution(9543483268375701237)
XLA Ops:
  0.6 0.0 copy-start.6
  0.6 0.0 copy-start
  0.7 1.5 %copy-done = bf16[1280,3,256]{2,0,1:T(8,128)(2,1)S(1)} copy-done((bf16[1280,3,256]{2,0,1:T(8,128)(2,1)S(1)}, bf16[1280,3,256]{2,0,1:T(8,128)(2,1)}, u32[]{:S(2)}) %copy-start) | copy-done | bytes 1966104
  2.2 0.0 copy-start.1
  2.2 0.7 copy-done.1
  2.9 0.0 copy-start.2
  2.9 0.0 copy-start.4
  2.9 1.6 %scale.1 = (bf16[1920,256]{1,0:T(8,128)(2,1)}, bf16[1920,256]{1,0:T(8,128)(2,1)}) custom-call(bf16[3,1280,256]{2,1,0:T(8,128)(2,1)S(1)} %bitcast.6, s32[1280]{0:T(1024)S(1)} %copy-done.1), custom_call_target="tpu_custom_call" | custom-call | flops 1048576 | bytes 4194304 | tf_op jit(solution)/shard_map/scale/pallas_call | solution.py:241
  4.5 2.5 %collective-permute-start = (bf16[1920,256]{1,0:T(8,128)(2,1)}, bf16[1920,256]{1,0:T(8,128)(2,1)S(1)}, u32[]{:S(2)}, u32[]{:S(2)}) collective-permute-start(bf16[1920,256]{1,0:T(8,128)(2,1)} %get-tuple-element.25.high), channel_id=1, source_target_pairs={{0,4},{4,8},{8,12},{12,16},{16,20},{20,24},{24,28},{28,32},{32,36}... | collective-permute-start | bytes 2949128 | tf_op jit(solution)/shard_map/ppermute | solution.py:246
  6.9 8.9 %collective-permute-start.1 = (bf16[1920,256]{1,0:T(8,128)(2,1)}, bf16[1920,256]{1,0:T(8,128)(2,1)S(1)}, u32[]{:S(2)}, u32[]{:S(2)}) collective-permute-start(bf16[1920,256]{1,0:T(8,128)(2,1)} %get-tuple-element.26.low), channel_id=1, source_target_pairs={{0,252},{4,0},{8,4},{12,8},{16,12},{20,16},{24,20},{28,24},{32,28}... | collective-permute-start | bytes 2949128 | tf_op jit(solution)/shard_map/ppermute | solution.py:247
  15.8 0.0 copy-done.6
  15.8 0.0 copy-done.2
  15.8 0.0 copy-done.4
  15.8 0.0 copy-start.3
  15.8 0.0 copy-start.7
  15.8 4.0 %forward.1 = (bf16[5120,256]{1,0:T(8,128)(2,1)S(1)}, bf16[5120,256]{1,0:T(8,128)(2,1)S(1)}, bf16[144,5120]{1,0:T(8,128)(2,1)S(1)}) custom-call(bf16[5120,128]{1,0:T(8,128)(2,1)S(1)} %copy-done.2, bf16[128,256]{1,0:T(8,128)(2,1)S(1)} %copy-done.4, f32[1,256]{1,0:T(1,128)S(1)} %bitcast.8), custom_call_target="tpu_custom_call" | custom-call | flops 4000000000 | bytes 8388608 | tf_op jit(solution)/shard_map/forward/pallas_call | solution.py:261
  19.8 0.0 copy-done.3
  19.8 0.0 copy-done.7
  19.8 11.7 %own.1 = (f32[9,160,128]{2,1,0:T(8,128)S(1)}, bf16[10,384,256]{2,1,0:T(8,128)(2,1)S(1)}, s16[10,128,128]{2,1,0:T(8,128)(2,1)S(1)}, s16[10,128,128]{2,1,0:T(8,128)(2,1)S(1)}) custom-call(bf16[1920,256]{1,0:T(8,128)(2,1)} %get-tuple-element.25.high, bf16[1920,256]{1,0:T(8,128)(2,1)} %get-tuple-element.26.low, f32[1,256]{1,0:T(1,128)S(1)} %bitcast.9, ...), custom_call_target="tpu_custom_call" | custom-call | flops 12000000000 | bytes 6291456 | tf_op jit(solution)/shard_map/own/pallas_call | solution.py:248
  31.5 5.9 %collective-permute-done.below = bf16[1920,256]{1,0:T(8,128)(2,1)S(1)} collective-permute-done((bf16[1920,256]{1,0:T(8,128)(2,1)}, bf16[1920,256]{1,0:T(8,128)(2,1)S(1)}, u32[]{:S(2)}, u32[]{:S(2)}) %collective-permute-start) | collective-permute-done | bytes 983072 | tf_op jit(solution)/shard_map/ppermute | solution.py:246
  37.5 0.0 collective-permute-done.1.above
  37.5 0.0 copy-start.5
  37.5 5.1 %halo.1 = (bf16[9,40,128]{2,1,0:T(8,128)(2,1)S(1)}, bf16[9,40,128]{2,1,0:T(8,128)(2,1)S(1)}, bf16[9,40,128]{2,1,0:T(8,128)(2,1)S(1)}, bf16[9,40,128]{2,1,0:T(8,128)(2,1)S(1)}) custom-call(s32[1]{0:T(128)} %bitcast.mode_index, bf16[1920,256]{1,0:T(8,128)(2,1)S(1)} %collective-permute-done.below, bf16[1920,256]{1,0:T(8,128)(2,1)S(1)} %collective-permute-done.1.above, ...), custom_call_target="tpu_custom_call" | custom-call | flops 5000000000 | bytes 6291456 | tf_op jit(solution)/shard_map/halo/pallas_call | solution.py:267
  42.5 1.5 %collective-permute-start.2 = (bf16[9,40,128]{2,1,0:T(8,128)(2,1)S(1)}, bf16[9,40,128]{2,1,0:T(8,128)(2,1)S(1)}, u32[]{:S(2)}, u32[]{:S(2)}) collective-permute-start(bf16[9,40,128]{2,1,0:T(8,128)(2,1)S(1)} %get-tuple-element.33), channel_id=1, source_target_pairs={{0,1},{1,2},{2,3},{3,0},{4,5},{5,6},{6,7},{7,4},{8,9},{9,10},{10,1... | collective-permute-start | bytes 276488 | tf_op jit(solution)/shard_map/ppermute | solution.py:274
  44.0 1.1 %collective-permute-start.3 = (bf16[9,40,128]{2,1,0:T(8,128)(2,1)S(1)}, bf16[9,40,128]{2,1,0:T(8,128)(2,1)S(1)}, u32[]{:S(2)}, u32[]{:S(2)}) collective-permute-start(bf16[9,40,128]{2,1,0:T(8,128)(2,1)S(1)} %get-tuple-element.34), channel_id=1, source_target_pairs={{0,2},{1,3},{2,0},{3,1},{4,6},{5,7},{6,4},{7,5},{8,10},{9,11},{10,... | collective-permute-start | bytes 276488 | tf_op jit(solution)/shard_map/ppermute | solution.py:274
  45.2 0.0 collective-permute-start.4
  45.2 0.7 collective-permute-done.2.p1
  45.9 3.6 %collective-permute-done.3.p2 = bf16[9,40,128]{2,1,0:T(8,128)(2,1)S(1)} collective-permute-done((bf16[9,40,128]{2,1,0:T(8,128)(2,1)S(1)}, bf16[9,40,128]{2,1,0:T(8,128)(2,1)S(1)}, u32[]{:S(2)}, u32[]{:S(2)}) %collective-permute-start.3) | collective-permute-done | bytes 92192 | tf_op jit(solution)/shard_map/ppermute | solution.py:274
  49.4 0.6 collective-permute-done.4.p3
  50.1 0.0 copy-done.5
  50.1 2.1 %gradient.1 = (bf16[5120,256]{1,0:T(8,128)(2,1)S(1)}, f32[80,128]{1,0:T(8,128)S(1)}, f32[80,128]{1,0:T(8,128)S(1)}, f32[80,128]{1,0:T(8,128)S(1)}, f32[80,128]{1,0:T(8,128)S(1)}) custom-call(s32[1]{0:T(128)} %bitcast.mode_index, bf16[9,40,128]{2,1,0:T(8,128)(2,1)S(1)} %get-tuple-element.32.p0, bf16[9,40,128]{2,1,0:T(8,128)(2,1)S(1)} %collective-permute-done.2.p1, ...), custom_call_target="tpu_custom_call" | custom-call | flops 2000000000 | bytes 9437184 | tf_op jit(solution)/shard_map/gradient/pallas_call | solution.py:275
  52.2 0.1 collective-permute-start.5
  52.2 0.7 collective-permute-start.6
  52.9 0.4 collective-permute-start.7
  53.4 0.1 collective-permute-done.5
  53.5 1.7 %collective-permute-done.6 = f32[80,128]{1,0:T(8,128)S(1)} collective-permute-done((f32[80,128]{1,0:T(8,128)S(1)}, f32[80,128]{1,0:T(8,128)S(1)}, u32[]{:S(2)}, u32[]{:S(2)}) %collective-permute-start.6) | collective-permute-done | bytes 40992 | tf_op jit(solution)/shard_map/ppermute | solution.py:290
  55.2 1.3 %collective-permute-done.7 = f32[80,128]{1,0:T(8,128)S(1)} collective-permute-done((f32[80,128]{1,0:T(8,128)S(1)}, f32[80,128]{1,0:T(8,128)S(1)}, u32[]{:S(2)}, u32[]{:S(2)}) %collective-permute-start.7) | collective-permute-done | bytes 40992 | tf_op jit(solution)/shard_map/ppermute | solution.py:290
  56.5 11.8 %all_to_all.10 = bf16[8,80,128]{2,1,0:T(8,128)(2,1)S(1)} all-to-all(bf16[8,80,128]{2,1,0:T(8,128)(2,1)S(1)} %broadcast_in_dim.4), channel_id=1, replica_groups={{0,4,8,12,16,20,24,28},{32,36,40,44,48,52,56,60},{64,68,72,76,80,84,88,..., dimensions={0} | all-to-all | bytes 327680 | tf_op jit(solution)/shard_map/all_to_all | solution.py:295
  68.4 14.5 %all_to_all.11 = bf16[8,80,128]{2,1,0:T(8,128)(2,1)S(1)} all-to-all(bf16[8,80,128]{2,1,0:T(8,128)(2,1)S(1)} %broadcast_in_dim.5), channel_id=1, replica_groups={{0,32,64,96,128,160,192,224},{4,36,68,100,132,164,196,228},{8,40,72,104..., dimensions={0} | all-to-all | bytes 327680 | tf_op jit(solution)/shard_map/all_to_all | solution.py:295
  82.9 2.9 %collective-permute-start.10 = (f32[80,128]{1,0:T(8,128)S(1)}, f32[80,128]{1,0:T(8,128)S(1)}, u32[]{:S(2)}, u32[]{:S(2)}) collective-permute-start(f32[80,128]{1,0:T(8,128)S(1)} %convert_reduce_fusion.c0), channel_id=1, source_target_pairs={{0,3},{1,0},{2,1},{3,2},{4,7},{5,4},{6,5},{7,6},{8,11},{9,8},{10,9... | collective-permute-start | bytes 122888 | tf_op jit(solution)/shard_map/ppermute | solution.py:297
  85.9 0.1 collective-permute-start.9
  86.0 1.6 %collective-permute-start.8 = (f32[80,128]{1,0:T(8,128)S(1)}, f32[80,128]{1,0:T(8,128)S(1)}, u32[]{:S(2)}, u32[]{:S(2)}) collective-permute-start(f32[80,128]{1,0:T(8,128)S(1)} %convert_reduce_fusion.c0), channel_id=1, source_target_pairs={{0,1},{1,2},{2,3},{3,0},{4,5},{5,6},{6,7},{7,4},{8,9},{9,10},{10,1... | collective-permute-start | bytes 122888 | tf_op jit(solution)/shard_map/ppermute | solution.py:297
  87.6 3.0 %features.3 = bf16[5120,128]{1,0:T(8,128)(2,1)} custom-call(bf16[5120,256]{1,0:T(8,128)(2,1)S(1)} %get-tuple-element.38.pre_cot, bf16[128,256]{1,0:T(8,128)(2,1)S(1)} %copy-done.4), custom_call_target="tpu_custom_call" | custom-call | flops 2000000000 | bytes 5242880 | tf_op jit(solution)/shard_map/features/pallas_call | solution.py:282
  90.6 0.0 collective-permute-done.10.c3
  90.6 0.0 collective-permute-done.9.c2
  90.6 0.0 collective-permute-done.8.c1
  90.6 0.9 finish.1
  (5 shorter events, 0.1 us)
Async XLA Ops:
  0.6 15.1 %copy-start.6 = (f32[256]{0:T(256)S(1)}, f32[256]{0:T(256)}, u32[]{:S(2)}) copy-start(f32[256]{0:T(256)} %param.14) | copy-start | bytes 3076
  0.6 1.6 %copy-start = (bf16[1280,3,256]{2,0,1:T(8,128)(2,1)S(1)}, bf16[1280,3,256]{2,0,1:T(8,128)(2,1)}, u32[]{:S(2)}) copy-start(bf16[1280,3,256]{2,0,1:T(8,128)(2,1)} %param.8) | copy-start | bytes 5898244
  2.2 0.7 copy-start.1
  2.9 12.9 %copy-start.2 = (bf16[5120,128]{1,0:T(8,128)(2,1)S(1)}, bf16[5120,128]{1,0:T(8,128)(2,1)}, u32[]{:S(2)}) copy-start(bf16[5120,128]{1,0:T(8,128)(2,1)} %features.2) | copy-start | bytes 3932164
  2.9 12.9 %copy-start.4 = (bf16[128,256]{1,0:T(8,128)(2,1)S(1)}, bf16[128,256]{1,0:T(8,128)(2,1)}, u32[]{:S(2)}) copy-start(bf16[128,256]{1,0:T(8,128)(2,1)} %w_in.3) | copy-start | bytes 196612
  4.5 33.0 %collective-permute-start = (bf16[1920,256]{1,0:T(8,128)(2,1)}, bf16[1920,256]{1,0:T(8,128)(2,1)S(1)}, u32[]{:S(2)}, u32[]{:S(2)}) collective-permute-start(bf16[1920,256]{1,0:T(8,128)(2,1)} %get-tuple-element.25.high), channel_id=1, source_target_pairs={{0,4},{4,8},{8,12},{12,16},{16,20},{20,24},{24,28},{28,32},{32,36}... | collective-permute-start | bytes 2949128 | tf_op jit(solution)/shard_map/ppermute | solution.py:246
  6.9 30.5 %collective-permute-start.1 = (bf16[1920,256]{1,0:T(8,128)(2,1)}, bf16[1920,256]{1,0:T(8,128)(2,1)S(1)}, u32[]{:S(2)}, u32[]{:S(2)}) collective-permute-start(bf16[1920,256]{1,0:T(8,128)(2,1)} %get-tuple-element.26.low), channel_id=1, source_target_pairs={{0,252},{4,0},{8,4},{12,8},{16,12},{20,16},{24,20},{28,24},{32,28}... | collective-permute-start | bytes 2949128 | tf_op jit(solution)/shard_map/ppermute | solution.py:247
  15.8 4.0 %copy-start.3 = (s32[1280,16]{0,1:T(8,128)S(1)}, s32[1280,16]{0,1:T(8,128)}, u32[]{:S(2)}) copy-start(s32[1280,16]{0,1:T(8,128)} %param.11) | copy-start | bytes 245764
  15.8 4.0 %copy-start.7 = (f32[256]{0:T(256)S(1)}, f32[256]{0:T(256)}, u32[]{:S(2)}) copy-start(f32[256]{0:T(256)} %param.10) | copy-start | bytes 3076
  37.5 12.6 %copy-start.5 = (bf16[9,256]{1,0:T(8,128)(2,1)S(1)}, bf16[9,256]{1,0:T(8,128)(2,1)}, u32[]{:S(2)}) copy-start(bf16[9,256]{1,0:T(8,128)(2,1)} %w_out.1) | copy-start | bytes 13828
  42.5 3.4 %collective-permute-start.2 = (bf16[9,40,128]{2,1,0:T(8,128)(2,1)S(1)}, bf16[9,40,128]{2,1,0:T(8,128)(2,1)S(1)}, u32[]{:S(2)}, u32[]{:S(2)}) collective-permute-start(bf16[9,40,128]{2,1,0:T(8,128)(2,1)S(1)} %get-tuple-element.33), channel_id=1, source_target_pairs={{0,1},{1,2},{2,3},{3,0},{4,5},{5,6},{6,7},{7,4},{8,9},{9,10},{10,1... | collective-permute-start | bytes 276488 | tf_op jit(solution)/shard_map/ppermute | solution.py:274
  44.0 5.4 %collective-permute-start.3 = (bf16[9,40,128]{2,1,0:T(8,128)(2,1)S(1)}, bf16[9,40,128]{2,1,0:T(8,128)(2,1)S(1)}, u32[]{:S(2)}, u32[]{:S(2)}) collective-permute-start(bf16[9,40,128]{2,1,0:T(8,128)(2,1)S(1)} %get-tuple-element.34), channel_id=1, source_target_pairs={{0,2},{1,3},{2,0},{3,1},{4,6},{5,7},{6,4},{7,5},{8,10},{9,11},{10,... | collective-permute-start | bytes 276488 | tf_op jit(solution)/shard_map/ppermute | solution.py:274
  45.2 4.9 %collective-permute-start.4 = (bf16[9,40,128]{2,1,0:T(8,128)(2,1)S(1)}, bf16[9,40,128]{2,1,0:T(8,128)(2,1)S(1)}, u32[]{:S(2)}, u32[]{:S(2)}) collective-permute-start(bf16[9,40,128]{2,1,0:T(8,128)(2,1)S(1)} %get-tuple-element.35), channel_id=1, source_target_pairs={{0,3},{1,0},{2,1},{3,2},{4,7},{5,4},{6,5},{7,6},{8,11},{9,8},{10,9... | collective-permute-start | bytes 276488 | tf_op jit(solution)/shard_map/ppermute | solution.py:274
  52.2 1.3 %collective-permute-start.5 = (f32[80,128]{1,0:T(8,128)S(1)}, f32[80,128]{1,0:T(8,128)S(1)}, u32[]{:S(2)}, u32[]{:S(2)}) collective-permute-start(f32[80,128]{1,0:T(8,128)S(1)} %get-tuple-element.40), channel_id=1, source_target_pairs={{0,1},{1,2},{2,3},{3,0},{4,5},{5,6},{6,7},{7,4},{8,9},{9,10},{10,1... | collective-permute-start | bytes 122888 | tf_op jit(solution)/shard_map/ppermute | solution.py:290
  52.2 2.9 %collective-permute-start.6 = (f32[80,128]{1,0:T(8,128)S(1)}, f32[80,128]{1,0:T(8,128)S(1)}, u32[]{:S(2)}, u32[]{:S(2)}) collective-permute-start(f32[80,128]{1,0:T(8,128)S(1)} %get-tuple-element.41), channel_id=1, source_target_pairs={{0,2},{1,3},{2,0},{3,1},{4,6},{5,7},{6,4},{7,5},{8,10},{9,11},{10,... | collective-permute-start | bytes 122888 | tf_op jit(solution)/shard_map/ppermute | solution.py:290
  52.9 3.6 %collective-permute-start.7 = (f32[80,128]{1,0:T(8,128)S(1)}, f32[80,128]{1,0:T(8,128)S(1)}, u32[]{:S(2)}, u32[]{:S(2)}) collective-permute-start(f32[80,128]{1,0:T(8,128)S(1)} %get-tuple-element.42), channel_id=1, source_target_pairs={{0,3},{1,0},{2,1},{3,2},{4,7},{5,4},{6,5},{7,6},{8,11},{9,8},{10,9... | collective-permute-start | bytes 122888 | tf_op jit(solution)/shard_map/ppermute | solution.py:290
  82.9 7.7 %collective-permute-start.10 = (f32[80,128]{1,0:T(8,128)S(1)}, f32[80,128]{1,0:T(8,128)S(1)}, u32[]{:S(2)}, u32[]{:S(2)}) collective-permute-start(f32[80,128]{1,0:T(8,128)S(1)} %convert_reduce_fusion.c0), channel_id=1, source_target_pairs={{0,3},{1,0},{2,1},{3,2},{4,7},{5,4},{6,5},{7,6},{8,11},{9,8},{10,9... | collective-permute-start | bytes 122888 | tf_op jit(solution)/shard_map/ppermute | solution.py:297
  85.9 4.7 %collective-permute-start.9 = (f32[80,128]{1,0:T(8,128)S(1)}, f32[80,128]{1,0:T(8,128)S(1)}, u32[]{:S(2)}, u32[]{:S(2)}) collective-permute-start(f32[80,128]{1,0:T(8,128)S(1)} %convert_reduce_fusion.c0), channel_id=1, source_target_pairs={{0,2},{1,3},{2,0},{3,1},{4,6},{5,7},{6,4},{7,5},{8,10},{9,11},{10,... | collective-permute-start | bytes 122888 | tf_op jit(solution)/shard_map/ppermute | solution.py:297
  86.0 4.6 %collective-permute-start.8 = (f32[80,128]{1,0:T(8,128)S(1)}, f32[80,128]{1,0:T(8,128)S(1)}, u32[]{:S(2)}, u32[]{:S(2)}) collective-permute-start(f32[80,128]{1,0:T(8,128)S(1)} %convert_reduce_fusion.c0), channel_id=1, source_target_pairs={{0,1},{1,2},{2,3},{3,0},{4,5},{5,6},{6,7},{7,4},{8,9},{9,10},{10,1... | collective-permute-start | bytes 122888 | tf_op jit(solution)/shard_map/ppermute | solution.py:297
